TPU v7x, 32 devices: a whole 2x2x4 slice. The times are simulated.
32 devices in a mesh: section: 8 (over z, core), expert: 4 (over y, x).
Axes of the slice: x: 2, y: 2, z: 4, core: 2. Of those that a mesh axis runs over, the one named last changes fastest.
Arguments:
- acts: bfloat16 [8, 512, 2048], P('section', 'expert'), may hold values from -6 to 6
- routes: int32 [8, 512, 2], P('section', 'expert'), may hold values from 0 to 3, all different within a row; in each aligned block of 128 rows (0 to 127, 128 to 255, ..., all dimensions but the last counted through in order) at most 96 rows name the same one
- gates: float32 [8, 512, 2], P('section', 'expert'), may hold values from 0.2 to 1
- norm_gain: float32 [8, 2048], P('section'), may hold values from 0.5 to 1.5
- gate_w: bfloat16 [8, 2048, 4096], P('section', None, 'expert'), may hold values from -0.125 to 0.125
- up_w: bfloat16 [8, 2048, 4096], P('section', None, 'expert'), may hold values from -0.125 to 0.125
- down_w: bfloat16 [8, 4096, 2048], P('section', 'expert'), may hold values from -0.1875 to 0.1875
Outputs:
- result: bfloat16 [8, 512, 2048], P('section', 'expert')
Inputs may be any that keep to these rules, and one draw needn't show every extreme that they name: `routes`: each token names 2 different experts. Among the rows of one device, no expert is named by more than 96 tokens, and in every draw some expert is named by exactly 96.
All inputs are finite; a program needn't handle non-finite values.
Results may differ from a plain program's by a relative error of at most 0.005.
Values may be sent and summed in bfloat16 or wider, within the bound.
No kernel may reach another device: no remote copies, remote signals or barrier semaphores. Data moves between devices by JAX's collectives and lax.ppermute only.
A program may use at most 64 MiB of HBM per device.

v0:
```python
import jax
import jax.numpy as jnp
from jax import lax
from jax.sharding import PartitionSpec as P

NEXP = 4
CAP = 96


def shifted(value, axis, steps):
    count = lax.axis_size(axis)
    pairs = [(source, (source + steps) % count) for source in range(count)]
    return lax.ppermute(value, axis, pairs)


def expert_rows(rows, wgate, wup, wdown):
    gpart = jnp.einsum("scd,dh->sch", rows, wgate, preferred_element_type=jnp.float32)
    upart = jnp.einsum("scd,dh->sch", rows, wup, preferred_element_type=jnp.float32)
    hidden = (jax.nn.silu(gpart) * upart).astype(jnp.bfloat16)
    return jnp.einsum("sch,hd->scd", hidden, wdown, preferred_element_type=jnp.float32).astype(
        jnp.bfloat16
    )


def local(acts, routes, gates, norm_gain, gate_w, up_w, down_w):
    arrived = shifted(acts, "section", 1)[0]
    ids = routes[0]
    weights = gates[0]
    gain = norm_gain[0]
    wgate = gate_w[0]
    wup = up_w[0]
    wdown = down_w[0]
    hsplit = lax.axis_size("expert") // NEXP
    tok_count = ids.shape[0]
    chosen = (ids[:, :, None] == jnp.arange(NEXP, dtype=jnp.int32)[None, None, :]).astype(jnp.int32)
    member = jnp.sum(chosen, axis=1)
    gate_of = jnp.sum(weights[:, :, None] * chosen.astype(jnp.float32), axis=1)
    slot_rank = jnp.cumsum(member, axis=0) - 1
    slots = jnp.arange(CAP, dtype=jnp.int32)
    place = (slot_rank.T[:, None, :] == slots[None, :, None]) & (member.T[:, None, :] > 0)
    place_bf = place.astype(jnp.bfloat16)
    xf = arrived.astype(jnp.float32)
    scale = lax.rsqrt(jnp.mean(xf * xf, axis=1, keepdims=True) + 1e-06)
    normed = (xf * scale * gain[None, :]).astype(jnp.bfloat16)
    packed = jnp.einsum("gct,td->gcd", place_bf, normed, preferred_element_type=jnp.float32).astype(
        jnp.bfloat16
    )
    outgoing = jnp.repeat(packed, hsplit, axis=0)
    received = lax.all_to_all(outgoing, "expert", split_axis=0, concat_axis=0, tiled=True)
    returned = lax.all_to_all(
        expert_rows(received, wgate, wup, wdown), "expert", split_axis=0, concat_axis=0, tiled=True
    )
    shards = returned.reshape(NEXP, hsplit, CAP, returned.shape[-1])
    per_expert = jnp.einsum("gct,ghcd->gtd", place_bf, shards, preferred_element_type=jnp.float32)
    contrib = jnp.sum(per_expert * gate_of.T[:, :, None], axis=0)
    result = (xf + contrib).astype(jnp.bfloat16)
    return result.reshape(1, tok_count, result.shape[-1])


def solution(mesh):
    in_specs = (
        P("section", "expert", None),
        P("section", "expert", None),
        P("section", "expert", None),
        P("section", None),
        P("section", None, "expert"),
        P("section", None, "expert"),
        P("section", "expert", None),
    )
    out_specs = P("section", "expert", None)
    return jax.shard_map(local, mesh=mesh, in_specs=in_specs, out_specs=out_specs, check_vma=False)
```

profile of v0, /device:TPU:0, one launch (start us, length us, event | category | flops | bytes accessed | tf_op | source)
XLA Modules:
  0.0 67.3 jit_solution(15087835155594649672)
XLA Ops:
  0.0 0.5 collective-permute-start
  0.5 0.7 %convert_reduce_fusion = s32[128,4]{0,1:T(4,128)S(1)} fusion(s32[128,2]{0,1:T(2,128)} %bitcast.50), kind=kLoop, calls=%fused_computation.30 | loop fusion | flops 2560 | bytes 3072 | tf_op jit(solution)/shard_map/reduce_sum | solution.py:36
  1.1 0.1 copy.12
  1.3 0.2 reduce_window_sum.11
  1.4 0.1 copy.13
  1.5 10.1 %collective-permute-done = bf16[1,128,2048]{2,1,0:T(8,128)(2,1)S(1)} collective-permute-done((bf16[1,128,2048]{2,1,0:T(8,128)(2,1)}, bf16[1,128,2048]{2,1,0:T(8,128)(2,1)S(1)}, u32[]{:S(2)}, u32[]{:S(2)}) %collective-permute-start) | collective-permute-done | bytes 524320 | tf_op jit(solution)/shard_map/ppermute | solution.py:13
  11.6 0.2 fusion.13
  11.8 0.0 copy-start.2
  11.8 1.5 %convolution_convert_fusion = bf16[4,96,2048]{2,1,0:T(8,128)(2,1)S(1)} fusion(bf16[1,128,2048]{2,1,0:T(8,128)(2,1)S(1)} %collective-permute-done, f32[2048]{0:T(1024)} %bitcast.49, f32[128]{0:T(128)S(1)} %add_rsqrt_fusion, s32[4,128]{1,0:T(4,128)S(1)} %copy.13, pred[4,128]{1,0:T(4,128)(4,1)S(1)} %compare_bitcast_fusion), kind=kOutput, calls=%fused_computation.8 | convolution fusion | flops 203259904 | bytes 2108416 | tf_op jit(solution)/shard_map/gct,td->gcd/dot_general | solution.py:45
  13.3 21.5 %all_to_all.10 = bf16[4,96,2048]{2,1,0:T(8,128)(2,1)S(1)} all-to-all(bf16[4,96,2048]{2,1,0:T(8,128)(2,1)S(1)} %convolution_convert_fusion), channel_id=1, replica_groups=mesh['section'=8,'expert'=4] {'expert'}, dimensions={0} | all-to-all | bytes 3145728 | tf_op jit(solution)/shard_map/all_to_all | solution.py:49
  34.7 0.0 copy-done.2
  34.7 3.0 %fusion.4 = f32[4,96,1024]{2,1,0:T(8,128)} fusion(bf16[4,96,2048]{2,1,0:T(8,128)(2,1)S(1)} %all_to_all.10, bf16[1,2048,1024]{2,1,0:T(8,128)(2,1)S(1)} %copy-done.2), kind=kOutput, calls=%fused_computation.4 | convolution fusion | flops 1610612736 | bytes 7340032 | tf_op jit(solution)/shard_map/scd,dh->sch/dot_general | solution.py:17
  37.7 8.6 %fusion.6 = bf16[4,96,2048]{2,1,0:T(8,128)(2,1)} fusion(bf16[1,1024,2048]{2,1,0:T(8,128)(2,1)} %param.13, f32[4,96,1024]{2,1,0:T(8,128)} %fusion.4, bf16[4,96,2048]{2,1,0:T(8,128)(2,1)S(1)} %all_to_all.10, bf16[1,2048,1024]{2,1,0:T(8,128)(2,1)} %param.12), kind=kOutput, calls=%fused_computation.7 | convolution fusion | flops 3224371200 | bytes 13107200 | tf_op jit(solution)/shard_map/sch,hd->scd/dot_general | solution.py:20
  46.3 0.0 copy-start
  46.3 0.0 copy-start.1
  46.3 3.7 %all-to-all-start.1 = ((bf16[4,96,2048]{2,1,0:T(8,128)(2,1)}), bf16[4,96,2048]{2,1,0:T(8,128)(2,1)S(1)}, u32[]{:S(2)}, u32[]{:S(2)}) async-start(bf16[4,96,2048]{2,1,0:T(8,128)(2,1)} %fusion.6), calls=%async_computation.1 | async-start | bytes 3145728 | tf_op jit(solution)/shard_map/all_to_all | solution.py:50
  50.0 0.0 copy-done
  50.0 0.0 copy-done.1
  50.0 15.6 %all-to-all-done.1 = bf16[4,96,2048]{2,1,0:T(8,128)(2,1)S(1)} async-done(((bf16[4,96,2048]{2,1,0:T(8,128)(2,1)}), bf16[4,96,2048]{2,1,0:T(8,128)(2,1)S(1)}, u32[]{:S(2)}, u32[]{:S(2)}) %all-to-all-start.1) | async-done | bytes 1572896 | tf_op jit(solution)/shard_map/all_to_all | solution.py:50
  65.6 0.8 %multiply_reduce_fusion = f32[128,2048]{1,0:T(8,128)S(1)} fusion(bf16[4,96,2048]{2,1,0:T(8,128)(2,1)S(1)} %all-to-all-done.1, f32[4,128]{1,0:T(4,128)S(1)} %bitcast.52, s32[4,128]{1,0:T(4,128)S(1)} %copy.13, pred[4,128]{1,0:T(4,128)(4,1)S(1)} %compare_bitcast_fusion), kind=kOutput, calls=%fused_computation.6 | convolution fusion | flops 203259904 | bytes 2626048 | tf_op jit(solution)/shard_map/gct,ghcd->gtd/dot_general | solution.py:54
  66.4 0.9 %fusion.16 = bf16[1,128,2048]{2,1,0:T(8,128)(2,1)} fusion(bf16[1,128,2048]{2,1,0:T(8,128)(2,1)S(1)} %collective-permute-done, f32[128,2048]{1,0:T(8,128)S(1)} %multiply_reduce_fusion), kind=kLoop, calls=%fused_computation.17 | loop fusion | flops 786432 | bytes 2097152 | tf_op jit(solution)/shard_map/convert_element_type | solution.py:56
  (4 shorter events, 0.0 us)
Async XLA Ops:
  0.0 11.6 %collective-permute-start = (bf16[1,128,2048]{2,1,0:T(8,128)(2,1)}, bf16[1,128,2048]{2,1,0:T(8,128)(2,1)S(1)}, u32[]{:S(2)}, u32[]{:S(2)}) collective-permute-start(bf16[1,128,2048]{2,1,0:T(8,128)(2,1)} %param.7), channel_id=1, source_target_pairs={{0,4},{4,8},{8,12},{12,16},{16,20},{20,24},{24,28},{28,0},{1,5},{5... | collective-permute-start | bytes 1572872 | tf_op jit(solution)/shard_map/ppermute | solution.py:13
  11.8 23.0 %copy-start.2 = (bf16[1,2048,1024]{2,1,0:T(8,128)(2,1)S(1)}, bf16[1,2048,1024]{2,1,0:T(8,128)(2,1)}, u32[]{:S(2)}) copy-start(bf16[1,2048,1024]{2,1,0:T(8,128)(2,1)} %param.11) | copy-start | bytes 12582916
  46.3 3.7 %copy-start = (s32[1,128,2]{1,2,0:T(2,128)S(1)}, s32[1,128,2]{1,2,0:T(2,128)}, u32[]{:S(2)}) copy-start(s32[1,128,2]{1,2,0:T(2,128)} %param.8) | copy-start | bytes 3076
  46.3 3.7 %copy-start.1 = (f32[1,128,2]{1,2,0:T(2,128)S(1)}, f32[1,128,2]{1,2,0:T(2,128)}, u32[]{:S(2)}) copy-start(f32[1,128,2]{1,2,0:T(2,128)} %param.9) | copy-start | bytes 3076
  46.3 19.3 %all-to-all-start.1 = ((bf16[4,96,2048]{2,1,0:T(8,128)(2,1)}), bf16[4,96,2048]{2,1,0:T(8,128)(2,1)S(1)}, u32[]{:S(2)}, u32[]{:S(2)}) async-start(bf16[4,96,2048]{2,1,0:T(8,128)(2,1)} %fusion.6), calls=%async_computation.1 | async-start | bytes 3145728 | tf_op jit(solution)/shard_map/all_to_all | solution.py:50
where the time goes:
time: 67.7 us; the launch traced here: 67.3 us
  waiting for transfers between devices  25.6 us (38%)
  blocking collectives  21.5 us (32%)
  matrix products  13.8 us (20%)
  starting transfers between devices  4.15 us (6%)
  other arithmetic  2 us (3%)
    all_to_all x1, blocking collectives, local(): lax.all_to_all(outgoing, 'expert', split_axis=0, concat_axis=0, tiled=True)  21.5 us
    all_to_all x1, waiting for transfers between devices, local(): lax.all_to_all(expert_rows(received, wgate, wup, wdown), 'expert', split_...  15.6 us
    ppermute x1, waiting for transfers between devices, shifted(): return lax.ppermute(value, axis, pairs)  10.1 us
    dot_general x1, matrix products, expert_rows(): jnp.einsum('sch,hd->scd', hidden, wdown, preferred_element_type=jnp.float32)  8.58 us
    all_to_all x1, starting transfers between devices, local(): lax.all_to_all(expert_rows(received, wgate, wup, wdown), 'expert', split_...  3.69 us
    dot_general x1, matrix products, expert_rows(): jnp.einsum('scd,dh->sch', rows, wgate, preferred_element_type=jnp.float32)  2.96 us
    dot_general x1, matrix products, local(): jnp.einsum('gct,td->gcd', place_bf, normed, preferred_element_type=jnp.fl...  1.5 us
  transfers between devices with their start and end apart: 2, of which 2 were waited for; matrix products, arithmetic and copies ran while one was open for 2% of the time, Pallas kernels for 0%

commit v1 on v0

--- a/solution.py
+++ b/solution.py
@@ -1,10 +1,16 @@
+import functools
+
 import jax
 import jax.numpy as jnp
 from jax import lax
+from jax.experimental import pallas as pl
+from jax.experimental.pallas import tpu as pltpu
 from jax.sharding import PartitionSpec as P
 
 NEXP = 4
 CAP = 96
+VMEM = pltpu.VMEM
+SMEM = pltpu.SMEM
 
 
 def shifted(value, axis, steps):
@@ -22,7 +28,7 @@
     )
 
 
-def local(acts, routes, gates, norm_gain, gate_w, up_w, down_w):
+def local_any(acts, routes, gates, norm_gain, gate_w, up_w, down_w):
     arrived = shifted(acts, "section", 1)[0]
     ids = routes[0]
     weights = gates[0]
@@ -57,6 +63,142 @@
     return result.reshape(1, tok_count, result.shape[-1])
 
 
+def spec(space=VMEM):
+    return pl.BlockSpec(memory_space=space)
+
+
+def call(body, outs, ins, spaces, limit=16, flops=0, scratch=()):
+    moved = sum(v.size * v.dtype.itemsize for v in (*ins, *outs))
+    return pl.pallas_call(
+        body,
+        out_shape=outs,
+        in_specs=[spec(s) for s in spaces],
+        out_specs=[spec() for _ in outs],
+        scratch_shapes=scratch,
+        compiler_params=pltpu.CompilerParams(vmem_limit_bytes=limit << 20),
+        cost_estimate=pl.CostEstimate(flops=flops, bytes_accessed=moved, transcendentals=0),
+    )(*ins)
+
+
+def like(shape, dtype=jnp.bfloat16):
+    return jax.ShapeDtypeStruct(shape, dtype)
+
+
+def members(ids, who, count):
+    rows = [((ids[0:1, :] == who[k]) | (ids[1:2, :] == who[k])).astype(jnp.float32) for k in range(count)]
+    rows += [jnp.zeros_like(rows[0])] * (8 - count)
+    return jnp.concatenate(rows, axis=0)
+
+
+def ranks(member):
+    tokens = member.shape[1]
+    before = lax.broadcasted_iota(jnp.int32, (tokens, tokens), 0)
+    at = lax.broadcasted_iota(jnp.int32, (tokens, tokens), 1)
+    upto = (before <= at).astype(jnp.bfloat16)
+    return jnp.dot(member.astype(jnp.bfloat16), upto, preferred_element_type=jnp.float32) - 1.0
+
+
+def one_hot(member, rank, k):
+    slots = lax.broadcasted_iota(jnp.int32, (CAP, member.shape[1]), 0).astype(jnp.float32)
+    hit = (slots == rank[k : k + 1, :]) & (member[k : k + 1, :] > 0)
+    return hit.astype(jnp.bfloat16)
+
+
+def pack_body(count, who, ids, rows, gain, *outs):
+    xf = rows[...].astype(jnp.float32)
+    scale = lax.rsqrt(jnp.mean(xf * xf, axis=1, keepdims=True) + 1e-06)
+    normed = (xf * scale * gain[...]).astype(jnp.bfloat16)
+    member = members(ids[...], who, count)
+    rank = ranks(member)
+    for k in range(count):
+        place = one_hot(member, rank, k)
+        outs[k][...] = jnp.dot(place, normed, preferred_element_type=jnp.float32).astype(jnp.bfloat16)
+
+
+def pack(who, ids, rows, gain, count):
+    out = like((CAP, rows.shape[1]))
+    return call(
+        functools.partial(pack_body, count), [out] * count, (who, ids, rows, gain), (SMEM, VMEM, VMEM, VMEM)
+    )
+
+
+def ffn_body(count, *refs):
+    xs, (wgate, wup, wdown), outs = refs[:count], refs[count : count + 3], refs[count + 3 :]
+    x = xs[0][...] if count == 1 else jnp.concatenate([r[...] for r in xs], axis=0)
+    gpart = jnp.dot(x, wgate[...], preferred_element_type=jnp.float32)
+    upart = jnp.dot(x, wup[...], preferred_element_type=jnp.float32)
+    hidden = (gpart * jax.nn.sigmoid(gpart) * upart).astype(jnp.bfloat16)
+    part = jnp.dot(hidden, wdown[...], preferred_element_type=jnp.float32).astype(jnp.bfloat16)
+    for k in range(count):
+        outs[k][...] = part[k * CAP : (k + 1) * CAP]
+
+
+def ffn(xs, weights):
+    count = len(xs)
+    flops = 6 * count * CAP * weights[0].size
+    return call(
+        functools.partial(ffn_body, count),
+        [like((CAP, weights[2].shape[1]))] * count,
+        (*xs, *weights),
+        [VMEM] * (count + 3),
+        limit=32,
+        flops=flops,
+    )
+
+
+def combine_body(count, who, ids, gates, rows, *refs):
+    parts, out = refs[:count], refs[count]
+    member = members(ids[...], who, count)
+    rank = ranks(member)
+    weight = [
+        jnp.where(ids[0:1, :] == who[k], gates[0:1, :], 0.0) + jnp.where(ids[1:2, :] == who[k], gates[1:2, :], 0.0)
+        for k in range(count)
+    ]
+    weight = jnp.concatenate(weight + [jnp.zeros_like(weight[0])] * (8 - count), axis=0).T
+    total = rows[...].astype(jnp.float32)
+    for k in range(count):
+        place = one_hot(member, rank, k)
+        spread = lax.dot_general(
+            place, parts[k][...], (((0,), (0,)), ((), ())), preferred_element_type=jnp.float32
+        )
+        total = total + weight[:, k : k + 1] * spread
+    out[...] = total.astype(jnp.bfloat16)
+
+
+def combine(who, ids, gates, rows, parts):
+    count = len(parts)
+    return call(
+        functools.partial(combine_body, count),
+        [like(rows.shape)],
+        (who, ids, gates, rows, *parts),
+        [SMEM] + [VMEM] * (count + 3),
+    )[0]
+
+
+def swapped(value, flip):
+    return lax.ppermute(value, "expert", [(e, e ^ flip) for e in range(NEXP)])
+
+
+def local_square(acts, routes, gates, norm_gain, gate_w, up_w, down_w):
+    arrived = shifted(acts, "section", 1)[0]
+    me = lax.axis_index("expert").astype(jnp.int32)
+    who = jnp.stack([me, me ^ 1, me ^ 2, me ^ 3])
+    ids = routes[0].T
+    weights = (gate_w[0], up_w[0], down_w[0])
+    own, px, py, pd = pack(who, ids, arrived, norm_gain, NEXP)
+    pd = swapped(pd, 3)
+    px = swapped(px, 1)
+    py = swapped(py, 2)
+    (td,) = ffn([pd], weights)
+    td = swapped(td, 3)
+    tx, ty = ffn([px, py], weights)
+    tx = swapped(tx, 1)
+    ty = swapped(ty, 2)
+    (to,) = ffn([own], weights)
+    result = combine(who, ids, gates[0].T, arrived, [to, tx, ty, td])
+    return result[None]
+
+
 def solution(mesh):
     in_specs = (
         P("section", "expert", None),
@@ -68,4 +210,5 @@
         P("section", "expert", None),
     )
     out_specs = P("section", "expert", None)
+    local = local_square if mesh.shape["expert"] == NEXP else local_any
     return jax.shard_map(local, mesh=mesh, in_specs=in_specs, out_specs=out_specs, check_vma=False)

time: 67.7 us -> 57.8 us (0.85)
  blocking collectives: 21.5 us -> 0 us
  matrix products: 13.8 us -> 0 us
  Pallas kernels: 0 us -> 10.5 us
  local copies, waits for them, and re-layouts: 0.19 us -> 7.95 us
  waiting for transfers between devices: 25.6 us -> 31.2 us
  starting transfers between devices: 4.15 us -> 7.66 us
  other arithmetic: 2 us -> 0.08 us
    all_to_all x1 -> x0, blocking collectives: 21.5 us -> none  [local(): lax.all_to_all(outgoing, 'expert', split_axis=0, concat_axis=0, tiled=True)]
    ppermute x0 -> x6, waiting for transfers between devices: none -> 20.2 us  [swapped(): return lax.ppermute(value, 'expert', [(e, e ^ flip) for e in range(NEXP)])]
    all_to_all x1 -> x0, waiting for transfers between devices: 15.6 us -> none  [local(): lax.all_to_all(expert_rows(received, wgate, wup, wdown), 'expert', split_...]
    dot_general x4 -> x0, matrix products: 13.8 us -> none  [the longest x1 8.58 us: expert_rows(): jnp.einsum('sch,hd->scd', hidden, wdown, preferred_element_type=jnp.float32)]
    pallas_call x0 -> x5, Pallas kernels: none -> 10.5 us  [call(): pl.pallas_call(body, out_shape=outs, in_specs=[spec(s) for s in spaces],...]
    unnamed x6 -> x16, local copies, waits for them, and re-layouts: 0.01 us -> 7.95 us
    ppermute x0 -> x6, starting transfers between devices: none -> 7.2 us  [swapped(): return lax.ppermute(value, 'expert', [(e, e ^ flip) for e in range(NEXP)])]
    all_to_all x1 -> x0, starting transfers between devices: 3.69 us -> none  [local(): lax.all_to_all(expert_rows(received, wgate, wup, wdown), 'expert', split_...]
  transfers between devices with their start and end apart: 2 -> 7, of which waited for: 2 -> 5; matrix products, arithmetic and copies ran while one was open for 2% -> 0% of each run, Pallas kernels for 0% -> 12%
where the time goes in v1:
time: 57.8 us; the launch traced here: 57.5 us
  waiting for transfers between devices  31.2 us (54%)
  Pallas kernels  10.5 us (18%)
  local copies, waits for them, and re-layouts  7.95 us (14%)
  starting transfers between devices  7.66 us (13%)
    ppermute x6, waiting for transfers between devices, swapped(): return lax.ppermute(value, 'expert', [(e, e ^ flip) for e in range(NEXP)])  20.2 us
    ppermute x1, waiting for transfers between devices, shifted(): return lax.ppermute(value, axis, pairs)  11 us
    pallas_call x5, Pallas kernels, call(): pl.pallas_call(body, out_shape=outs, in_specs=[spec(s) for s in spaces],...  10.5 us
    unnamed x16, local copies, waits for them, and re-layouts  7.95 us
    ppermute x6, starting transfers between devices, swapped(): return lax.ppermute(value, 'expert', [(e, e ^ flip) for e in range(NEXP)])  7.2 us
  transfers between devices with their start and end apart: 7, of which 5 were waited for; matrix products, arithmetic and copies ran while one was open for 0% of the time, Pallas kernels for 12%

profile of v1, /device:TPU:0, one launch (start us, length us, event | category | flops | bytes accessed | tf_op | source)
XLA Modules:
  0.0 57.5 jit_solution(17348767517217597127)
XLA Ops:
  0.0 0.5 collective-permute-start
  0.5 0.1 pad_add_fusion.who
  0.5 11.0 %collective-permute-done = bf16[1,128,2048]{2,1,0:T(8,128)(2,1)S(1)} collective-permute-done((bf16[1,128,2048]{2,1,0:T(8,128)(2,1)}, bf16[1,128,2048]{2,1,0:T(8,128)(2,1)S(1)}, u32[]{:S(2)}, u32[]{:S(2)}) %collective-permute-start) | collective-permute-done | bytes 524320 | tf_op jit(solution)/shard_map/ppermute | solution.py:19
  11.6 0.0 copy-start.4
  11.6 0.7 %copy-done.4 = f32[1,2048]{1,0:T(1,128)S(1)} copy-done((f32[1,2048]{1,0:T(1,128)S(1)}, f32[1,2048]{1,0:T(1,128)}, u32[]{:S(2)}) %copy-start.4) | copy-done | bytes 8216
  12.3 0.0 copy-start.5
  12.3 0.7 %copy-done.5 = s32[1,128,2]{1,2,0:T(2,128)S(1)} copy-done((s32[1,128,2]{1,2,0:T(2,128)S(1)}, s32[1,128,2]{1,2,0:T(2,128)}, u32[]{:S(2)}) %copy-start.5) | copy-done | bytes 1048
  12.9 1.3 %shard_map.73 = (bf16[96,2048]{1,0:T(8,128)(2,1)S(1)}, bf16[96,2048]{1,0:T(8,128)(2,1)S(1)}, bf16[96,2048]{1,0:T(8,128)(2,1)S(1)}, bf16[96,2048]{1,0:T(8,128)(2,1)S(1)}) custom-call(s32[4]{0:T(128)S(1)} %pad_add_fusion.who, s32[2,128]{1,0:T(2,128)S(1)} %bitcast.26, bf16[128,2048]{1,0:T(8,128)(2,1)S(1)} %bitcast.24, f32[1,2048]{1,0:T(1,128)S(1)} %copy-done.4), custom_call_target="tpu_custom_call" | custom-call | bytes 2106384 | tf_op jit(solution)/shard_map/pallas_call | solution.py:72
  14.2 2.1 %collective-permute-start.1 = (bf16[96,2048]{1,0:T(8,128)(2,1)S(1)}, bf16[96,2048]{1,0:T(8,128)(2,1)S(1)}, u32[]{:S(2)}, u32[]{:S(2)}) collective-permute-start(bf16[96,2048]{1,0:T(8,128)(2,1)S(1)} %get-tuple-element.12), channel_id=1, source_target_pairs={{0,1},{1,0},{2,3},{3,2},{4,5},{5,4},{6,7},{7,6},{8,9},{9,8},{10,11... | collective-permute-start | bytes 1179656 | tf_op jit(solution)/shard_map/ppermute | solution.py:179
  16.3 1.5 %collective-permute-start.2 = (bf16[96,2048]{1,0:T(8,128)(2,1)S(1)}, bf16[96,2048]{1,0:T(8,128)(2,1)S(1)}, u32[]{:S(2)}, u32[]{:S(2)}) collective-permute-start(bf16[96,2048]{1,0:T(8,128)(2,1)S(1)} %get-tuple-element.13), channel_id=1, source_target_pairs={{0,2},{1,3},{2,0},{3,1},{4,6},{5,7},{6,4},{7,5},{8,10},{9,11},{10,... | collective-permute-start | bytes 1179656 | tf_op jit(solution)/shard_map/ppermute | solution.py:179
  17.8 0.0 collective-permute-start.5
  17.9 8.5 %collective-permute-done.1.refs_0_ = bf16[96,2048]{1,0:T(8,128)(2,1)S(1)} collective-permute-done((bf16[96,2048]{1,0:T(8,128)(2,1)S(1)}, bf16[96,2048]{1,0:T(8,128)(2,1)S(1)}, u32[]{:S(2)}, u32[]{:S(2)}) %collective-permute-start.1) | collective-permute-done | bytes 393248 | tf_op jit(solution)/shard_map/ppermute | solution.py:179
  26.4 6.6 %collective-permute-done.2.refs_1_ = bf16[96,2048]{1,0:T(8,128)(2,1)S(1)} collective-permute-done((bf16[96,2048]{1,0:T(8,128)(2,1)S(1)}, bf16[96,2048]{1,0:T(8,128)(2,1)S(1)}, u32[]{:S(2)}, u32[]{:S(2)}) %collective-permute-start.2) | collective-permute-done | bytes 393248 | tf_op jit(solution)/shard_map/ppermute | solution.py:179
  33.0 0.0 copy-start
  33.0 2.2 %copy-done = bf16[1,2048,1024]{2,1,0:T(8,128)(2,1)S(1)} copy-done((bf16[1,2048,1024]{2,1,0:T(8,128)(2,1)S(1)}, bf16[1,2048,1024]{2,1,0:T(8,128)(2,1)}, u32[]{:S(2)}) %copy-start) | copy-done | bytes 4194328
  35.2 0.0 copy-start.2
  35.2 2.2 %copy-done.2 = bf16[1,2048,1024]{2,1,0:T(8,128)(2,1)S(1)} copy-done((bf16[1,2048,1024]{2,1,0:T(8,128)(2,1)S(1)}, bf16[1,2048,1024]{2,1,0:T(8,128)(2,1)}, u32[]{:S(2)}) %copy-start.2) | copy-done | bytes 4194328
  37.4 0.0 copy-start.3
  37.4 2.2 %copy-done.3 = bf16[1,1024,2048]{2,1,0:T(8,128)(2,1)S(1)} copy-done((bf16[1,1024,2048]{2,1,0:T(8,128)(2,1)S(1)}, bf16[1,1024,2048]{2,1,0:T(8,128)(2,1)}, u32[]{:S(2)}) %copy-start.3) | copy-done | bytes 4194328
  39.6 2.6 %shard_map.75 = (bf16[96,2048]{1,0:T(8,128)(2,1)S(1)}, bf16[96,2048]{1,0:T(8,128)(2,1)S(1)}) custom-call(bf16[96,2048]{1,0:T(8,128)(2,1)S(1)} %collective-permute-done.1.refs_0_, bf16[96,2048]{1,0:T(8,128)(2,1)S(1)} %collective-permute-done.2.refs_1_, bf16[2048,1024]{1,0:T(8,128)(2,1)S(1)} %bitcast.15, bf16[2048,1024]{1,0:T(8,128)(2,1)S(1)} %bitcast.18, ...), custom_call_target="tpu_custom_call" | custom-call | flops 2415919104 | bytes 14155776 | tf_op jit(solution)/shard_map/pallas_call | solution.py:72
  42.2 0.1 collective-permute-start.3
  42.3 0.0 copy-start.1
  42.3 2.0 %collective-permute-start.4 = (bf16[96,2048]{1,0:T(8,128)(2,1)S(1)}, bf16[96,2048]{1,0:T(8,128)(2,1)S(1)}, u32[]{:S(2)}, u32[]{:S(2)}) collective-permute-start(bf16[96,2048]{1,0:T(8,128)(2,1)S(1)} %get-tuple-element.15), channel_id=1, source_target_pairs={{0,2},{1,3},{2,0},{3,1},{4,6},{5,7},{6,4},{7,5},{8,10},{9,11},{10,... | collective-permute-start | bytes 1179656 | tf_op jit(solution)/shard_map/ppermute | solution.py:179
  44.3 0.0 collective-permute-done.5.refs_0_
  44.3 2.2 %shard_map.76 = bf16[96,2048]{1,0:T(8,128)(2,1)S(1)} custom-call(bf16[96,2048]{1,0:T(8,128)(2,1)S(1)} %collective-permute-done.5.refs_0_, bf16[2048,1024]{1,0:T(8,128)(2,1)S(1)} %bitcast.16, bf16[2048,1024]{1,0:T(8,128)(2,1)S(1)} %bitcast.19, bf16[1024,2048]{1,0:T(8,128)(2,1)S(1)} %bitcast.22), custom_call_target="tpu_custom_call" | custom-call | flops 1207959552 | bytes 13369344 | tf_op jit(solution)/shard_map/pallas_call | solution.py:72
  46.5 1.5 %collective-permute-start.6 = (bf16[96,2048]{1,0:T(8,128)(2,1)S(1)}, bf16[96,2048]{1,0:T(8,128)(2,1)S(1)}, u32[]{:S(2)}, u32[]{:S(2)}) collective-permute-start(bf16[96,2048]{1,0:T(8,128)(2,1)S(1)} %shard_map.76), channel_id=1, source_target_pairs={{0,3},{1,2},{2,1},{3,0},{4,7},{5,6},{6,5},{7,4},{8,11},{9,10},{10,... | collective-permute-start | bytes 1179656 | tf_op jit(solution)/shard_map/ppermute | solution.py:179
  48.0 0.0 copy-done.1
  48.0 0.0 copy-start.6
  48.0 0.0 copy-start.7
  48.0 2.2 %shard_map.74.refs_0_ = bf16[96,2048]{1,0:T(8,128)(2,1)S(1)} custom-call(bf16[96,2048]{1,0:T(8,128)(2,1)S(1)} %get-tuple-element.11.refs_0_, bf16[2048,1024]{1,0:T(8,128)(2,1)S(1)} %bitcast.17, bf16[2048,1024]{1,0:T(8,128)(2,1)S(1)} %bitcast.20, bf16[1024,2048]{1,0:T(8,128)(2,1)S(1)} %bitcast.23), custom_call_target="tpu_custom_call" | custom-call | flops 1207959552 | bytes 13369344 | tf_op jit(solution)/shard_map/pallas_call | solution.py:72
  50.1 0.0 collective-permute-done.3.refs_1_
  50.1 3.7 %collective-permute-done.4.refs_2_ = bf16[96,2048]{1,0:T(8,128)(2,1)S(1)} collective-permute-done((bf16[96,2048]{1,0:T(8,128)(2,1)S(1)}, bf16[96,2048]{1,0:T(8,128)(2,1)S(1)}, u32[]{:S(2)}, u32[]{:S(2)}) %collective-permute-start.4) | collective-permute-done | bytes 393248 | tf_op jit(solution)/shard_map/ppermute | solution.py:179
  53.9 1.4 %collective-permute-done.6.refs_3_ = bf16[96,2048]{1,0:T(8,128)(2,1)S(1)} collective-permute-done((bf16[96,2048]{1,0:T(8,128)(2,1)S(1)}, bf16[96,2048]{1,0:T(8,128)(2,1)S(1)}, u32[]{:S(2)}, u32[]{:S(2)}) %collective-permute-start.6) | collective-permute-done | bytes 393248 | tf_op jit(solution)/shard_map/ppermute | solution.py:179
  55.2 0.0 copy-done.6
  55.2 0.0 copy-done.7
  55.2 2.3 %shard_map.77 = bf16[128,2048]{1,0:T(8,128)(2,1)} custom-call(s32[4]{0:T(128)S(1)} %pad_add_fusion.who, s32[2,128]{1,0:T(2,128)S(1)} %bitcast.27, f32[2,128]{1,0:T(2,128)S(1)} %bitcast.28, bf16[128,2048]{1,0:T(8,128)(2,1)S(1)} %bitcast.25, bf16[96,2048]{1,0:T(8,128)(2,1)S(1)} %shard_map.74.refs_0_, bf16[96,2048]{1,0:T(8,128)(2,1)S(1)} %collective-permute-done.3.refs_1_, ...), custom_call_target="tpu_custom_call" | custom-call | bytes 2623504 | tf_op jit(solution)/shard_map/pallas_call | solution.py:72
Async XLA Ops:
  0.0 11.6 %collective-permute-start = (bf16[1,128,2048]{2,1,0:T(8,128)(2,1)}, bf16[1,128,2048]{2,1,0:T(8,128)(2,1)S(1)}, u32[]{:S(2)}, u32[]{:S(2)}) collective-permute-start(bf16[1,128,2048]{2,1,0:T(8,128)(2,1)} %param.7), channel_id=1, source_target_pairs={{0,4},{4,8},{8,12},{12,16},{16,20},{20,24},{24,28},{28,0},{1,5},{5... | collective-permute-start | bytes 1572872 | tf_op jit(solution)/shard_map/ppermute | solution.py:19
  11.6 0.7 %copy-start.4 = (f32[1,2048]{1,0:T(1,128)S(1)}, f32[1,2048]{1,0:T(1,128)}, u32[]{:S(2)}) copy-start(f32[1,2048]{1,0:T(1,128)} %gain.1) | copy-start | bytes 24580
  12.3 0.7 %copy-start.5 = (s32[1,128,2]{1,2,0:T(2,128)S(1)}, s32[1,128,2]{1,2,0:T(2,128)}, u32[]{:S(2)}) copy-start(s32[1,128,2]{1,2,0:T(2,128)} %param.8) | copy-start | bytes 3076
  14.2 12.1 %collective-permute-start.1 = (bf16[96,2048]{1,0:T(8,128)(2,1)S(1)}, bf16[96,2048]{1,0:T(8,128)(2,1)S(1)}, u32[]{:S(2)}, u32[]{:S(2)}) collective-permute-start(bf16[96,2048]{1,0:T(8,128)(2,1)S(1)} %get-tuple-element.12), channel_id=1, source_target_pairs={{0,1},{1,0},{2,3},{3,2},{4,5},{5,4},{6,7},{7,6},{8,9},{9,8},{10,11... | collective-permute-start | bytes 1179656 | tf_op jit(solution)/shard_map/ppermute | solution.py:179
  16.3 16.7 %collective-permute-start.2 = (bf16[96,2048]{1,0:T(8,128)(2,1)S(1)}, bf16[96,2048]{1,0:T(8,128)(2,1)S(1)}, u32[]{:S(2)}, u32[]{:S(2)}) collective-permute-start(bf16[96,2048]{1,0:T(8,128)(2,1)S(1)} %get-tuple-element.13), channel_id=1, source_target_pairs={{0,2},{1,3},{2,0},{3,1},{4,6},{5,7},{6,4},{7,5},{8,10},{9,11},{10,... | collective-permute-start | bytes 1179656 | tf_op jit(solution)/shard_map/ppermute | solution.py:179
  17.8 26.5 %collective-permute-start.5 = (bf16[96,2048]{1,0:T(8,128)(2,1)S(1)}, bf16[96,2048]{1,0:T(8,128)(2,1)S(1)}, u32[]{:S(2)}, u32[]{:S(2)}) collective-permute-start(bf16[96,2048]{1,0:T(8,128)(2,1)S(1)} %get-tuple-element.16), channel_id=1, source_target_pairs={{0,3},{1,2},{2,1},{3,0},{4,7},{5,6},{6,5},{7,4},{8,11},{9,10},{10,... | collective-permute-start | bytes 1179656 | tf_op jit(solution)/shard_map/ppermute | solution.py:179
  33.0 2.2 %copy-start = (bf16[1,2048,1024]{2,1,0:T(8,128)(2,1)S(1)}, bf16[1,2048,1024]{2,1,0:T(8,128)(2,1)}, u32[]{:S(2)}) copy-start(bf16[1,2048,1024]{2,1,0:T(8,128)(2,1)} %param.11) | copy-start | bytes 12582916
  35.2 2.2 %copy-start.2 = (bf16[1,2048,1024]{2,1,0:T(8,128)(2,1)S(1)}, bf16[1,2048,1024]{2,1,0:T(8,128)(2,1)}, u32[]{:S(2)}) copy-start(bf16[1,2048,1024]{2,1,0:T(8,128)(2,1)} %param.12) | copy-start | bytes 12582916
  37.4 2.2 %copy-start.3 = (bf16[1,1024,2048]{2,1,0:T(8,128)(2,1)S(1)}, bf16[1,1024,2048]{2,1,0:T(8,128)(2,1)}, u32[]{:S(2)}) copy-start(bf16[1,1024,2048]{2,1,0:T(8,128)(2,1)} %param.13) | copy-start | bytes 12582916
  42.2 7.9 %collective-permute-start.3 = (bf16[96,2048]{1,0:T(8,128)(2,1)S(1)}, bf16[96,2048]{1,0:T(8,128)(2,1)S(1)}, u32[]{:S(2)}, u32[]{:S(2)}) collective-permute-start(bf16[96,2048]{1,0:T(8,128)(2,1)S(1)} %get-tuple-element.14), channel_id=1, source_target_pairs={{0,1},{1,0},{2,3},{3,2},{4,5},{5,4},{6,7},{7,6},{8,9},{9,8},{10,11... | collective-permute-start | bytes 1179656 | tf_op jit(solution)/shard_map/ppermute | solution.py:179
  42.3 5.7 %copy-start.1 = (bf16[1,2048,1024]{2,1,0:T(8,128)(2,1)S(1)}, bf16[1,2048,1024]{2,1,0:T(8,128)(2,1)}, u32[]{:S(2)}) copy-start(bf16[1,2048,1024]{2,1,0:T(8,128)(2,1)} %param.11) | copy-start | bytes 12582916
  42.3 11.6 %collective-permute-start.4 = (bf16[96,2048]{1,0:T(8,128)(2,1)S(1)}, bf16[96,2048]{1,0:T(8,128)(2,1)S(1)}, u32[]{:S(2)}, u32[]{:S(2)}) collective-permute-start(bf16[96,2048]{1,0:T(8,128)(2,1)S(1)} %get-tuple-element.15), channel_id=1, source_target_pairs={{0,2},{1,3},{2,0},{3,1},{4,6},{5,7},{6,4},{7,5},{8,10},{9,11},{10,... | collective-permute-start | bytes 1179656 | tf_op jit(solution)/shard_map/ppermute | solution.py:179
  46.5 8.7 %collective-permute-start.6 = (bf16[96,2048]{1,0:T(8,128)(2,1)S(1)}, bf16[96,2048]{1,0:T(8,128)(2,1)S(1)}, u32[]{:S(2)}, u32[]{:S(2)}) collective-permute-start(bf16[96,2048]{1,0:T(8,128)(2,1)S(1)} %shard_map.76), channel_id=1, source_target_pairs={{0,3},{1,2},{2,1},{3,0},{4,7},{5,6},{6,5},{7,4},{8,11},{9,10},{10,... | collective-permute-start | bytes 1179656 | tf_op jit(solution)/shard_map/ppermute | solution.py:179
  48.0 7.2 %copy-start.6 = (s32[1,128,2]{1,2,0:T(2,128)S(1)}, s32[1,128,2]{1,2,0:T(2,128)}, u32[]{:S(2)}) copy-start(s32[1,128,2]{1,2,0:T(2,128)} %param.8) | copy-start | bytes 3076
  48.0 7.2 %copy-start.7 = (f32[1,128,2]{1,2,0:T(2,128)S(1)}, f32[1,128,2]{1,2,0:T(2,128)}, u32[]{:S(2)}) copy-start(f32[1,128,2]{1,2,0:T(2,128)} %param.9) | copy-start | bytes 3076

commit v2 on v0

--- a/solution.py
+++ b/solution.py
@@ -1,10 +1,15 @@
+import functools
+
 import jax
 import jax.numpy as jnp
 from jax import lax
+from jax.experimental import pallas as pl
+from jax.experimental.pallas import tpu as pltpu
 from jax.sharding import PartitionSpec as P
 
 NEXP = 4
 CAP = 96
+VMEM = pltpu.VMEM
 
 
 def shifted(value, axis, steps):
@@ -22,7 +27,7 @@
     )
 
 
-def local(acts, routes, gates, norm_gain, gate_w, up_w, down_w):
+def local_any(acts, routes, gates, norm_gain, gate_w, up_w, down_w):
     arrived = shifted(acts, "section", 1)[0]
     ids = routes[0]
     weights = gates[0]
@@ -57,6 +62,209 @@
     return result.reshape(1, tok_count, result.shape[-1])
 
 
+def spec(space=VMEM):
+    return pl.BlockSpec(memory_space=space)
+
+
+def call(body, outs, ins, limit=16, flops=0, scratch=()):
+    return pl.pallas_call(
+        body,
+        out_shape=outs,
+        in_specs=[spec()] * len(ins),
+        out_specs=[spec() for _ in outs],
+        scratch_shapes=scratch,
+        compiler_params=pltpu.CompilerParams(vmem_limit_bytes=limit << 20),
+        cost_estimate=pl.CostEstimate(flops=flops, bytes_accessed=0, transcendentals=0),
+    )(*ins)
+
+
+def like(shape, dtype=jnp.bfloat16):
+    return jax.ShapeDtypeStruct(shape, dtype)
+
+
+def flips(section):
+    odd = section % 2
+    return 1 + odd, 2 - odd
+
+
+def position():
+    me = lax.axis_index("expert")
+    return me, me ^ (2 - lax.rem(lax.axis_index("section"), 2))
+
+
+def table_body(ids, gates, gain, table, gain_out, ids_here, gates_here, done):
+    copies = [(ids, ids_here), (gates, gates_here), (gain, gain_out)]
+    copies = [pltpu.make_async_copy(source, target, done.at[n]) for n, (source, target) in enumerate(copies)]
+    for copy in copies:
+        copy.start()
+    for copy in copies:
+        copy.wait()
+    table[0:2, :] = ids_here[...].astype(jnp.float32)
+    table[2:4, :] = gates_here[...]
+    table[4:8, :] = jnp.zeros((4, table.shape[1]), jnp.float32)
+
+
+def tabled(ids, gates, gain):
+    ins = [pltpu.with_memory_space_constraint(v, pltpu.HBM) for v in (ids, gates, gain)]
+    return pl.pallas_call(
+        table_body,
+        out_shape=[like((8, ids.shape[1]), jnp.float32), like(gain.shape, gain.dtype)],
+        in_specs=[spec(pltpu.HBM)] * 3,
+        out_specs=[spec()] * 2,
+        scratch_shapes=[VMEM(ids.shape, ids.dtype), VMEM(gates.shape, gates.dtype), pltpu.SemaphoreType.DMA((3,))],
+        compiler_params=pltpu.CompilerParams(vmem_limit_bytes=4 << 20),
+        cost_estimate=pl.CostEstimate(flops=LONG, bytes_accessed=0, transcendentals=0),
+    )(*ins)
+
+
+OWN_HERE, OWN_SIDE, NEAR_HERE, NEAR_SIDE = range(4)
+
+
+def routing_body(own, near, place, place_t, weight_t):
+    me, side = position()
+    ask = [(own, me), (own, side), (near, me), (near, side)]
+    names = [(table[0:1, :] == g.astype(jnp.float32), table[1:2, :] == g.astype(jnp.float32)) for table, g in ask]
+    rows = [(first | second).astype(jnp.float32) for first, second in names]
+    member = jnp.concatenate(rows + [jnp.zeros_like(rows[0])] * (8 - len(rows)), axis=0)
+    tokens = member.shape[1]
+    before = lax.broadcasted_iota(jnp.int32, (tokens, tokens), 0)
+    at = lax.broadcasted_iota(jnp.int32, (tokens, tokens), 1)
+    upto = (before <= at).astype(jnp.bfloat16)
+    rank = jnp.dot(member.astype(jnp.bfloat16), upto, preferred_element_type=jnp.float32) - 1.0
+    slots = lax.broadcasted_iota(jnp.int32, (CAP, tokens), 0).astype(jnp.float32)
+    lanes = lax.broadcasted_iota(jnp.int32, (tokens, CAP), 1).astype(jnp.float32)
+    member_t, rank_t = member.T, rank.T
+    for k in range(len(ask)):
+        hit = (slots == rank[k : k + 1, :]) & (member[k : k + 1, :] > 0)
+        place[k * CAP : (k + 1) * CAP, :] = hit.astype(jnp.bfloat16)
+        hit = (lanes == rank_t[:, k : k + 1]) & (member_t[:, k : k + 1] > 0)
+        place_t[k * tokens : (k + 1) * tokens, :] = hit.astype(jnp.bfloat16)
+    weight = [
+        jnp.where(first, table[2:3, :], 0.0) + jnp.where(second, table[3:4, :], 0.0)
+        for (table, _), (first, second) in zip(ask, names)
+    ]
+    weight_t[...] = jnp.concatenate(weight + [jnp.zeros_like(weight[0])] * (8 - len(weight)), axis=0).T
+
+
+def routing(own, near):
+    tokens = own.shape[1]
+    outs = [like((4 * CAP, tokens)), like((4 * tokens, CAP)), like((tokens, 8), jnp.float32)]
+    return call(routing_body, outs, (own, near))
+
+
+def packed(place, k, rows):
+    hit = place[k * CAP : (k + 1) * CAP, :]
+    return jnp.dot(hit, rows[...], preferred_element_type=jnp.float32).astype(jnp.bfloat16)
+
+
+def pack_body(k, rows, place, after, out):
+    out[...] = packed(place, k, rows)
+
+
+def pack(k, rows, place, after):
+    return call(functools.partial(pack_body, k), [like((CAP, rows.shape[1]))], (rows, place, after))[0]
+
+
+def expert(rows, gain, wgate, wup, wdown):
+    xf = rows.astype(jnp.float32)
+    scale = lax.rsqrt(jnp.mean(xf * xf, axis=1, keepdims=True) + 1e-06)
+    x = (xf * scale * gain[...]).astype(jnp.bfloat16)
+    gpart = jnp.dot(x, wgate[...], preferred_element_type=jnp.float32)
+    upart = jnp.dot(x, wup[...], preferred_element_type=jnp.float32)
+    hidden = (gpart * jax.nn.sigmoid(gpart) * upart).astype(jnp.bfloat16)
+    return jnp.dot(hidden, wdown[...], preferred_element_type=jnp.float32).astype(jnp.bfloat16)
+
+
+def slots_body(rows, gain, wgate, wup, wdown, after, out):
+    out[...] = expert(rows[...], gain, wgate, wup, wdown)
+
+
+def slots(rows, gain, weights, after):
+    outs = [like((CAP, weights[2].shape[1]))]
+    return call(slots_body, outs, (rows, gain, *weights, after), flops=6 * CAP * weights[0].size)[0]
+
+
+def tokens_body(k, rows, place, gain, wgate, wup, wdown, after, out):
+    out[...] = expert(packed(place, k, rows), gain, wgate, wup, wdown)
+
+
+def tokens(k, rows, place, gain, weights, after):
+    outs = [like((CAP, weights[2].shape[1]))]
+    ins = (rows, place, gain, *weights, after)
+    return call(functools.partial(tokens_body, k), outs, ins, flops=6 * CAP * weights[0].size)[0]
+
+
+STRIP = 256
+
+
+def spread_body(which, count, *refs):
+    bases, (place_t, weight_t, *parts), out = refs[:count], refs[count:-2], refs[-1]
+    size = weight_t.shape[0]
+    for at in range(0, out.shape[1], STRIP):
+        strip = slice(at, at + STRIP)
+        terms = [base[:, strip].astype(jnp.float32) for base in bases]
+        for k, part in zip(which, parts):
+            hit = place_t[k * size : (k + 1) * size, :]
+            terms.append(weight_t[:, k : k + 1] * jnp.dot(hit, part[:, strip], preferred_element_type=jnp.float32))
+        out[:, strip] = sum(terms[1:], terms[0]).astype(out.dtype)
+
+
+def spread(which, bases, place_t, weight_t, parts, dtype, after):
+    outs = [like((weight_t.shape[0], parts[0].shape[1]), dtype)]
+    body = functools.partial(spread_body, which, len(bases))
+    return call(body, outs, (*bases, place_t, weight_t, *parts, after))[0]
+
+
+def added_body(left, right, out):
+    for at in range(0, out.shape[1], STRIP):
+        strip = slice(at, at + STRIP)
+        out[:, strip] = (left[:, strip] + right[:, strip].astype(jnp.float32)).astype(out.dtype)
+
+
+def moved(value, back, flip):
+    sections, experts = lax.axis_size("section"), lax.axis_size("expert")
+    pairs = [
+        ((s - back) % sections * experts + (e ^ flip(s)), s * experts + e)
+        for s in range(sections)
+        for e in range(experts)
+    ]
+    return lax.ppermute(value, ("section", "expert"), pairs)
+
+
+def near_flip(section):
+    return flips(section)[0]
+
+
+def side_flip(section):
+    return flips(section)[1]
+
+
+LONG = 20_000_000_000
+
+
+def local_square(acts, routes, gates, norm_gain, gate_w, up_w, down_w):
+    weights = (gate_w[0], up_w[0], down_w[0])
+    near_rows = moved(acts[0], 1, near_flip)
+    table, gain = tabled(routes[0].T, gates[0].T, norm_gain)
+    near_table = moved(table, 0, near_flip)
+    rows = moved(acts[0], 1, lambda s: 0)
+    place, place_t, weight_t = routing(table, near_table)
+    onward = pack(NEAR_SIDE, near_rows, place, near_rows)
+    far_rows = moved(onward, 0, side_flip)
+    near_out = tokens(NEAR_HERE, near_rows, place, gain, weights, onward)
+    side_send = pack(OWN_SIDE, rows, place, near_out)
+    side_rows = moved(side_send, 0, side_flip)
+    far_out = slots(far_rows, gain, weights, side_send)
+    on_out = moved(far_out, 0, side_flip)
+    side_out = slots(side_rows, gain, weights, far_out)
+    from_side = moved(side_out, 0, side_flip)
+    back = spread((NEAR_HERE, NEAR_SIDE), (), place_t, weight_t, (near_out, on_out), jnp.bfloat16, side_out)
+    from_near = moved(back, 0, near_flip)
+    here = tokens(OWN_HERE, rows, place, gain, weights, back)
+    total = spread((OWN_HERE, OWN_SIDE), (rows,), place_t, weight_t, (here, from_side), jnp.float32, here)
+    return call(added_body, [like(total.shape)], (total, from_near))[0][None]
+
+
 def solution(mesh):
     in_specs = (
         P("section", "expert", None),
@@ -68,4 +276,5 @@
         P("section", "expert", None),
     )
     out_specs = P("section", "expert", None)
+    local = local_square if mesh.shape["expert"] == NEXP else local_any
     return jax.shard_map(local, mesh=mesh, in_specs=in_specs, out_specs=out_specs, check_vma=False)

time: 67.7 us -> 43.9 us (0.65)
  blocking collectives: 21.5 us -> 0 us
  matrix products: 13.8 us -> 0 us
  Pallas kernels: 0 us -> 13.3 us
  starting transfers between devices: 4.15 us -> 15 us
  waiting for transfers between devices: 25.6 us -> 15.3 us
  other arithmetic: 2 us -> 0 us
    all_to_all x1 -> x0, blocking collectives: 21.5 us -> none  [local(): lax.all_to_all(outgoing, 'expert', split_axis=0, concat_axis=0, tiled=True)]
    all_to_all x1 -> x0, waiting for transfers between devices: 15.6 us -> none  [local(): lax.all_to_all(expert_rows(received, wgate, wup, wdown), 'expert', split_...]
    ppermute x1 -> x8, starting transfers between devices: 0.45 us -> 15 us  [moved(): return lax.ppermute(value, ('section', 'expert'), pairs)]
    dot_general x4 -> x0, matrix products: 13.8 us -> none  [the longest x1 8.58 us: expert_rows(): jnp.einsum('sch,hd->scd', hidden, wdown, preferred_element_type=jnp.float32)]
    pallas_call x0 -> x11, Pallas kernels: none -> 13.3 us  [the longest x10 12.4 us: call(): pl.pallas_call(body, out_shape=outs, in_specs=[spec()] * len(ins), out_sp...]
    ppermute x1 -> x8, waiting for transfers between devices: 10.1 us -> 15.3 us  [moved(): return lax.ppermute(value, ('section', 'expert'), pairs)]
    all_to_all x1 -> x0, starting transfers between devices: 3.69 us -> none  [local(): lax.all_to_all(expert_rows(received, wgate, wup, wdown), 'expert', split_...]
    convert_element_type x1 -> x0, other arithmetic: 0.92 us -> none  [local(): result = (xf + contrib).astype(jnp.bfloat16)]
  transfers between devices with their start and end apart: 2 -> 8, of which waited for: 2 -> 7; matrix products, arithmetic and copies ran while one was open for 2% -> 0% of each run, Pallas kernels for 0% -> 27%
where the time goes in v2:
time: 43.9 us; the launch traced here: 43.8 us
  waiting for transfers between devices  15.3 us (35%)
  starting transfers between devices  15 us (34%)
  Pallas kernels  13.3 us (30%)
    ppermute x8, waiting for transfers between devices, moved(): return lax.ppermute(value, ('section', 'expert'), pairs)  15.3 us
    ppermute x8, starting transfers between devices, moved(): return lax.ppermute(value, ('section', 'expert'), pairs)  15 us
    pallas_call x10, Pallas kernels, call(): pl.pallas_call(body, out_shape=outs, in_specs=[spec()] * len(ins), out_sp...  12.4 us
    pallas_call x1, Pallas kernels, tabled(): pl.pallas_call(table_body, out_shape=[like((8, ids.shape[1]), jnp.float32...  0.91 us
  transfers between devices with their start and end apart: 8, of which 7 were waited for; matrix products, arithmetic and copies ran while one was open for 0% of the time, Pallas kernels for 27%

profile of v2, /device:TPU:0, one launch (start us, length us, event | category | flops | bytes accessed | tf_op | source)
XLA Modules:
  0.0 43.8 jit_solution(11818195281775270383)
XLA Ops:
  0.0 2.4 %collective-permute-start.2 = (bf16[128,2048]{1,0:T(8,128)(2,1)}, bf16[128,2048]{1,0:T(8,128)(2,1)S(1)}, u32[]{:S(2)}, u32[]{:S(2)}) collective-permute-start(bf16[128,2048]{1,0:T(8,128)(2,1)} %bitcast.23), channel_id=1, source_target_pairs={{29,0},{28,1},{31,2},{30,3},{2,4},{3,5},{0,6},{1,7},{5,8},{4,9},{7... | collective-permute-start | bytes 1572872 | tf_op jit(solution)/shard_map/ppermute | solution.py:231
  2.4 1.7 %collective-permute-start = (bf16[128,2048]{1,0:T(8,128)(2,1)}, bf16[128,2048]{1,0:T(8,128)(2,1)S(1)}, u32[]{:S(2)}, u32[]{:S(2)}) collective-permute-start(bf16[128,2048]{1,0:T(8,128)(2,1)} %bitcast.24), channel_id=1, source_target_pairs={{28,0},{29,1},{30,2},{31,3},{0,4},{1,5},{2,6},{3,7},{4,8},{5,9},{6... | collective-permute-start | bytes 1572872 | tf_op jit(solution)/shard_map/ppermute | solution.py:231
  4.1 0.0 copy-start
  4.1 0.0 copy-start.1
  4.1 0.0 copy-start.2
  4.1 0.9 %shard_map.73 = (f32[8,128]{1,0:T(8,128)S(1)}, f32[1,2048]{1,0:T(1,128)S(1)}) custom-call(s32[2,128]{1,0:T(2,128)} %bitcast.25, f32[2,128]{1,0:T(2,128)} %bitcast.26, f32[1,2048]{1,0:T(1,128)} %gain.1), custom_call_target="tpu_custom_call" | custom-call | flops 20000000000 | tf_op jit(solution)/shard_map/pallas_call | solution.py:109
  5.0 0.6 %collective-permute-start.1 = (f32[8,128]{1,0:T(8,128)S(1)}, f32[8,128]{1,0:T(8,128)S(1)}, u32[]{:S(2)}, u32[]{:S(2)}) collective-permute-start(f32[8,128]{1,0:T(8,128)S(1)} %get-tuple-element.10.own), channel_id=1, source_target_pairs={{1,0},{0,1},{3,2},{2,3},{6,4},{7,5},{4,6},{5,7},{9,8},{8,9},{11,10... | collective-permute-start | bytes 12296 | tf_op jit(solution)/shard_map/ppermute | solution.py:231
  5.6 3.5 %collective-permute-done.1.near = f32[8,128]{1,0:T(8,128)S(1)} collective-permute-done((f32[8,128]{1,0:T(8,128)S(1)}, f32[8,128]{1,0:T(8,128)S(1)}, u32[]{:S(2)}, u32[]{:S(2)}) %collective-permute-start.1) | collective-permute-done | bytes 4128 | tf_op jit(solution)/shard_map/ppermute | solution.py:231
  9.1 0.5 %shard_map.74 = (bf16[384,128]{1,0:T(8,128)(2,1)S(1)}, bf16[512,96]{1,0:T(8,128)(2,1)S(1)}, f32[128,8]{1,0:T(8,128)S(1)}) custom-call(f32[8,128]{1,0:T(8,128)S(1)} %get-tuple-element.10.own, f32[8,128]{1,0:T(8,128)S(1)} %collective-permute-done.1.near), custom_call_target="tpu_custom_call" | custom-call | tf_op jit(solution)/shard_map/pallas_call | solution.py:70
  9.5 3.0 %collective-permute-done.2.rows.after = bf16[128,2048]{1,0:T(8,128)(2,1)S(1)} collective-permute-done((bf16[128,2048]{1,0:T(8,128)(2,1)}, bf16[128,2048]{1,0:T(8,128)(2,1)S(1)}, u32[]{:S(2)}, u32[]{:S(2)}) %collective-permute-start.2) | collective-permute-done | bytes 524320 | tf_op jit(solution)/shard_map/ppermute | solution.py:231
  12.5 0.3 shard_map.75.after
  12.8 2.1 %collective-permute-start.3 = (bf16[96,2048]{1,0:T(8,128)(2,1)S(1)}, bf16[96,2048]{1,0:T(8,128)(2,1)S(1)}, u32[]{:S(2)}, u32[]{:S(2)}) collective-permute-start(bf16[96,2048]{1,0:T(8,128)(2,1)S(1)} %shard_map.75.after), channel_id=1, source_target_pairs={{2,0},{3,1},{0,2},{1,3},{5,4},{4,5},{7,6},{6,7},{10,8},{11,9},{8,1... | collective-permute-start | bytes 1179656 | tf_op jit(solution)/shard_map/ppermute | solution.py:231
  14.9 0.0 copy-done
  14.9 0.0 copy-done.1
  14.9 0.0 copy-done.2
  14.9 2.5 %shard_map.76.after.refs_2_ = bf16[96,2048]{1,0:T(8,128)(2,1)S(1)} custom-call(bf16[128,2048]{1,0:T(8,128)(2,1)S(1)} %collective-permute-done.2.rows.after, bf16[384,128]{1,0:T(8,128)(2,1)S(1)} %get-tuple-element.13.place, f32[1,2048]{1,0:T(1,128)S(1)} %get-tuple-element.14.gain, bf16[2048,1024]{1,0:T(8,128)(2,1)S(1)} %bitcast.11, ...), custom_call_target="tpu_custom_call" | custom-call | flops 1207959552 | tf_op jit(solution)/shard_map/pallas_call | solution.py:70
  17.4 1.2 %collective-permute-done.rows.refs_0_ = bf16[128,2048]{1,0:T(8,128)(2,1)S(1)} collective-permute-done((bf16[128,2048]{1,0:T(8,128)(2,1)}, bf16[128,2048]{1,0:T(8,128)(2,1)S(1)}, u32[]{:S(2)}, u32[]{:S(2)}) %collective-permute-start) | collective-permute-done | bytes 524320 | tf_op jit(solution)/shard_map/ppermute | solution.py:231
  18.6 0.3 shard_map.77.after
  18.9 1.6 %collective-permute-start.5 = (bf16[96,2048]{1,0:T(8,128)(2,1)S(1)}, bf16[96,2048]{1,0:T(8,128)(2,1)S(1)}, u32[]{:S(2)}, u32[]{:S(2)}) collective-permute-start(bf16[96,2048]{1,0:T(8,128)(2,1)S(1)} %shard_map.77.after), channel_id=1, source_target_pairs={{2,0},{3,1},{0,2},{1,3},{5,4},{4,5},{7,6},{6,7},{10,8},{11,9},{8,1... | collective-permute-start | bytes 1179656 | tf_op jit(solution)/shard_map/ppermute | solution.py:231
  20.5 0.2 collective-permute-done.3.rows
  20.6 2.3 %shard_map.78.after = bf16[96,2048]{1,0:T(8,128)(2,1)S(1)} custom-call(bf16[96,2048]{1,0:T(8,128)(2,1)S(1)} %collective-permute-done.3.rows, f32[1,2048]{1,0:T(1,128)S(1)} %get-tuple-element.14.gain, bf16[2048,1024]{1,0:T(8,128)(2,1)S(1)} %bitcast.12, bf16[2048,1024]{1,0:T(8,128)(2,1)S(1)} %bitcast.16, bf16[1024,2048]{1,0:T(8,128)(2,1)S(1)} %bitcast.20, ...), custom_call_target="tpu_custom_call" | custom-call | flops 1207959552 | tf_op jit(solution)/shard_map/pallas_call | solution.py:70
  22.9 2.1 %collective-permute-start.4 = (bf16[96,2048]{1,0:T(8,128)(2,1)S(1)}, bf16[96,2048]{1,0:T(8,128)(2,1)S(1)}, u32[]{:S(2)}, u32[]{:S(2)}) collective-permute-start(bf16[96,2048]{1,0:T(8,128)(2,1)S(1)} %shard_map.78.after), channel_id=1, source_target_pairs={{2,0},{3,1},{0,2},{1,3},{5,4},{4,5},{7,6},{6,7},{10,8},{11,9},{8,1... | collective-permute-start | bytes 1179656 | tf_op jit(solution)/shard_map/ppermute | solution.py:231
  25.0 1.7 %collective-permute-done.5.rows = bf16[96,2048]{1,0:T(8,128)(2,1)S(1)} collective-permute-done((bf16[96,2048]{1,0:T(8,128)(2,1)S(1)}, bf16[96,2048]{1,0:T(8,128)(2,1)S(1)}, u32[]{:S(2)}, u32[]{:S(2)}) %collective-permute-start.5) | collective-permute-done | bytes 393248 | tf_op jit(solution)/shard_map/ppermute | solution.py:231
  26.7 2.3 %shard_map.79.refs_4_ = bf16[96,2048]{1,0:T(8,128)(2,1)S(1)} custom-call(bf16[96,2048]{1,0:T(8,128)(2,1)S(1)} %collective-permute-done.5.rows, f32[1,2048]{1,0:T(1,128)S(1)} %get-tuple-element.14.gain, bf16[2048,1024]{1,0:T(8,128)(2,1)S(1)} %bitcast.13, bf16[2048,1024]{1,0:T(8,128)(2,1)S(1)} %bitcast.17, bf16[1024,2048]{1,0:T(8,128)(2,1)S(1)} %bitcast.21, ...), custom_call_target="tpu_custom_call" | custom-call | flops 1207959552 | tf_op jit(solution)/shard_map/pallas_call | solution.py:70
  29.0 2.1 %collective-permute-done.4.refs_3_ = bf16[96,2048]{1,0:T(8,128)(2,1)S(1)} collective-permute-done((bf16[96,2048]{1,0:T(8,128)(2,1)S(1)}, bf16[96,2048]{1,0:T(8,128)(2,1)S(1)}, u32[]{:S(2)}, u32[]{:S(2)}) %collective-permute-start.4) | collective-permute-done | bytes 393248 | tf_op jit(solution)/shard_map/ppermute | solution.py:231
  31.1 0.4 shard_map.80.after
  31.5 3.1 %collective-permute-start.7 = (bf16[128,2048]{1,0:T(8,128)(2,1)S(1)}, bf16[128,2048]{1,0:T(8,128)(2,1)S(1)}, u32[]{:S(2)}, u32[]{:S(2)}) collective-permute-start(bf16[128,2048]{1,0:T(8,128)(2,1)S(1)} %shard_map.80.after), channel_id=1, source_target_pairs={{1,0},{0,1},{3,2},{2,3},{6,4},{7,5},{4,6},{5,7},{9,8},{8,9},{11,10... | collective-permute-start | bytes 1572872 | tf_op jit(solution)/shard_map/ppermute | solution.py:231
  34.6 1.6 %collective-permute-start.6 = (bf16[96,2048]{1,0:T(8,128)(2,1)S(1)}, bf16[96,2048]{1,0:T(8,128)(2,1)S(1)}, u32[]{:S(2)}, u32[]{:S(2)}) collective-permute-start(bf16[96,2048]{1,0:T(8,128)(2,1)S(1)} %shard_map.79.refs_4_), channel_id=1, source_target_pairs={{2,0},{3,1},{0,2},{1,3},{5,4},{4,5},{7,6},{6,7},{10,8},{11,9},{8,1... | collective-permute-start | bytes 1179656 | tf_op jit(solution)/shard_map/ppermute | solution.py:231
  36.2 2.5 %shard_map.81.refs_3_.refs_5_ = bf16[96,2048]{1,0:T(8,128)(2,1)S(1)} custom-call(bf16[128,2048]{1,0:T(8,128)(2,1)S(1)} %collective-permute-done.rows.refs_0_, bf16[384,128]{1,0:T(8,128)(2,1)S(1)} %get-tuple-element.13.place, f32[1,2048]{1,0:T(1,128)S(1)} %get-tuple-element.14.gain, bf16[2048,1024]{1,0:T(8,128)(2,1)S(1)} %bitcast.14, ...), custom_call_target="tpu_custom_call" | custom-call | flops 1207959552 | tf_op jit(solution)/shard_map/pallas_call | solution.py:70
  38.7 3.7 %collective-permute-done.6.refs_4_ = bf16[96,2048]{1,0:T(8,128)(2,1)S(1)} collective-permute-done((bf16[96,2048]{1,0:T(8,128)(2,1)S(1)}, bf16[96,2048]{1,0:T(8,128)(2,1)S(1)}, u32[]{:S(2)}, u32[]{:S(2)}) %collective-permute-start.6) | collective-permute-done | bytes 393248 | tf_op jit(solution)/shard_map/ppermute | solution.py:231
  42.4 0.4 %shard_map.82.left = f32[128,2048]{1,0:T(8,128)S(1)} custom-call(bf16[128,2048]{1,0:T(8,128)(2,1)S(1)} %collective-permute-done.rows.refs_0_, bf16[512,96]{1,0:T(8,128)(2,1)S(1)} %get-tuple-element.11.refs_0_.refs_1_, f32[128,8]{1,0:T(8,128)S(1)} %get-tuple-element.12.refs_1_.refs_2_, bf16[96,2048]{1,0:T(8,128)(2,1)S(1)} %shard_map.81.refs_3_.refs_5_, ...), custom_call_target="tpu_custom_call" | custom-call | tf_op jit(solution)/shard_map/pallas_call | solution.py:70
  42.8 0.0 collective-permute-done.7.right
  42.8 0.9 %shard_map.83 = bf16[128,2048]{1,0:T(8,128)(2,1)} custom-call(f32[128,2048]{1,0:T(8,128)S(1)} %shard_map.82.left, bf16[128,2048]{1,0:T(8,128)(2,1)S(1)} %collective-permute-done.7.right), custom_call_target="tpu_custom_call" | custom-call | tf_op jit(solution)/shard_map/pallas_call | solution.py:70
Async XLA Ops:
  0.0 12.5 %collective-permute-start.2 = (bf16[128,2048]{1,0:T(8,128)(2,1)}, bf16[128,2048]{1,0:T(8,128)(2,1)S(1)}, u32[]{:S(2)}, u32[]{:S(2)}) collective-permute-start(bf16[128,2048]{1,0:T(8,128)(2,1)} %bitcast.23), channel_id=1, source_target_pairs={{29,0},{28,1},{31,2},{30,3},{2,4},{3,5},{0,6},{1,7},{5,8},{4,9},{7... | collective-permute-start | bytes 1572872 | tf_op jit(solution)/shard_map/ppermute | solution.py:231
  2.4 16.2 %collective-permute-start = (bf16[128,2048]{1,0:T(8,128)(2,1)}, bf16[128,2048]{1,0:T(8,128)(2,1)S(1)}, u32[]{:S(2)}, u32[]{:S(2)}) collective-permute-start(bf16[128,2048]{1,0:T(8,128)(2,1)} %bitcast.24), channel_id=1, source_target_pairs={{28,0},{29,1},{30,2},{31,3},{0,4},{1,5},{2,6},{3,7},{4,8},{5,9},{6... | collective-permute-start | bytes 1572872 | tf_op jit(solution)/shard_map/ppermute | solution.py:231
  4.1 10.8 %copy-start = (bf16[1,2048,1024]{2,1,0:T(8,128)(2,1)S(1)}, bf16[1,2048,1024]{2,1,0:T(8,128)(2,1)}, u32[]{:S(2)}) copy-start(bf16[1,2048,1024]{2,1,0:T(8,128)(2,1)} %param.11) | copy-start | bytes 12582916
  4.1 10.8 %copy-start.1 = (bf16[1,2048,1024]{2,1,0:T(8,128)(2,1)S(1)}, bf16[1,2048,1024]{2,1,0:T(8,128)(2,1)}, u32[]{:S(2)}) copy-start(bf16[1,2048,1024]{2,1,0:T(8,128)(2,1)} %param.12) | copy-start | bytes 12582916
  4.1 10.8 %copy-start.2 = (bf16[1,1024,2048]{2,1,0:T(8,128)(2,1)S(1)}, bf16[1,1024,2048]{2,1,0:T(8,128)(2,1)}, u32[]{:S(2)}) copy-start(bf16[1,1024,2048]{2,1,0:T(8,128)(2,1)} %param.13) | copy-start | bytes 12582916
  5.0 4.1 %collective-permute-start.1 = (f32[8,128]{1,0:T(8,128)S(1)}, f32[8,128]{1,0:T(8,128)S(1)}, u32[]{:S(2)}, u32[]{:S(2)}) collective-permute-start(f32[8,128]{1,0:T(8,128)S(1)} %get-tuple-element.10.own), channel_id=1, source_target_pairs={{1,0},{0,1},{3,2},{2,3},{6,4},{7,5},{4,6},{5,7},{9,8},{8,9},{11,10... | collective-permute-start | bytes 12296 | tf_op jit(solution)/shard_map/ppermute | solution.py:231
  12.8 7.8 %collective-permute-start.3 = (bf16[96,2048]{1,0:T(8,128)(2,1)S(1)}, bf16[96,2048]{1,0:T(8,128)(2,1)S(1)}, u32[]{:S(2)}, u32[]{:S(2)}) collective-permute-start(bf16[96,2048]{1,0:T(8,128)(2,1)S(1)} %shard_map.75.after), channel_id=1, source_target_pairs={{2,0},{3,1},{0,2},{1,3},{5,4},{4,5},{7,6},{6,7},{10,8},{11,9},{8,1... | collective-permute-start | bytes 1179656 | tf_op jit(solution)/shard_map/ppermute | solution.py:231
  18.9 7.8 %collective-permute-start.5 = (bf16[96,2048]{1,0:T(8,128)(2,1)S(1)}, bf16[96,2048]{1,0:T(8,128)(2,1)S(1)}, u32[]{:S(2)}, u32[]{:S(2)}) collective-permute-start(bf16[96,2048]{1,0:T(8,128)(2,1)S(1)} %shard_map.77.after), channel_id=1, source_target_pairs={{2,0},{3,1},{0,2},{1,3},{5,4},{4,5},{7,6},{6,7},{10,8},{11,9},{8,1... | collective-permute-start | bytes 1179656 | tf_op jit(solution)/shard_map/ppermute | solution.py:231
  22.9 8.2 %collective-permute-start.4 = (bf16[96,2048]{1,0:T(8,128)(2,1)S(1)}, bf16[96,2048]{1,0:T(8,128)(2,1)S(1)}, u32[]{:S(2)}, u32[]{:S(2)}) collective-permute-start(bf16[96,2048]{1,0:T(8,128)(2,1)S(1)} %shard_map.78.after), channel_id=1, source_target_pairs={{2,0},{3,1},{0,2},{1,3},{5,4},{4,5},{7,6},{6,7},{10,8},{11,9},{8,1... | collective-permute-start | bytes 1179656 | tf_op jit(solution)/shard_map/ppermute | solution.py:231
  31.5 11.3 %collective-permute-start.7 = (bf16[128,2048]{1,0:T(8,128)(2,1)S(1)}, bf16[128,2048]{1,0:T(8,128)(2,1)S(1)}, u32[]{:S(2)}, u32[]{:S(2)}) collective-permute-start(bf16[128,2048]{1,0:T(8,128)(2,1)S(1)} %shard_map.80.after), channel_id=1, source_target_pairs={{1,0},{0,1},{3,2},{2,3},{6,4},{7,5},{4,6},{5,7},{9,8},{8,9},{11,10... | collective-permute-start | bytes 1572872 | tf_op jit(solution)/shard_map/ppermute | solution.py:231
  34.6 7.8 %collective-permute-start.6 = (bf16[96,2048]{1,0:T(8,128)(2,1)S(1)}, bf16[96,2048]{1,0:T(8,128)(2,1)S(1)}, u32[]{:S(2)}, u32[]{:S(2)}) collective-permute-start(bf16[96,2048]{1,0:T(8,128)(2,1)S(1)} %shard_map.79.refs_4_), channel_id=1, source_target_pairs={{2,0},{3,1},{0,2},{1,3},{5,4},{4,5},{7,6},{6,7},{10,8},{11,9},{8,1... | collective-permute-start | bytes 1179656 | tf_op jit(solution)/shard_map/ppermute | solution.py:231

commit v3 on v2

--- a/solution.py
+++ b/solution.py
@@ -120,7 +120,9 @@
 OWN_HERE, OWN_SIDE, NEAR_HERE, NEAR_SIDE = range(4)
 
 
-def routing_body(own, near, place, place_t, weight_t):
+def routing_body(own, near, sent, place, place_t, weight_t, rows, done):
+    copy = pltpu.make_async_copy(sent, rows, done)
+    copy.start()
     me, side = position()
     ask = [(own, me), (own, side), (near, me), (near, side)]
     names = [(table[0:1, :] == g.astype(jnp.float32), table[1:2, :] == g.astype(jnp.float32)) for table, g in ask]
@@ -144,12 +146,21 @@
         for (table, _), (first, second) in zip(ask, names)
     ]
     weight_t[...] = jnp.concatenate(weight + [jnp.zeros_like(weight[0])] * (8 - len(weight)), axis=0).T
-
-
-def routing(own, near):
+    copy.wait()
+
+
+def routing(own, near, sent):
     tokens = own.shape[1]
-    outs = [like((4 * CAP, tokens)), like((4 * tokens, CAP)), like((tokens, 8), jnp.float32)]
-    return call(routing_body, outs, (own, near))
+    outs = [like((4 * CAP, tokens)), like((4 * tokens, CAP)), like((tokens, 8), jnp.float32), like(sent.shape)]
+    return pl.pallas_call(
+        routing_body,
+        out_shape=outs,
+        in_specs=[spec()] * 2 + [spec(pltpu.HBM)],
+        out_specs=[spec()] * 4,
+        scratch_shapes=[pltpu.SemaphoreType.DMA],
+        compiler_params=pltpu.CompilerParams(vmem_limit_bytes=8 << 20),
+        cost_estimate=pl.CostEstimate(flops=0, bytes_accessed=0, transcendentals=0),
+    )(own, near, pltpu.with_memory_space_constraint(sent, pltpu.HBM))
 
 
 def packed(place, k, rows):
@@ -175,13 +186,16 @@
     return jnp.dot(hidden, wdown[...], preferred_element_type=jnp.float32).astype(jnp.bfloat16)
 
 
-def slots_body(rows, gain, wgate, wup, wdown, after, out):
-    out[...] = expert(rows[...], gain, wgate, wup, wdown)
-
-
-def slots(rows, gain, weights, after):
-    outs = [like((CAP, weights[2].shape[1]))]
-    return call(slots_body, outs, (rows, gain, *weights, after), flops=6 * CAP * weights[0].size)[0]
+def slots_body(rows, gain, wgate, wup, wdown, after, *outs):
+    part = expert(rows[...], gain, wgate, wup, wdown)
+    width = outs[0].shape[1]
+    for n, out in enumerate(outs):
+        out[...] = part[:, n * width : (n + 1) * width]
+
+
+def slots(rows, gain, weights, after, pieces):
+    outs = [like((CAP, weights[2].shape[1] // pieces))] * pieces
+    return call(slots_body, outs, (rows, gain, *weights, after), flops=6 * CAP * weights[0].size)
 
 
 def tokens_body(k, rows, place, gain, wgate, wup, wdown, after, out):
@@ -197,28 +211,53 @@
 STRIP = 256
 
 
-def spread_body(which, count, *refs):
+def spread_body(which, count, first, *refs):
     bases, (place_t, weight_t, *parts), out = refs[:count], refs[count:-2], refs[-1]
-    size = weight_t.shape[0]
-    for at in range(0, out.shape[1], STRIP):
+    size, width = weight_t.shape[0], out.shape[1]
+    for at in range(0, width, STRIP):
         strip = slice(at, at + STRIP)
         terms = [base[:, strip].astype(jnp.float32) for base in bases]
         for k, part in zip(which, parts):
             hit = place_t[k * size : (k + 1) * size, :]
-            terms.append(weight_t[:, k : k + 1] * jnp.dot(hit, part[:, strip], preferred_element_type=jnp.float32))
+            begin = at if part.shape[1] == width else first + at
+            rows = jnp.dot(hit, part[:, begin : begin + STRIP], preferred_element_type=jnp.float32)
+            terms.append(weight_t[:, k : k + 1] * rows)
         out[:, strip] = sum(terms[1:], terms[0]).astype(out.dtype)
 
 
-def spread(which, bases, place_t, weight_t, parts, dtype, after):
-    outs = [like((weight_t.shape[0], parts[0].shape[1]), dtype)]
-    body = functools.partial(spread_body, which, len(bases))
+def spread(which, bases, place_t, weight_t, parts, dtype, after, columns):
+    outs = [like((weight_t.shape[0], columns.stop - columns.start), dtype)]
+    body = functools.partial(spread_body, which, len(bases), columns.start)
     return call(body, outs, (*bases, place_t, weight_t, *parts, after))[0]
 
 
-def added_body(left, right, out):
-    for at in range(0, out.shape[1], STRIP):
-        strip = slice(at, at + STRIP)
-        out[:, strip] = (left[:, strip] + right[:, strip].astype(jnp.float32)).astype(out.dtype)
+def added_body(total, left, right, out, here, done):
+    half = left.shape[1]
+    copies = []
+    for n, at in enumerate(range(0, out.shape[1], WIDE)):
+        strip = slice(at, at + WIDE)
+        more = (left if at < half else right)[:, at % half : at % half + WIDE]
+        here[:, strip] = (total[:, strip] + more.astype(jnp.float32)).astype(out.dtype)
+        copies.append(pltpu.make_async_copy(here.at[:, pl.ds(at, WIDE)], out.at[:, pl.ds(at, WIDE)], done.at[n]))
+        copies[-1].start()
+    for copy in copies:
+        copy.wait()
+
+
+WIDE = 512
+
+
+def added(total, left, right, dtype):
+    out = like(total.shape, dtype)
+    return pl.pallas_call(
+        added_body,
+        out_shape=out,
+        in_specs=[spec()] * 3,
+        out_specs=spec(pltpu.HBM),
+        scratch_shapes=[VMEM(out.shape, dtype), pltpu.SemaphoreType.DMA((total.shape[1] // WIDE,))],
+        compiler_params=pltpu.CompilerParams(vmem_limit_bytes=8 << 20),
+        cost_estimate=pl.CostEstimate(flops=0, bytes_accessed=0, transcendentals=0),
+    )(total, left, right)
 
 
 def moved(value, back, flip):
@@ -247,22 +286,27 @@
     near_rows = moved(acts[0], 1, near_flip)
     table, gain = tabled(routes[0].T, gates[0].T, norm_gain)
     near_table = moved(table, 0, near_flip)
-    rows = moved(acts[0], 1, lambda s: 0)
-    place, place_t, weight_t = routing(table, near_table)
+    place, place_t, weight_t, sent = routing(table, near_table, acts[0])
+    rows = moved(sent, 1, lambda s: 0)
     onward = pack(NEAR_SIDE, near_rows, place, near_rows)
     far_rows = moved(onward, 0, side_flip)
     near_out = tokens(NEAR_HERE, near_rows, place, gain, weights, onward)
     side_send = pack(OWN_SIDE, rows, place, near_out)
     side_rows = moved(side_send, 0, side_flip)
-    far_out = slots(far_rows, gain, weights, side_send)
+    (far_out,) = slots(far_rows, gain, weights, side_send, 1)
     on_out = moved(far_out, 0, side_flip)
-    side_out = slots(side_rows, gain, weights, far_out)
+    (side_out,) = slots(side_rows, gain, weights, far_out, 1)
     from_side = moved(side_out, 0, side_flip)
-    back = spread((NEAR_HERE, NEAR_SIDE), (), place_t, weight_t, (near_out, on_out), jnp.bfloat16, side_out)
-    from_near = moved(back, 0, near_flip)
-    here = tokens(OWN_HERE, rows, place, gain, weights, back)
-    total = spread((OWN_HERE, OWN_SIDE), (rows,), place_t, weight_t, (here, from_side), jnp.float32, here)
-    return call(added_body, [like(total.shape)], (total, from_near))[0][None]
+    half, width = acts.shape[2] // 2, acts.shape[2]
+    both = (NEAR_HERE, NEAR_SIDE)
+    right = spread(both, (), place_t, weight_t, (near_out, on_out), jnp.bfloat16, side_out, slice(half, width))
+    left = spread(both, (), place_t, weight_t, (near_out, on_out), jnp.bfloat16, right, slice(0, half))
+    from_left = moved(left, 0, near_flip)
+    from_right = moved(right, 0, near_flip)
+    here = tokens(OWN_HERE, rows, place, gain, weights, left)
+    parts = (here, from_side)
+    total = spread((OWN_HERE, OWN_SIDE), (rows,), place_t, weight_t, parts, jnp.float32, here, slice(0, width))
+    return added(total, from_left, from_right, acts.dtype)[None]
 
 
 def solution(mesh):

time: 43.9 us -> 42.6 us (0.970)
  starting transfers between devices: 15 us -> 13.2 us
  Pallas kernels: 13.3 us -> 14 us
    pallas_call x0 -> x2, Pallas kernels: none -> 1.91 us  [the longest x1 1.06 us: routing(): pl.pallas_call(routing_body, out_shape=outs, in_specs=[spec()] * 2 + [spe...]
    ppermute x8 -> x9, starting transfers between devices: 15 us -> 13.2 us  [moved(): return lax.ppermute(value, ('section', 'expert'), pairs)]
    pallas_call x10 -> x9, Pallas kernels: 12.4 us -> 11.2 us  [call(): pl.pallas_call(body, out_shape=outs, in_specs=[spec()] * len(ins), out_sp...]
    ppermute x8 -> x9, waiting for transfers between devices: 15.3 us -> 15.1 us  [moved(): return lax.ppermute(value, ('section', 'expert'), pairs)]
  transfers between devices with their start and end apart: 8 -> 9, of which waited for: 7 -> 7; matrix products, arithmetic and copies ran while one was open for 0% -> 0% of each run, Pallas kernels for 27% -> 31%
where the time goes in v3:
time: 42.6 us; the launch traced here: 42.4 us
  waiting for transfers between devices  15.1 us (35%)
  Pallas kernels  14 us (33%)
  starting transfers between devices  13.2 us (31%)
    ppermute x9, waiting for transfers between devices, moved(): return lax.ppermute(value, ('section', 'expert'), pairs)  15.1 us
    ppermute x9, starting transfers between devices, moved(): return lax.ppermute(value, ('section', 'expert'), pairs)  13.2 us
    pallas_call x9, Pallas kernels, call(): pl.pallas_call(body, out_shape=outs, in_specs=[spec()] * len(ins), out_sp...  11.2 us
    pallas_call x1, Pallas kernels, routing(): pl.pallas_call(routing_body, out_shape=outs, in_specs=[spec()] * 2 + [spe...  1.06 us
    pallas_call x1, Pallas kernels, tabled(): pl.pallas_call(table_body, out_shape=[like((8, ids.shape[1]), jnp.float32...  0.91 us
  transfers between devices with their start and end apart: 9, of which 7 were waited for; matrix products, arithmetic and copies ran while one was open for 0% of the time, Pallas kernels for 31%

profile of v3, /device:TPU:0, one launch (start us, length us, event | category | flops | bytes accessed | tf_op | source)
XLA Modules:
  0.0 42.4 jit_solution(13535733099149879379)
XLA Ops:
  0.0 2.4 %collective-permute-start.2 = (bf16[128,2048]{1,0:T(8,128)(2,1)}, bf16[128,2048]{1,0:T(8,128)(2,1)S(1)}, u32[]{:S(2)}, u32[]{:S(2)}) collective-permute-start(bf16[128,2048]{1,0:T(8,128)(2,1)} %bitcast.23), channel_id=1, source_target_pairs={{29,0},{28,1},{31,2},{30,3},{2,4},{3,5},{0,6},{1,7},{5,8},{4,9},{7... | collective-permute-start | bytes 1572872 | tf_op jit(solution)/shard_map/ppermute | solution.py:270
  2.4 0.0 copy-start
  2.4 0.0 copy-start.1
  2.4 0.0 copy-start.2
  2.4 0.9 %shard_map.73 = (f32[8,128]{1,0:T(8,128)S(1)}, f32[1,2048]{1,0:T(1,128)S(1)}) custom-call(s32[2,128]{1,0:T(2,128)} %bitcast.25, f32[2,128]{1,0:T(2,128)} %bitcast.26, f32[1,2048]{1,0:T(1,128)} %gain.1), custom_call_target="tpu_custom_call" | custom-call | flops 20000000000 | tf_op jit(solution)/shard_map/pallas_call | solution.py:109
  3.3 1.6 %collective-permute-start = (f32[8,128]{1,0:T(8,128)S(1)}, f32[8,128]{1,0:T(8,128)S(1)}, u32[]{:S(2)}, u32[]{:S(2)}) collective-permute-start(f32[8,128]{1,0:T(8,128)S(1)} %get-tuple-element.11.own), channel_id=1, source_target_pairs={{1,0},{0,1},{3,2},{2,3},{6,4},{7,5},{4,6},{5,7},{9,8},{8,9},{11,10... | collective-permute-start | bytes 12296 | tf_op jit(solution)/shard_map/ppermute | solution.py:270
  4.9 2.5 %collective-permute-done.near = f32[8,128]{1,0:T(8,128)S(1)} collective-permute-done((f32[8,128]{1,0:T(8,128)S(1)}, f32[8,128]{1,0:T(8,128)S(1)}, u32[]{:S(2)}, u32[]{:S(2)}) %collective-permute-start) | collective-permute-done | bytes 4128 | tf_op jit(solution)/shard_map/ppermute | solution.py:270
  7.4 1.1 %shard_map.74 = (bf16[384,128]{1,0:T(8,128)(2,1)S(1)}, bf16[512,96]{1,0:T(8,128)(2,1)S(1)}, f32[128,8]{1,0:T(8,128)S(1)}, bf16[128,2048]{1,0:T(8,128)(2,1)S(1)}) custom-call(f32[8,128]{1,0:T(8,128)S(1)} %get-tuple-element.11.own, f32[8,128]{1,0:T(8,128)S(1)} %collective-permute-done.near, bf16[128,2048]{1,0:T(8,128)(2,1)} %bitcast.24), custom_call_target="tpu_custom_call" | custom-call | tf_op jit(solution)/shard_map/pallas_call | solution.py:155
  8.5 0.6 %collective-permute-start.1 = (bf16[128,2048]{1,0:T(8,128)(2,1)S(1)}, bf16[128,2048]{1,0:T(8,128)(2,1)S(1)}, u32[]{:S(2)}, u32[]{:S(2)}) collective-permute-start(bf16[128,2048]{1,0:T(8,128)(2,1)S(1)} %get-tuple-element.12), channel_id=1, source_target_pairs={{28,0},{29,1},{30,2},{31,3},{0,4},{1,5},{2,6},{3,7},{4,8},{5,9},{6... | collective-permute-start | bytes 1572872 | tf_op jit(solution)/shard_map/ppermute | solution.py:270
  9.0 3.5 %collective-permute-done.2.rows.after = bf16[128,2048]{1,0:T(8,128)(2,1)S(1)} collective-permute-done((bf16[128,2048]{1,0:T(8,128)(2,1)}, bf16[128,2048]{1,0:T(8,128)(2,1)S(1)}, u32[]{:S(2)}, u32[]{:S(2)}) %collective-permute-start.2) | collective-permute-done | bytes 524320 | tf_op jit(solution)/shard_map/ppermute | solution.py:270
  12.5 0.3 shard_map.75.after
  12.8 2.0 %collective-permute-start.3 = (bf16[96,2048]{1,0:T(8,128)(2,1)S(1)}, bf16[96,2048]{1,0:T(8,128)(2,1)S(1)}, u32[]{:S(2)}, u32[]{:S(2)}) collective-permute-start(bf16[96,2048]{1,0:T(8,128)(2,1)S(1)} %shard_map.75.after), channel_id=1, source_target_pairs={{2,0},{3,1},{0,2},{1,3},{5,4},{4,5},{7,6},{6,7},{10,8},{11,9},{8,1... | collective-permute-start | bytes 1179656 | tf_op jit(solution)/shard_map/ppermute | solution.py:270
  14.8 0.0 copy-done
  14.8 0.0 copy-done.1
  14.8 0.0 copy-done.2
  14.8 2.5 %shard_map.76.after.refs_2_ = bf16[96,2048]{1,0:T(8,128)(2,1)S(1)} custom-call(bf16[128,2048]{1,0:T(8,128)(2,1)S(1)} %collective-permute-done.2.rows.after, bf16[384,128]{1,0:T(8,128)(2,1)S(1)} %get-tuple-element.15.place, f32[1,2048]{1,0:T(1,128)S(1)} %get-tuple-element.16.gain, bf16[2048,1024]{1,0:T(8,128)(2,1)S(1)} %bitcast.11, ...), custom_call_target="tpu_custom_call" | custom-call | flops 1207959552 | tf_op jit(solution)/shard_map/pallas_call | solution.py:70
  17.3 1.6 %collective-permute-done.1.rows.refs_0_ = bf16[128,2048]{1,0:T(8,128)(2,1)S(1)} collective-permute-done((bf16[128,2048]{1,0:T(8,128)(2,1)S(1)}, bf16[128,2048]{1,0:T(8,128)(2,1)S(1)}, u32[]{:S(2)}, u32[]{:S(2)}) %collective-permute-start.1) | collective-permute-done | bytes 524320 | tf_op jit(solution)/shard_map/ppermute | solution.py:270
  18.9 0.3 shard_map.77.after
  19.2 1.3 %collective-permute-start.5 = (bf16[96,2048]{1,0:T(8,128)(2,1)S(1)}, bf16[96,2048]{1,0:T(8,128)(2,1)S(1)}, u32[]{:S(2)}, u32[]{:S(2)}) collective-permute-start(bf16[96,2048]{1,0:T(8,128)(2,1)S(1)} %shard_map.77.after), channel_id=1, source_target_pairs={{2,0},{3,1},{0,2},{1,3},{5,4},{4,5},{7,6},{6,7},{10,8},{11,9},{8,1... | collective-permute-start | bytes 1179656 | tf_op jit(solution)/shard_map/ppermute | solution.py:270
  20.5 0.2 collective-permute-done.3.rows
  20.6 2.3 %shard_map.78.after = bf16[96,2048]{1,0:T(8,128)(2,1)S(1)} custom-call(bf16[96,2048]{1,0:T(8,128)(2,1)S(1)} %collective-permute-done.3.rows, f32[1,2048]{1,0:T(1,128)S(1)} %get-tuple-element.16.gain, bf16[2048,1024]{1,0:T(8,128)(2,1)S(1)} %bitcast.12, bf16[2048,1024]{1,0:T(8,128)(2,1)S(1)} %bitcast.16, bf16[1024,2048]{1,0:T(8,128)(2,1)S(1)} %bitcast.20, ...), custom_call_target="tpu_custom_call" | custom-call | flops 1207959552 | tf_op jit(solution)/shard_map/pallas_call | solution.py:70
  22.9 2.0 %collective-permute-start.4 = (bf16[96,2048]{1,0:T(8,128)(2,1)S(1)}, bf16[96,2048]{1,0:T(8,128)(2,1)S(1)}, u32[]{:S(2)}, u32[]{:S(2)}) collective-permute-start(bf16[96,2048]{1,0:T(8,128)(2,1)S(1)} %shard_map.78.after), channel_id=1, source_target_pairs={{2,0},{3,1},{0,2},{1,3},{5,4},{4,5},{7,6},{6,7},{10,8},{11,9},{8,1... | collective-permute-start | bytes 1179656 | tf_op jit(solution)/shard_map/ppermute | solution.py:270
  25.0 2.1 %collective-permute-done.5.rows = bf16[96,2048]{1,0:T(8,128)(2,1)S(1)} collective-permute-done((bf16[96,2048]{1,0:T(8,128)(2,1)S(1)}, bf16[96,2048]{1,0:T(8,128)(2,1)S(1)}, u32[]{:S(2)}, u32[]{:S(2)}) %collective-permute-start.5) | collective-permute-done | bytes 393248 | tf_op jit(solution)/shard_map/ppermute | solution.py:270
  27.0 2.3 %shard_map.79.refs_4_ = bf16[96,2048]{1,0:T(8,128)(2,1)S(1)} custom-call(bf16[96,2048]{1,0:T(8,128)(2,1)S(1)} %collective-permute-done.5.rows, f32[1,2048]{1,0:T(1,128)S(1)} %get-tuple-element.16.gain, bf16[2048,1024]{1,0:T(8,128)(2,1)S(1)} %bitcast.13, bf16[2048,1024]{1,0:T(8,128)(2,1)S(1)} %bitcast.17, bf16[1024,2048]{1,0:T(8,128)(2,1)S(1)} %bitcast.21, ...), custom_call_target="tpu_custom_call" | custom-call | flops 1207959552 | tf_op jit(solution)/shard_map/pallas_call | solution.py:70
  29.3 1.3 %collective-permute-start.6 = (bf16[96,2048]{1,0:T(8,128)(2,1)S(1)}, bf16[96,2048]{1,0:T(8,128)(2,1)S(1)}, u32[]{:S(2)}, u32[]{:S(2)}) collective-permute-start(bf16[96,2048]{1,0:T(8,128)(2,1)S(1)} %shard_map.79.refs_4_), channel_id=1, source_target_pairs={{2,0},{3,1},{0,2},{1,3},{5,4},{4,5},{7,6},{6,7},{10,8},{11,9},{8,1... | collective-permute-start | bytes 1179656 | tf_op jit(solution)/shard_map/ppermute | solution.py:270
  30.6 0.8 %collective-permute-done.4.refs_3_ = bf16[96,2048]{1,0:T(8,128)(2,1)S(1)} collective-permute-done((bf16[96,2048]{1,0:T(8,128)(2,1)S(1)}, bf16[96,2048]{1,0:T(8,128)(2,1)S(1)}, u32[]{:S(2)}, u32[]{:S(2)}) %collective-permute-start.4) | collective-permute-done | bytes 393248 | tf_op jit(solution)/shard_map/ppermute | solution.py:270
  31.4 0.3 shard_map.80.refs_4_
  31.7 0.3 shard_map.81.after
  32.0 1.6 %collective-permute-start.7 = (bf16[128,1024]{1,0:T(8,128)(2,1)S(1)}, bf16[128,1024]{1,0:T(8,128)(2,1)S(1)}, u32[]{:S(2)}, u32[]{:S(2)}) collective-permute-start(bf16[128,1024]{1,0:T(8,128)(2,1)S(1)} %shard_map.81.after), channel_id=1, source_target_pairs={{1,0},{0,1},{3,2},{2,3},{6,4},{7,5},{4,6},{5,7},{9,8},{8,9},{11,10... | collective-permute-start | bytes 786440 | tf_op jit(solution)/shard_map/ppermute | solution.py:270
  33.6 0.4 %collective-permute-start.8 = (bf16[128,1024]{1,0:T(8,128)(2,1)S(1)}, bf16[128,1024]{1,0:T(8,128)(2,1)S(1)}, u32[]{:S(2)}, u32[]{:S(2)}) collective-permute-start(bf16[128,1024]{1,0:T(8,128)(2,1)S(1)} %shard_map.80.refs_4_), channel_id=1, source_target_pairs={{1,0},{0,1},{3,2},{2,3},{6,4},{7,5},{4,6},{5,7},{9,8},{8,9},{11,10... | collective-permute-start | bytes 786440 | tf_op jit(solution)/shard_map/ppermute | solution.py:270
  34.1 2.5 %shard_map.82.refs_3_.refs_5_ = bf16[96,2048]{1,0:T(8,128)(2,1)S(1)} custom-call(bf16[128,2048]{1,0:T(8,128)(2,1)S(1)} %collective-permute-done.1.rows.refs_0_, bf16[384,128]{1,0:T(8,128)(2,1)S(1)} %get-tuple-element.15.place, f32[1,2048]{1,0:T(1,128)S(1)} %get-tuple-element.16.gain, bf16[2048,1024]{1,0:T(8,128)(2,1)S(1)} %bitcast.14, ...), custom_call_target="tpu_custom_call" | custom-call | flops 1207959552 | tf_op jit(solution)/shard_map/pallas_call | solution.py:70
  36.6 4.5 %collective-permute-done.6.refs_4_ = bf16[96,2048]{1,0:T(8,128)(2,1)S(1)} collective-permute-done((bf16[96,2048]{1,0:T(8,128)(2,1)S(1)}, bf16[96,2048]{1,0:T(8,128)(2,1)S(1)}, u32[]{:S(2)}, u32[]{:S(2)}) %collective-permute-start.6) | collective-permute-done | bytes 393248 | tf_op jit(solution)/shard_map/ppermute | solution.py:270
  41.1 0.4 %shard_map.83.total = f32[128,2048]{1,0:T(8,128)S(1)} custom-call(bf16[128,2048]{1,0:T(8,128)(2,1)S(1)} %collective-permute-done.1.rows.refs_0_, bf16[512,96]{1,0:T(8,128)(2,1)S(1)} %get-tuple-element.13.refs_0_.refs_1_, f32[128,8]{1,0:T(8,128)S(1)} %get-tuple-element.14.refs_1_.refs_2_, bf16[96,2048]{1,0:T(8,128)(2,1)S(1)} %shard_map.82.refs_3_.refs_5_, ...), custom_call_target="tpu_custom_call" | custom-call | tf_op jit(solution)/shard_map/pallas_call | solution.py:70
  41.5 0.0 collective-permute-done.7.left
  41.5 0.0 collective-permute-done.8.right
  41.6 0.8 %shard_map.84 = bf16[128,2048]{1,0:T(8,128)(2,1)} custom-call(f32[128,2048]{1,0:T(8,128)S(1)} %shard_map.83.total, bf16[128,1024]{1,0:T(8,128)(2,1)S(1)} %collective-permute-done.7.left, bf16[128,1024]{1,0:T(8,128)(2,1)S(1)} %collective-permute-done.8.right), custom_call_target="tpu_custom_call" | custom-call | tf_op jit(solution)/shard_map/pallas_call | solution.py:252
Async XLA Ops:
  0.0 12.5 %collective-permute-start.2 = (bf16[128,2048]{1,0:T(8,128)(2,1)}, bf16[128,2048]{1,0:T(8,128)(2,1)S(1)}, u32[]{:S(2)}, u32[]{:S(2)}) collective-permute-start(bf16[128,2048]{1,0:T(8,128)(2,1)} %bitcast.23), channel_id=1, source_target_pairs={{29,0},{28,1},{31,2},{30,3},{2,4},{3,5},{0,6},{1,7},{5,8},{4,9},{7... | collective-permute-start | bytes 1572872 | tf_op jit(solution)/shard_map/ppermute | solution.py:270
  2.4 12.4 %copy-start = (bf16[1,2048,1024]{2,1,0:T(8,128)(2,1)S(1)}, bf16[1,2048,1024]{2,1,0:T(8,128)(2,1)}, u32[]{:S(2)}) copy-start(bf16[1,2048,1024]{2,1,0:T(8,128)(2,1)} %param.11) | copy-start | bytes 12582916
  2.4 12.4 %copy-start.1 = (bf16[1,2048,1024]{2,1,0:T(8,128)(2,1)S(1)}, bf16[1,2048,1024]{2,1,0:T(8,128)(2,1)}, u32[]{:S(2)}) copy-start(bf16[1,2048,1024]{2,1,0:T(8,128)(2,1)} %param.12) | copy-start | bytes 12582916
  2.4 12.4 %copy-start.2 = (bf16[1,1024,2048]{2,1,0:T(8,128)(2,1)S(1)}, bf16[1,1024,2048]{2,1,0:T(8,128)(2,1)}, u32[]{:S(2)}) copy-start(bf16[1,1024,2048]{2,1,0:T(8,128)(2,1)} %param.13) | copy-start | bytes 12582916
  3.3 4.1 %collective-permute-start = (f32[8,128]{1,0:T(8,128)S(1)}, f32[8,128]{1,0:T(8,128)S(1)}, u32[]{:S(2)}, u32[]{:S(2)}) collective-permute-start(f32[8,128]{1,0:T(8,128)S(1)} %get-tuple-element.11.own), channel_id=1, source_target_pairs={{1,0},{0,1},{3,2},{2,3},{6,4},{7,5},{4,6},{5,7},{9,8},{8,9},{11,10... | collective-permute-start | bytes 12296 | tf_op jit(solution)/shard_map/ppermute | solution.py:270
  8.5 10.5 %collective-permute-start.1 = (bf16[128,2048]{1,0:T(8,128)(2,1)S(1)}, bf16[128,2048]{1,0:T(8,128)(2,1)S(1)}, u32[]{:S(2)}, u32[]{:S(2)}) collective-permute-start(bf16[128,2048]{1,0:T(8,128)(2,1)S(1)} %get-tuple-element.12), channel_id=1, source_target_pairs={{28,0},{29,1},{30,2},{31,3},{0,4},{1,5},{2,6},{3,7},{4,8},{5,9},{6... | collective-permute-start | bytes 1572872 | tf_op jit(solution)/shard_map/ppermute | solution.py:270
  12.8 7.8 %collective-permute-start.3 = (bf16[96,2048]{1,0:T(8,128)(2,1)S(1)}, bf16[96,2048]{1,0:T(8,128)(2,1)S(1)}, u32[]{:S(2)}, u32[]{:S(2)}) collective-permute-start(bf16[96,2048]{1,0:T(8,128)(2,1)S(1)} %shard_map.75.after), channel_id=1, source_target_pairs={{2,0},{3,1},{0,2},{1,3},{5,4},{4,5},{7,6},{6,7},{10,8},{11,9},{8,1... | collective-permute-start | bytes 1179656 | tf_op jit(solution)/shard_map/ppermute | solution.py:270
  19.2 7.8 %collective-permute-start.5 = (bf16[96,2048]{1,0:T(8,128)(2,1)S(1)}, bf16[96,2048]{1,0:T(8,128)(2,1)S(1)}, u32[]{:S(2)}, u32[]{:S(2)}) collective-permute-start(bf16[96,2048]{1,0:T(8,128)(2,1)S(1)} %shard_map.77.after), channel_id=1, source_target_pairs={{2,0},{3,1},{0,2},{1,3},{5,4},{4,5},{7,6},{6,7},{10,8},{11,9},{8,1... | collective-permute-start | bytes 1179656 | tf_op jit(solution)/shard_map/ppermute | solution.py:270
  22.9 8.4 %collective-permute-start.4 = (bf16[96,2048]{1,0:T(8,128)(2,1)S(1)}, bf16[96,2048]{1,0:T(8,128)(2,1)S(1)}, u32[]{:S(2)}, u32[]{:S(2)}) collective-permute-start(bf16[96,2048]{1,0:T(8,128)(2,1)S(1)} %shard_map.78.after), channel_id=1, source_target_pairs={{2,0},{3,1},{0,2},{1,3},{5,4},{4,5},{7,6},{6,7},{10,8},{11,9},{8,1... | collective-permute-start | bytes 1179656 | tf_op jit(solution)/shard_map/ppermute | solution.py:270
  29.3 11.7 %collective-permute-start.6 = (bf16[96,2048]{1,0:T(8,128)(2,1)S(1)}, bf16[96,2048]{1,0:T(8,128)(2,1)S(1)}, u32[]{:S(2)}, u32[]{:S(2)}) collective-permute-start(bf16[96,2048]{1,0:T(8,128)(2,1)S(1)} %shard_map.79.refs_4_), channel_id=1, source_target_pairs={{2,0},{3,1},{0,2},{1,3},{5,4},{4,5},{7,6},{6,7},{10,8},{11,9},{8,1... | collective-permute-start | bytes 1179656 | tf_op jit(solution)/shard_map/ppermute | solution.py:270
  32.0 9.6 %collective-permute-start.7 = (bf16[128,1024]{1,0:T(8,128)(2,1)S(1)}, bf16[128,1024]{1,0:T(8,128)(2,1)S(1)}, u32[]{:S(2)}, u32[]{:S(2)}) collective-permute-start(bf16[128,1024]{1,0:T(8,128)(2,1)S(1)} %shard_map.81.after), channel_id=1, source_target_pairs={{1,0},{0,1},{3,2},{2,3},{6,4},{7,5},{4,6},{5,7},{9,8},{8,9},{11,10... | collective-permute-start | bytes 786440 | tf_op jit(solution)/shard_map/ppermute | solution.py:270
  33.6 7.9 %collective-permute-start.8 = (bf16[128,1024]{1,0:T(8,128)(2,1)S(1)}, bf16[128,1024]{1,0:T(8,128)(2,1)S(1)}, u32[]{:S(2)}, u32[]{:S(2)}) collective-permute-start(bf16[128,1024]{1,0:T(8,128)(2,1)S(1)} %shard_map.80.refs_4_), channel_id=1, source_target_pairs={{1,0},{0,1},{3,2},{2,3},{6,4},{7,5},{4,6},{5,7},{9,8},{8,9},{11,10... | collective-permute-start | bytes 786440 | tf_op jit(solution)/shard_map/ppermute | solution.py:270

commit v4 on v3

--- a/solution.py
+++ b/solution.py
@@ -117,14 +117,17 @@
     )(*ins)
 
 
-OWN_HERE, OWN_SIDE, NEAR_HERE, NEAR_SIDE = range(4)
-
-
-def routing_body(own, near, sent, place, place_t, weight_t, rows, done):
-    copy = pltpu.make_async_copy(sent, rows, done)
-    copy.start()
+PACKED = OWN_HERE, OWN_SIDE, NEAR_HERE, NEAR_SIDE = range(4)
+BACK_HERE, BACK_LEFT, BACK_RIGHT, LEFT_HERE, LEFT_ON, RIGHT_HERE, RIGHT_ON = range(7)
+
+
+def routing_body(own, near, beside, place, place_t, weight_t):
     me, side = position()
-    ask = [(own, me), (own, side), (near, me), (near, side)]
+    odd = lax.rem(lax.axis_index("section"), 2)
+    other = side ^ (3 - 3 * odd)
+    third = jnp.where(odd == 1, near[...], beside[...])
+    own, near = own[...], near[...]
+    ask = [(own, me), (own, side), (own, other), (near, me), (near, side), (third, me), (third, other)]
     names = [(table[0:1, :] == g.astype(jnp.float32), table[1:2, :] == g.astype(jnp.float32)) for table, g in ask]
     rows = [(first | second).astype(jnp.float32) for first, second in names]
     member = jnp.concatenate(rows + [jnp.zeros_like(rows[0])] * (8 - len(rows)), axis=0)
@@ -136,9 +139,10 @@
     slots = lax.broadcasted_iota(jnp.int32, (CAP, tokens), 0).astype(jnp.float32)
     lanes = lax.broadcasted_iota(jnp.int32, (tokens, CAP), 1).astype(jnp.float32)
     member_t, rank_t = member.T, rank.T
+    for n, k in enumerate((BACK_HERE, BACK_LEFT, LEFT_HERE, LEFT_ON)):
+        hit = (slots == rank[k : k + 1, :]) & (member[k : k + 1, :] > 0)
+        place[n * CAP : (n + 1) * CAP, :] = hit.astype(jnp.bfloat16)
     for k in range(len(ask)):
-        hit = (slots == rank[k : k + 1, :]) & (member[k : k + 1, :] > 0)
-        place[k * CAP : (k + 1) * CAP, :] = hit.astype(jnp.bfloat16)
         hit = (lanes == rank_t[:, k : k + 1]) & (member_t[:, k : k + 1] > 0)
         place_t[k * tokens : (k + 1) * tokens, :] = hit.astype(jnp.bfloat16)
     weight = [
@@ -146,21 +150,12 @@
         for (table, _), (first, second) in zip(ask, names)
     ]
     weight_t[...] = jnp.concatenate(weight + [jnp.zeros_like(weight[0])] * (8 - len(weight)), axis=0).T
-    copy.wait()
-
-
-def routing(own, near, sent):
+
+
+def routing(own, near, side):
     tokens = own.shape[1]
-    outs = [like((4 * CAP, tokens)), like((4 * tokens, CAP)), like((tokens, 8), jnp.float32), like(sent.shape)]
-    return pl.pallas_call(
-        routing_body,
-        out_shape=outs,
-        in_specs=[spec()] * 2 + [spec(pltpu.HBM)],
-        out_specs=[spec()] * 4,
-        scratch_shapes=[pltpu.SemaphoreType.DMA],
-        compiler_params=pltpu.CompilerParams(vmem_limit_bytes=8 << 20),
-        cost_estimate=pl.CostEstimate(flops=0, bytes_accessed=0, transcendentals=0),
-    )(own, near, pltpu.with_memory_space_constraint(sent, pltpu.HBM))
+    outs = [like((len(PACKED) * CAP, tokens)), like((7 * tokens, CAP)), like((tokens, 8), jnp.float32)]
+    return call(routing_body, outs, (own, near, side))
 
 
 def packed(place, k, rows):
@@ -186,16 +181,30 @@
     return jnp.dot(hidden, wdown[...], preferred_element_type=jnp.float32).astype(jnp.bfloat16)
 
 
-def slots_body(rows, gain, wgate, wup, wdown, after, *outs):
+def slots_body(rows, gain, wgate, wup, wdown, after, left, right):
     part = expert(rows[...], gain, wgate, wup, wdown)
-    width = outs[0].shape[1]
-    for n, out in enumerate(outs):
-        out[...] = part[:, n * width : (n + 1) * width]
-
-
-def slots(rows, gain, weights, after, pieces):
-    outs = [like((CAP, weights[2].shape[1] // pieces))] * pieces
+    left[...] = part[:, : left.shape[1]]
+    right[...] = part[:, left.shape[1] :]
+
+
+def slots(rows, gain, weights, after, cut):
+    outs = [like((CAP, cut)), like((CAP, weights[2].shape[1] - cut))]
     return call(slots_body, outs, (rows, gain, *weights, after), flops=6 * CAP * weights[0].size)
+
+
+def side_body(rows, gain, wgate, wup, wdown, near_out, after, left, right, keep):
+    part = expert(rows[...], gain, wgate, wup, wdown)
+    half = left.shape[1]
+    odd = lax.rem(lax.axis_index("section"), 2) == 1
+    left[...] = part[:, :half]
+    right[...] = jnp.where(odd, part[:, half:], near_out[:, half:])
+    keep[...] = jnp.where(odd, near_out[:, half:], part[:, half:])
+
+
+def sided(rows, gain, weights, near_out, after, cut):
+    rest = like((CAP, weights[2].shape[1] - cut))
+    outs = [like((CAP, cut)), rest, rest]
+    return call(side_body, outs, (rows, gain, *weights, near_out, after), flops=6 * CAP * weights[0].size)
 
 
 def tokens_body(k, rows, place, gain, wgate, wup, wdown, after, out):
@@ -225,39 +234,62 @@
         out[:, strip] = sum(terms[1:], terms[0]).astype(out.dtype)
 
 
-def spread(which, bases, place_t, weight_t, parts, dtype, after, columns):
+def spread(which, bases, place_t, weight_t, parts, dtype, after, columns, flops=0):
     outs = [like((weight_t.shape[0], columns.stop - columns.start), dtype)]
     body = functools.partial(spread_body, which, len(bases), columns.start)
-    return call(body, outs, (*bases, place_t, weight_t, *parts, after))[0]
-
-
-def added_body(total, left, right, out, here, done):
-    half = left.shape[1]
+    return call(body, outs, (*bases, place_t, weight_t, *parts, after), flops=flops)[0]
+
+
+def based_body(rows, place_t, weight_t, here, left, out):
+    half, size = left.shape[1], weight_t.shape[0]
+    for at in range(0, out.shape[1], STRIP):
+        strip = slice(at, at + STRIP)
+        total = rows[:, strip].astype(jnp.float32)
+        for k, part in ((BACK_HERE, here), (BACK_LEFT, left)):
+            if at < half or k == BACK_HERE:
+                hit = place_t[k * size : (k + 1) * size, :]
+                slots_here = jnp.dot(hit, part[:, strip], preferred_element_type=jnp.float32)
+                total = total + weight_t[:, k : k + 1] * slots_here
+        out[:, strip] = total
+
+
+def based(rows, place_t, weight_t, here, left):
+    return call(based_body, [like(rows.shape, jnp.float32)], (rows, place_t, weight_t, here, left), flops=LONG)[0]
+
+
+def last_body(base, place_t, weight_t, slots_right, left, right, out, here, done):
+    half, size = left.shape[1], weight_t.shape[0]
+    hit = place_t[BACK_RIGHT * size : (BACK_RIGHT + 1) * size, :]
+    weight = weight_t[:, BACK_RIGHT : BACK_RIGHT + 1]
     copies = []
     for n, at in enumerate(range(0, out.shape[1], WIDE)):
-        strip = slice(at, at + WIDE)
-        more = (left if at < half else right)[:, at % half : at % half + WIDE]
-        here[:, strip] = (total[:, strip] + more.astype(jnp.float32)).astype(out.dtype)
+        for begin in range(at, at + WIDE, STRIP):
+            first = begin if begin < half else begin - half
+            strip, within = slice(begin, begin + STRIP), slice(first, first + STRIP)
+            total = base[:, strip] + (left if begin < half else right)[:, within].astype(jnp.float32)
+            if begin >= half:
+                total += weight * jnp.dot(hit, slots_right[:, within], preferred_element_type=jnp.float32)
+            here[:, strip] = total.astype(out.dtype)
         copies.append(pltpu.make_async_copy(here.at[:, pl.ds(at, WIDE)], out.at[:, pl.ds(at, WIDE)], done.at[n]))
         copies[-1].start()
     for copy in copies:
         copy.wait()
 
 
-WIDE = 512
-
-
-def added(total, left, right, dtype):
-    out = like(total.shape, dtype)
+WIDE = 256
+
+
+def last(base, place_t, weight_t, slots_right, left, right, dtype):
+    out = like(base.shape, dtype)
     return pl.pallas_call(
-        added_body,
+        last_body,
         out_shape=out,
-        in_specs=[spec()] * 3,
+        in_specs=[spec()] * 6,
         out_specs=spec(pltpu.HBM),
-        scratch_shapes=[VMEM(out.shape, dtype), pltpu.SemaphoreType.DMA((total.shape[1] // WIDE,))],
+        scratch_shapes=[VMEM(out.shape, dtype), pltpu.SemaphoreType.DMA((base.shape[1] // WIDE,))],
         compiler_params=pltpu.CompilerParams(vmem_limit_bytes=8 << 20),
         cost_estimate=pl.CostEstimate(flops=0, bytes_accessed=0, transcendentals=0),
-    )(total, left, right)
+    )(base, place_t, weight_t, slots_right, left, right)
 
 
 def moved(value, back, flip):
@@ -279,34 +311,37 @@
 
 
 LONG = 20_000_000_000
+CUT = 5
 
 
 def local_square(acts, routes, gates, norm_gain, gate_w, up_w, down_w):
     weights = (gate_w[0], up_w[0], down_w[0])
     near_rows = moved(acts[0], 1, near_flip)
+    rows = moved(acts[0], 1, lambda s: 0)
     table, gain = tabled(routes[0].T, gates[0].T, norm_gain)
     near_table = moved(table, 0, near_flip)
-    place, place_t, weight_t, sent = routing(table, near_table, acts[0])
-    rows = moved(sent, 1, lambda s: 0)
+    side_table = moved(table, 0, side_flip)
+    place, place_t, weight_t = routing(table, near_table, side_table)
     onward = pack(NEAR_SIDE, near_rows, place, near_rows)
     far_rows = moved(onward, 0, side_flip)
     near_out = tokens(NEAR_HERE, near_rows, place, gain, weights, onward)
     side_send = pack(OWN_SIDE, rows, place, near_out)
     side_rows = moved(side_send, 0, side_flip)
-    (far_out,) = slots(far_rows, gain, weights, side_send, 1)
-    on_out = moved(far_out, 0, side_flip)
-    (side_out,) = slots(side_rows, gain, weights, far_out, 1)
-    from_side = moved(side_out, 0, side_flip)
-    half, width = acts.shape[2] // 2, acts.shape[2]
-    both = (NEAR_HERE, NEAR_SIDE)
-    right = spread(both, (), place_t, weight_t, (near_out, on_out), jnp.bfloat16, side_out, slice(half, width))
-    left = spread(both, (), place_t, weight_t, (near_out, on_out), jnp.bfloat16, right, slice(0, half))
+    width = acts.shape[2]
+    cut = width * CUT // 8
+    far_left, far_right = slots(far_rows, gain, weights, side_send, cut)
+    on_left = moved(far_left, 0, side_flip)
+    on_right = moved(far_right, 0, lambda s: side_flip(s) if s % 2 else near_flip(s))
+    left_slots, right_slots, keep = sided(side_rows, gain, weights, near_out, far_left, cut)
+    left_slots = moved(left_slots, 0, side_flip)
+    right_slots = moved(right_slots, 0, lambda s: side_flip(s) if s % 2 else near_flip(s))
+    left = spread((LEFT_HERE, LEFT_ON), (), place_t, weight_t, (near_out, on_left), jnp.bfloat16, keep, slice(0, cut))
+    right = spread((RIGHT_HERE, RIGHT_ON), (), place_t, weight_t, (keep, on_right), jnp.bfloat16, left, slice(cut, width))
     from_left = moved(left, 0, near_flip)
-    from_right = moved(right, 0, near_flip)
-    here = tokens(OWN_HERE, rows, place, gain, weights, left)
-    parts = (here, from_side)
-    total = spread((OWN_HERE, OWN_SIDE), (rows,), place_t, weight_t, parts, jnp.float32, here, slice(0, width))
-    return added(total, from_left, from_right, acts.dtype)[None]
+    from_right = moved(right, 0, lambda s: near_flip(s) if s % 2 else side_flip(s))
+    here = tokens(OWN_HERE, rows, place, gain, weights, right)
+    base = based(rows, place_t, weight_t, here, left_slots)
+    return last(base, place_t, weight_t, right_slots, from_left, from_right, acts.dtype)[None]
 
 
 def solution(mesh):

time: 42.6 us -> 41.7 us (0.979)
  waiting for transfers between devices: 15.1 us -> 10.3 us
  starting transfers between devices: 13.2 us -> 17.6 us
  Pallas kernels: 14 us -> 13.5 us
    ppermute x9 -> x12, waiting for transfers between devices: 15.1 us -> 10.3 us  [moved(): return lax.ppermute(value, ('section', 'expert'), pairs)]
    ppermute x9 -> x12, starting transfers between devices: 13.2 us -> 17.6 us  [moved(): return lax.ppermute(value, ('section', 'expert'), pairs)]
    pallas_call x2 -> x1, Pallas kernels: 1.91 us -> 0.93 us  [last(): pl.pallas_call(last_body, out_shape=out, in_specs=[spec()] * 6, out_specs...]
    pallas_call x9 -> x10, Pallas kernels: 11.2 us -> 11.7 us  [call(): pl.pallas_call(body, out_shape=outs, in_specs=[spec()] * len(ins), out_sp...]
  transfers between devices with their start and end apart: 9 -> 12, of which waited for: 7 -> 8; matrix products, arithmetic and copies ran while one was open for 0% -> 0% of each run, Pallas kernels for 31% -> 30%
where the time goes in v4:
time: 41.7 us; the launch traced here: 41.5 us
  starting transfers between devices  17.6 us (42%)
  Pallas kernels  13.5 us (32%)
  waiting for transfers between devices  10.3 us (25%)
    ppermute x12, starting transfers between devices, moved(): return lax.ppermute(value, ('section', 'expert'), pairs)  17.6 us
    pallas_call x10, Pallas kernels, call(): pl.pallas_call(body, out_shape=outs, in_specs=[spec()] * len(ins), out_sp...  11.7 us
    ppermute x12, waiting for transfers between devices, moved(): return lax.ppermute(value, ('section', 'expert'), pairs)  10.3 us
    pallas_call x1, Pallas kernels, last(): pl.pallas_call(last_body, out_shape=out, in_specs=[spec()] * 6, out_specs...  0.93 us
    pallas_call x1, Pallas kernels, tabled(): pl.pallas_call(table_body, out_shape=[like((8, ids.shape[1]), jnp.float32...  0.91 us
  transfers between devices with their start and end apart: 12, of which 8 were waited for; matrix products, arithmetic and copies ran while one was open for 0% of the time, Pallas kernels for 30%

profile of v4, /device:TPU:0, one launch (start us, length us, event | category | flops | bytes accessed | tf_op | source)
XLA Modules:
  0.0 41.5 jit_solution(13748996463984732496)
XLA Ops:
  0.0 2.4 %collective-permute-start.3 = (bf16[128,2048]{1,0:T(8,128)(2,1)}, bf16[128,2048]{1,0:T(8,128)(2,1)S(1)}, u32[]{:S(2)}, u32[]{:S(2)}) collective-permute-start(bf16[128,2048]{1,0:T(8,128)(2,1)} %bitcast.23), channel_id=1, source_target_pairs={{29,0},{28,1},{31,2},{30,3},{2,4},{3,5},{0,6},{1,7},{5,8},{4,9},{7... | collective-permute-start | bytes 1572872 | tf_op jit(solution)/shard_map/ppermute | solution.py:302
  2.4 1.7 %collective-permute-start = (bf16[128,2048]{1,0:T(8,128)(2,1)}, bf16[128,2048]{1,0:T(8,128)(2,1)S(1)}, u32[]{:S(2)}, u32[]{:S(2)}) collective-permute-start(bf16[128,2048]{1,0:T(8,128)(2,1)} %bitcast.24), channel_id=1, source_target_pairs={{28,0},{29,1},{30,2},{31,3},{0,4},{1,5},{2,6},{3,7},{4,8},{5,9},{6... | collective-permute-start | bytes 1572872 | tf_op jit(solution)/shard_map/ppermute | solution.py:302
  4.1 0.0 copy-start
  4.1 0.0 copy-start.1
  4.1 0.0 copy-start.2
  4.1 0.9 %shard_map.73 = (f32[8,128]{1,0:T(8,128)S(1)}, f32[1,2048]{1,0:T(1,128)S(1)}) custom-call(s32[2,128]{1,0:T(2,128)} %bitcast.25, f32[2,128]{1,0:T(2,128)} %bitcast.26, f32[1,2048]{1,0:T(1,128)} %gain.1), custom_call_target="tpu_custom_call" | custom-call | flops 20000000000 | tf_op jit(solution)/shard_map/pallas_call | solution.py:109
  5.0 1.6 %collective-permute-start.2 = (f32[8,128]{1,0:T(8,128)S(1)}, f32[8,128]{1,0:T(8,128)S(1)}, u32[]{:S(2)}, u32[]{:S(2)}) collective-permute-start(f32[8,128]{1,0:T(8,128)S(1)} %get-tuple-element.15.own), channel_id=1, source_target_pairs={{2,0},{3,1},{0,2},{1,3},{5,4},{4,5},{7,6},{6,7},{10,8},{11,9},{8,1... | collective-permute-start | bytes 12296 | tf_op jit(solution)/shard_map/ppermute | solution.py:302
  6.6 0.5 %collective-permute-start.1 = (f32[8,128]{1,0:T(8,128)S(1)}, f32[8,128]{1,0:T(8,128)S(1)}, u32[]{:S(2)}, u32[]{:S(2)}) collective-permute-start(f32[8,128]{1,0:T(8,128)S(1)} %get-tuple-element.15.own), channel_id=1, source_target_pairs={{1,0},{0,1},{3,2},{2,3},{6,4},{7,5},{4,6},{5,7},{9,8},{8,9},{11,10... | collective-permute-start | bytes 12296 | tf_op jit(solution)/shard_map/ppermute | solution.py:302
  7.1 3.3 %collective-permute-done.2.beside = f32[8,128]{1,0:T(8,128)S(1)} collective-permute-done((f32[8,128]{1,0:T(8,128)S(1)}, f32[8,128]{1,0:T(8,128)S(1)}, u32[]{:S(2)}, u32[]{:S(2)}) %collective-permute-start.2) | collective-permute-done | bytes 4128 | tf_op jit(solution)/shard_map/ppermute | solution.py:302
  10.4 0.1 collective-permute-done.1.near
  10.5 0.6 %shard_map.74 = (bf16[384,128]{1,0:T(8,128)(2,1)S(1)}, bf16[896,96]{1,0:T(8,128)(2,1)S(1)}, f32[128,8]{1,0:T(8,128)S(1)}) custom-call(f32[8,128]{1,0:T(8,128)S(1)} %get-tuple-element.15.own, f32[8,128]{1,0:T(8,128)S(1)} %collective-permute-done.1.near, f32[8,128]{1,0:T(8,128)S(1)} %collective-permute-done.2.beside), custom_call_target="tpu_custom_call" | custom-call | tf_op jit(solution)/shard_map/pallas_call | solution.py:70
  11.1 1.4 %collective-permute-done.3.rows.after = bf16[128,2048]{1,0:T(8,128)(2,1)S(1)} collective-permute-done((bf16[128,2048]{1,0:T(8,128)(2,1)}, bf16[128,2048]{1,0:T(8,128)(2,1)S(1)}, u32[]{:S(2)}, u32[]{:S(2)}) %collective-permute-start.3) | collective-permute-done | bytes 524320 | tf_op jit(solution)/shard_map/ppermute | solution.py:302
  12.6 0.3 shard_map.75.after
  12.8 2.1 %collective-permute-start.5 = (bf16[96,2048]{1,0:T(8,128)(2,1)S(1)}, bf16[96,2048]{1,0:T(8,128)(2,1)S(1)}, u32[]{:S(2)}, u32[]{:S(2)}) collective-permute-start(bf16[96,2048]{1,0:T(8,128)(2,1)S(1)} %shard_map.75.after), channel_id=1, source_target_pairs={{2,0},{3,1},{0,2},{1,3},{5,4},{4,5},{7,6},{6,7},{10,8},{11,9},{8,1... | collective-permute-start | bytes 1179656 | tf_op jit(solution)/shard_map/ppermute | solution.py:302
  14.9 0.0 copy-done
  14.9 0.0 copy-done.1
  14.9 0.0 copy-done.2
  14.9 2.5 %shard_map.76.after.near_out.refs_2_ = bf16[96,2048]{1,0:T(8,128)(2,1)S(1)} custom-call(bf16[128,2048]{1,0:T(8,128)(2,1)S(1)} %collective-permute-done.3.rows.after, bf16[384,128]{1,0:T(8,128)(2,1)S(1)} %get-tuple-element.18.place, f32[1,2048]{1,0:T(1,128)S(1)} %get-tuple-element.19.gain, bf16[2048,1024]{1,0:T(8,128)(2,1)S(1)} %bitcast.11, ...), custom_call_target="tpu_custom_call" | custom-call | flops 1207959552 | tf_op jit(solution)/shard_map/pallas_call | solution.py:70
  17.4 1.2 %collective-permute-done.rows = bf16[128,2048]{1,0:T(8,128)(2,1)S(1)} collective-permute-done((bf16[128,2048]{1,0:T(8,128)(2,1)}, bf16[128,2048]{1,0:T(8,128)(2,1)S(1)}, u32[]{:S(2)}, u32[]{:S(2)}) %collective-permute-start) | collective-permute-done | bytes 524320 | tf_op jit(solution)/shard_map/ppermute | solution.py:302
  18.6 0.3 shard_map.77.after
  18.9 1.6 %collective-permute-start.4 = (bf16[96,2048]{1,0:T(8,128)(2,1)S(1)}, bf16[96,2048]{1,0:T(8,128)(2,1)S(1)}, u32[]{:S(2)}, u32[]{:S(2)}) collective-permute-start(bf16[96,2048]{1,0:T(8,128)(2,1)S(1)} %shard_map.77.after), channel_id=1, source_target_pairs={{2,0},{3,1},{0,2},{1,3},{5,4},{4,5},{7,6},{6,7},{10,8},{11,9},{8,1... | collective-permute-start | bytes 1179656 | tf_op jit(solution)/shard_map/ppermute | solution.py:302
  20.5 0.2 collective-permute-done.5.rows
  20.7 2.3 %shard_map.78 = (bf16[96,1280]{1,0:T(8,128)(2,1)S(1)}, bf16[96,768]{1,0:T(8,128)(2,1)S(1)}) custom-call(bf16[96,2048]{1,0:T(8,128)(2,1)S(1)} %collective-permute-done.5.rows, f32[1,2048]{1,0:T(1,128)S(1)} %get-tuple-element.19.gain, bf16[2048,1024]{1,0:T(8,128)(2,1)S(1)} %bitcast.12, bf16[2048,1024]{1,0:T(8,128)(2,1)S(1)} %bitcast.16, ...), custom_call_target="tpu_custom_call" | custom-call | flops 1207959552 | tf_op jit(solution)/shard_map/pallas_call | solution.py:70
  23.0 2.1 %collective-permute-start.7 = (bf16[96,1280]{1,0:T(8,128)(2,1)S(1)}, bf16[96,1280]{1,0:T(8,128)(2,1)S(1)}, u32[]{:S(2)}, u32[]{:S(2)}) collective-permute-start(bf16[96,1280]{1,0:T(8,128)(2,1)S(1)} %get-tuple-element.20.after), channel_id=1, source_target_pairs={{2,0},{3,1},{0,2},{1,3},{5,4},{4,5},{7,6},{6,7},{10,8},{11,9},{8,1... | collective-permute-start | bytes 737288 | tf_op jit(solution)/shard_map/ppermute | solution.py:302
  25.0 1.4 %collective-permute-start.6 = (bf16[96,768]{1,0:T(8,128)(2,1)S(1)}, bf16[96,768]{1,0:T(8,128)(2,1)S(1)}, u32[]{:S(2)}, u32[]{:S(2)}) collective-permute-start(bf16[96,768]{1,0:T(8,128)(2,1)S(1)} %get-tuple-element.22), channel_id=1, source_target_pairs={{1,0},{0,1},{3,2},{2,3},{5,4},{4,5},{7,6},{6,7},{9,8},{8,9},{11,10... | collective-permute-start | bytes 442376 | tf_op jit(solution)/shard_map/ppermute | solution.py:302
  26.5 0.3 collective-permute-done.4.rows
  26.7 2.3 %shard_map.79 = (bf16[96,1280]{1,0:T(8,128)(2,1)S(1)}, bf16[96,768]{1,0:T(8,128)(2,1)S(1)}, bf16[96,768]{1,0:T(8,128)(2,1)S(1)}) custom-call(bf16[96,2048]{1,0:T(8,128)(2,1)S(1)} %collective-permute-done.4.rows, f32[1,2048]{1,0:T(1,128)S(1)} %get-tuple-element.19.gain, bf16[2048,1024]{1,0:T(8,128)(2,1)S(1)} %bitcast.13, bf16[2048,1024]{1,0:T(8,128)(2,1)S(1)} %bitcast.17, ...), custom_call_target="tpu_custom_call" | custom-call | flops 1207959552 | tf_op jit(solution)/shard_map/pallas_call | solution.py:70
  29.1 1.6 %collective-permute-start.8 = (bf16[96,1280]{1,0:T(8,128)(2,1)S(1)}, bf16[96,1280]{1,0:T(8,128)(2,1)S(1)}, u32[]{:S(2)}, u32[]{:S(2)}) collective-permute-start(bf16[96,1280]{1,0:T(8,128)(2,1)S(1)} %get-tuple-element.23), channel_id=1, source_target_pairs={{2,0},{3,1},{0,2},{1,3},{5,4},{4,5},{7,6},{6,7},{10,8},{11,9},{8,1... | collective-permute-start | bytes 737288 | tf_op jit(solution)/shard_map/ppermute | solution.py:302
  30.6 0.6 %collective-permute-start.9 = (bf16[96,768]{1,0:T(8,128)(2,1)S(1)}, bf16[96,768]{1,0:T(8,128)(2,1)S(1)}, u32[]{:S(2)}, u32[]{:S(2)}) collective-permute-start(bf16[96,768]{1,0:T(8,128)(2,1)S(1)} %get-tuple-element.24), channel_id=1, source_target_pairs={{1,0},{0,1},{3,2},{2,3},{5,4},{4,5},{7,6},{6,7},{9,8},{8,9},{11,10... | collective-permute-start | bytes 442376 | tf_op jit(solution)/shard_map/ppermute | solution.py:302
  31.2 0.0 collective-permute-done.7.refs_3_
  31.2 0.3 shard_map.80.refs_4_
  31.5 1.5 %collective-permute-start.10 = (bf16[128,1280]{1,0:T(8,128)(2,1)S(1)}, bf16[128,1280]{1,0:T(8,128)(2,1)S(1)}, u32[]{:S(2)}, u32[]{:S(2)}) collective-permute-start(bf16[128,1280]{1,0:T(8,128)(2,1)S(1)} %shard_map.80.refs_4_), channel_id=1, source_target_pairs={{1,0},{0,1},{3,2},{2,3},{6,4},{7,5},{4,6},{5,7},{9,8},{8,9},{11,10... | collective-permute-start | bytes 983048 | tf_op jit(solution)/shard_map/ppermute | solution.py:302
  33.0 0.0 collective-permute-done.6.refs_3_
  33.0 0.3 shard_map.81.after
  33.3 0.6 %collective-permute-start.11 = (bf16[128,768]{1,0:T(8,128)(2,1)S(1)}, bf16[128,768]{1,0:T(8,128)(2,1)S(1)}, u32[]{:S(2)}, u32[]{:S(2)}) collective-permute-start(bf16[128,768]{1,0:T(8,128)(2,1)S(1)} %shard_map.81.after), channel_id=1, source_target_pairs={{2,0},{3,1},{0,2},{1,3},{6,4},{7,5},{4,6},{5,7},{10,8},{11,9},{8,1... | collective-permute-start | bytes 589832 | tf_op jit(solution)/shard_map/ppermute | solution.py:302
  33.9 2.5 %shard_map.82.here = bf16[96,2048]{1,0:T(8,128)(2,1)S(1)} custom-call(bf16[128,2048]{1,0:T(8,128)(2,1)S(1)} %collective-permute-done.rows, bf16[384,128]{1,0:T(8,128)(2,1)S(1)} %get-tuple-element.18.place, f32[1,2048]{1,0:T(1,128)S(1)} %get-tuple-element.19.gain, bf16[2048,1024]{1,0:T(8,128)(2,1)S(1)} %bitcast.14, bf16[2048,1024]{1,0:T(8,128)(2,1)S(1)} %bitcast.18, ...), custom_call_target="tpu_custom_call" | custom-call | flops 1207959552 | tf_op jit(solution)/shard_map/pallas_call | solution.py:70
  36.4 1.6 %collective-permute-done.8.left = bf16[96,1280]{1,0:T(8,128)(2,1)S(1)} collective-permute-done((bf16[96,1280]{1,0:T(8,128)(2,1)S(1)}, bf16[96,1280]{1,0:T(8,128)(2,1)S(1)}, u32[]{:S(2)}, u32[]{:S(2)}) %collective-permute-start.8) | collective-permute-done | bytes 245792 | tf_op jit(solution)/shard_map/ppermute | solution.py:302
  38.0 0.4 shard_map.83.base
  38.4 0.0 collective-permute-done.9.slots_right
  38.4 2.2 %collective-permute-done.11.right = bf16[128,768]{1,0:T(8,128)(2,1)S(1)} collective-permute-done((bf16[128,768]{1,0:T(8,128)(2,1)S(1)}, bf16[128,768]{1,0:T(8,128)(2,1)S(1)}, u32[]{:S(2)}, u32[]{:S(2)}) %collective-permute-start.11) | collective-permute-done | bytes 196640 | tf_op jit(solution)/shard_map/ppermute | solution.py:302
  40.6 0.0 collective-permute-done.10.left
  40.6 0.9 %shard_map.84 = bf16[128,2048]{1,0:T(8,128)(2,1)} custom-call(f32[128,2048]{1,0:T(8,128)S(1)} %shard_map.83.base, bf16[896,96]{1,0:T(8,128)(2,1)S(1)} %get-tuple-element.16.refs_0_.place_t, f32[128,8]{1,0:T(8,128)S(1)} %get-tuple-element.17.refs_1_.weight_t, bf16[96,768]{1,0:T(8,128)(2,1)S(1)} %collective-permute-done.9.slots_right, ...), custom_call_target="tpu_custom_call" | custom-call | tf_op jit(solution)/shard_map/pallas_call | solution.py:284
Async XLA Ops:
  0.0 12.6 %collective-permute-start.3 = (bf16[128,2048]{1,0:T(8,128)(2,1)}, bf16[128,2048]{1,0:T(8,128)(2,1)S(1)}, u32[]{:S(2)}, u32[]{:S(2)}) collective-permute-start(bf16[128,2048]{1,0:T(8,128)(2,1)} %bitcast.23), channel_id=1, source_target_pairs={{29,0},{28,1},{31,2},{30,3},{2,4},{3,5},{0,6},{1,7},{5,8},{4,9},{7... | collective-permute-start | bytes 1572872 | tf_op jit(solution)/shard_map/ppermute | solution.py:302
  2.4 16.2 %collective-permute-start = (bf16[128,2048]{1,0:T(8,128)(2,1)}, bf16[128,2048]{1,0:T(8,128)(2,1)S(1)}, u32[]{:S(2)}, u32[]{:S(2)}) collective-permute-start(bf16[128,2048]{1,0:T(8,128)(2,1)} %bitcast.24), channel_id=1, source_target_pairs={{28,0},{29,1},{30,2},{31,3},{0,4},{1,5},{2,6},{3,7},{4,8},{5,9},{6... | collective-permute-start | bytes 1572872 | tf_op jit(solution)/shard_map/ppermute | solution.py:302
  4.1 10.8 %copy-start = (bf16[1,2048,1024]{2,1,0:T(8,128)(2,1)S(1)}, bf16[1,2048,1024]{2,1,0:T(8,128)(2,1)}, u32[]{:S(2)}) copy-start(bf16[1,2048,1024]{2,1,0:T(8,128)(2,1)} %param.11) | copy-start | bytes 12582916
  4.1 10.8 %copy-start.1 = (bf16[1,2048,1024]{2,1,0:T(8,128)(2,1)S(1)}, bf16[1,2048,1024]{2,1,0:T(8,128)(2,1)}, u32[]{:S(2)}) copy-start(bf16[1,2048,1024]{2,1,0:T(8,128)(2,1)} %param.12) | copy-start | bytes 12582916
  4.1 10.8 %copy-start.2 = (bf16[1,1024,2048]{2,1,0:T(8,128)(2,1)S(1)}, bf16[1,1024,2048]{2,1,0:T(8,128)(2,1)}, u32[]{:S(2)}) copy-start(bf16[1,1024,2048]{2,1,0:T(8,128)(2,1)} %param.13) | copy-start | bytes 12582916
  5.0 5.4 %collective-permute-start.2 = (f32[8,128]{1,0:T(8,128)S(1)}, f32[8,128]{1,0:T(8,128)S(1)}, u32[]{:S(2)}, u32[]{:S(2)}) collective-permute-start(f32[8,128]{1,0:T(8,128)S(1)} %get-tuple-element.15.own), channel_id=1, source_target_pairs={{2,0},{3,1},{0,2},{1,3},{5,4},{4,5},{7,6},{6,7},{10,8},{11,9},{8,1... | collective-permute-start | bytes 12296 | tf_op jit(solution)/shard_map/ppermute | solution.py:302
  6.6 3.9 %collective-permute-start.1 = (f32[8,128]{1,0:T(8,128)S(1)}, f32[8,128]{1,0:T(8,128)S(1)}, u32[]{:S(2)}, u32[]{:S(2)}) collective-permute-start(f32[8,128]{1,0:T(8,128)S(1)} %get-tuple-element.15.own), channel_id=1, source_target_pairs={{1,0},{0,1},{3,2},{2,3},{6,4},{7,5},{4,6},{5,7},{9,8},{8,9},{11,10... | collective-permute-start | bytes 12296 | tf_op jit(solution)/shard_map/ppermute | solution.py:302
  12.8 7.8 %collective-permute-start.5 = (bf16[96,2048]{1,0:T(8,128)(2,1)S(1)}, bf16[96,2048]{1,0:T(8,128)(2,1)S(1)}, u32[]{:S(2)}, u32[]{:S(2)}) collective-permute-start(bf16[96,2048]{1,0:T(8,128)(2,1)S(1)} %shard_map.75.after), channel_id=1, source_target_pairs={{2,0},{3,1},{0,2},{1,3},{5,4},{4,5},{7,6},{6,7},{10,8},{11,9},{8,1... | collective-permute-start | bytes 1179656 | tf_op jit(solution)/shard_map/ppermute | solution.py:302
  18.9 7.8 %collective-permute-start.4 = (bf16[96,2048]{1,0:T(8,128)(2,1)S(1)}, bf16[96,2048]{1,0:T(8,128)(2,1)S(1)}, u32[]{:S(2)}, u32[]{:S(2)}) collective-permute-start(bf16[96,2048]{1,0:T(8,128)(2,1)S(1)} %shard_map.77.after), channel_id=1, source_target_pairs={{2,0},{3,1},{0,2},{1,3},{5,4},{4,5},{7,6},{6,7},{10,8},{11,9},{8,1... | collective-permute-start | bytes 1179656 | tf_op jit(solution)/shard_map/ppermute | solution.py:302
  23.0 8.2 %collective-permute-start.7 = (bf16[96,1280]{1,0:T(8,128)(2,1)S(1)}, bf16[96,1280]{1,0:T(8,128)(2,1)S(1)}, u32[]{:S(2)}, u32[]{:S(2)}) collective-permute-start(bf16[96,1280]{1,0:T(8,128)(2,1)S(1)} %get-tuple-element.20.after), channel_id=1, source_target_pairs={{2,0},{3,1},{0,2},{1,3},{5,4},{4,5},{7,6},{6,7},{10,8},{11,9},{8,1... | collective-permute-start | bytes 737288 | tf_op jit(solution)/shard_map/ppermute | solution.py:302
  25.0 8.0 %collective-permute-start.6 = (bf16[96,768]{1,0:T(8,128)(2,1)S(1)}, bf16[96,768]{1,0:T(8,128)(2,1)S(1)}, u32[]{:S(2)}, u32[]{:S(2)}) collective-permute-start(bf16[96,768]{1,0:T(8,128)(2,1)S(1)} %get-tuple-element.22), channel_id=1, source_target_pairs={{1,0},{0,1},{3,2},{2,3},{5,4},{4,5},{7,6},{6,7},{9,8},{8,9},{11,10... | collective-permute-start | bytes 442376 | tf_op jit(solution)/shard_map/ppermute | solution.py:302
  29.1 9.0 %collective-permute-start.8 = (bf16[96,1280]{1,0:T(8,128)(2,1)S(1)}, bf16[96,1280]{1,0:T(8,128)(2,1)S(1)}, u32[]{:S(2)}, u32[]{:S(2)}) collective-permute-start(bf16[96,1280]{1,0:T(8,128)(2,1)S(1)} %get-tuple-element.23), channel_id=1, source_target_pairs={{2,0},{3,1},{0,2},{1,3},{5,4},{4,5},{7,6},{6,7},{10,8},{11,9},{8,1... | collective-permute-start | bytes 737288 | tf_op jit(solution)/shard_map/ppermute | solution.py:302
  30.6 7.8 %collective-permute-start.9 = (bf16[96,768]{1,0:T(8,128)(2,1)S(1)}, bf16[96,768]{1,0:T(8,128)(2,1)S(1)}, u32[]{:S(2)}, u32[]{:S(2)}) collective-permute-start(bf16[96,768]{1,0:T(8,128)(2,1)S(1)} %get-tuple-element.24), channel_id=1, source_target_pairs={{1,0},{0,1},{3,2},{2,3},{5,4},{4,5},{7,6},{6,7},{9,8},{8,9},{11,10... | collective-permute-start | bytes 442376 | tf_op jit(solution)/shard_map/ppermute | solution.py:302
  31.5 9.1 %collective-permute-start.10 = (bf16[128,1280]{1,0:T(8,128)(2,1)S(1)}, bf16[128,1280]{1,0:T(8,128)(2,1)S(1)}, u32[]{:S(2)}, u32[]{:S(2)}) collective-permute-start(bf16[128,1280]{1,0:T(8,128)(2,1)S(1)} %shard_map.80.refs_4_), channel_id=1, source_target_pairs={{1,0},{0,1},{3,2},{2,3},{6,4},{7,5},{4,6},{5,7},{9,8},{8,9},{11,10... | collective-permute-start | bytes 983048 | tf_op jit(solution)/shard_map/ppermute | solution.py:302
  33.3 7.3 %collective-permute-start.11 = (bf16[128,768]{1,0:T(8,128)(2,1)S(1)}, bf16[128,768]{1,0:T(8,128)(2,1)S(1)}, u32[]{:S(2)}, u32[]{:S(2)}) collective-permute-start(bf16[128,768]{1,0:T(8,128)(2,1)S(1)} %shard_map.81.after), channel_id=1, source_target_pairs={{2,0},{3,1},{0,2},{1,3},{6,4},{7,5},{4,6},{5,7},{10,8},{11,9},{8,1... | collective-permute-start | bytes 589832 | tf_op jit(solution)/shard_map/ppermute | solution.py:302

commit v5 on v4

--- a/solution.py
+++ b/solution.py
@@ -257,39 +257,63 @@
     return call(based_body, [like(rows.shape, jnp.float32)], (rows, place_t, weight_t, here, left), flops=LONG)[0]
 
 
-def last_body(base, place_t, weight_t, slots_right, left, right, out, here, done):
-    half, size = left.shape[1], weight_t.shape[0]
+def written(value, here, out, first, done, n):
+    width = value.shape[1]
+    here[:, first : first + width] = value.astype(out.dtype)
+    copy = pltpu.make_async_copy(here.at[:, pl.ds(first, width)], out.at[:, pl.ds(first, width)], done.at[n])
+    copy.start()
+    return copy
+
+
+def first_body(base, place_t, weight_t, slots_right, left, out, rest, here, done):
+    cut, size = left.shape[1], weight_t.shape[0]
+    copies = []
+    for n, at in enumerate(range(0, cut, STRIP)):
+        strip = slice(at, at + STRIP)
+        copies.append(written(base[:, strip] + left[:, strip].astype(jnp.float32), here, out, at, done, n))
     hit = place_t[BACK_RIGHT * size : (BACK_RIGHT + 1) * size, :]
     weight = weight_t[:, BACK_RIGHT : BACK_RIGHT + 1]
-    copies = []
-    for n, at in enumerate(range(0, out.shape[1], WIDE)):
-        for begin in range(at, at + WIDE, STRIP):
-            first = begin if begin < half else begin - half
-            strip, within = slice(begin, begin + STRIP), slice(first, first + STRIP)
-            total = base[:, strip] + (left if begin < half else right)[:, within].astype(jnp.float32)
-            if begin >= half:
-                total += weight * jnp.dot(hit, slots_right[:, within], preferred_element_type=jnp.float32)
-            here[:, strip] = total.astype(out.dtype)
-        copies.append(pltpu.make_async_copy(here.at[:, pl.ds(at, WIDE)], out.at[:, pl.ds(at, WIDE)], done.at[n]))
-        copies[-1].start()
+    for at in range(0, rest.shape[1], STRIP):
+        strip = slice(at, at + STRIP)
+        rows = jnp.dot(hit, slots_right[:, strip], preferred_element_type=jnp.float32)
+        rest[:, strip] = base[:, cut + at : cut + at + STRIP] + weight * rows
     for copy in copies:
         copy.wait()
 
 
-WIDE = 256
+def rest_body(_, rest, right, out, here, done):
+    cut = out.shape[1] - rest.shape[1]
+    copies = []
+    for n, at in enumerate(range(0, rest.shape[1], STRIP)):
+        strip = slice(at, at + STRIP)
+        copies.append(written(rest[:, strip] + right[:, strip].astype(jnp.float32), here, out, cut + at, done, n))
+    for copy in copies:
+        copy.wait()
 
 
 def last(base, place_t, weight_t, slots_right, left, right, dtype):
     out = like(base.shape, dtype)
-    return pl.pallas_call(
-        last_body,
-        out_shape=out,
-        in_specs=[spec()] * 6,
-        out_specs=spec(pltpu.HBM),
-        scratch_shapes=[VMEM(out.shape, dtype), pltpu.SemaphoreType.DMA((base.shape[1] // WIDE,))],
+    rest = like(right.shape, jnp.float32)
+    common = dict(
+        scratch_shapes=[VMEM(out.shape, dtype), pltpu.SemaphoreType.DMA((base.shape[1] // STRIP,))],
         compiler_params=pltpu.CompilerParams(vmem_limit_bytes=8 << 20),
         cost_estimate=pl.CostEstimate(flops=0, bytes_accessed=0, transcendentals=0),
-    )(base, place_t, weight_t, slots_right, left, right)
+    )
+    result, rest = pl.pallas_call(
+        first_body,
+        out_shape=[out, rest],
+        in_specs=[spec()] * 5,
+        out_specs=[spec(pltpu.HBM), spec()],
+        **common,
+    )(base, place_t, weight_t, slots_right, left)
+    return pl.pallas_call(
+        rest_body,
+        out_shape=out,
+        in_specs=[spec(pltpu.HBM)] + [spec()] * 2,
+        out_specs=spec(pltpu.HBM),
+        input_output_aliases={0: 0},
+        **common,
+    )(result, rest, right)
 
 
 def moved(value, back, flip):

time: 41.7 us -> 41.5 us (level)
  waiting for transfers between devices: 10.3 us -> 9.41 us
  Pallas kernels: 13.5 us -> 14.3 us
    ppermute x12, waiting for transfers between devices: 10.3 us -> 9.41 us  [moved(): return lax.ppermute(value, ('section', 'expert'), pairs)]
    pallas_call x1 -> x2, Pallas kernels: 0.93 us -> 1.69 us  [the longest x1 0.93 us: last(): pl.pallas_call(first_body, out_shape=[out, rest], in_specs=[spec()] * 5,...]
  transfers between devices with their start and end apart: 12 -> 12, of which waited for: 8 -> 9; matrix products, arithmetic and copies ran while one was open for 0% -> 0% of each run, Pallas kernels for 30% -> 33%
where the time goes in v5:
time: 41.5 us; the launch traced here: 41.4 us
  starting transfers between devices  17.6 us (42%)
  Pallas kernels  14.3 us (34%)
  waiting for transfers between devices  9.41 us (23%)
    ppermute x12, starting transfers between devices, moved(): return lax.ppermute(value, ('section', 'expert'), pairs)  17.6 us
    pallas_call x10, Pallas kernels, call(): pl.pallas_call(body, out_shape=outs, in_specs=[spec()] * len(ins), out_sp...  11.7 us
    ppermute x12, waiting for transfers between devices, moved(): return lax.ppermute(value, ('section', 'expert'), pairs)  9.41 us
    pallas_call x1, Pallas kernels, last(): pl.pallas_call(first_body, out_shape=[out, rest], in_specs=[spec()] * 5,...  0.93 us
    pallas_call x1, Pallas kernels, tabled(): pl.pallas_call(table_body, out_shape=[like((8, ids.shape[1]), jnp.float32...  0.91 us
  transfers between devices with their start and end apart: 12, of which 9 were waited for; matrix products, arithmetic and copies ran while one was open for 0% of the time, Pallas kernels for 33%

profile of v5, /device:TPU:0, one launch (start us, length us, event | category | flops | bytes accessed | tf_op | source)
XLA Modules:
  0.0 41.4 jit_solution(11102176146594474401)
XLA Ops:
  0.0 2.4 %collective-permute-start.3 = (bf16[128,2048]{1,0:T(8,128)(2,1)}, bf16[128,2048]{1,0:T(8,128)(2,1)S(1)}, u32[]{:S(2)}, u32[]{:S(2)}) collective-permute-start(bf16[128,2048]{1,0:T(8,128)(2,1)} %bitcast.23), channel_id=1, source_target_pairs={{29,0},{28,1},{31,2},{30,3},{2,4},{3,5},{0,6},{1,7},{5,8},{4,9},{7... | collective-permute-start | bytes 1572872 | tf_op jit(solution)/shard_map/ppermute | solution.py:326
  2.4 1.7 %collective-permute-start = (bf16[128,2048]{1,0:T(8,128)(2,1)}, bf16[128,2048]{1,0:T(8,128)(2,1)S(1)}, u32[]{:S(2)}, u32[]{:S(2)}) collective-permute-start(bf16[128,2048]{1,0:T(8,128)(2,1)} %bitcast.24), channel_id=1, source_target_pairs={{28,0},{29,1},{30,2},{31,3},{0,4},{1,5},{2,6},{3,7},{4,8},{5,9},{6... | collective-permute-start | bytes 1572872 | tf_op jit(solution)/shard_map/ppermute | solution.py:326
  4.1 0.0 copy-start
  4.1 0.0 copy-start.1
  4.1 0.0 copy-start.2
  4.1 0.9 %shard_map.73 = (f32[8,128]{1,0:T(8,128)S(1)}, f32[1,2048]{1,0:T(1,128)S(1)}) custom-call(s32[2,128]{1,0:T(2,128)} %bitcast.25, f32[2,128]{1,0:T(2,128)} %bitcast.26, f32[1,2048]{1,0:T(1,128)} %gain.1), custom_call_target="tpu_custom_call" | custom-call | flops 20000000000 | tf_op jit(solution)/shard_map/pallas_call | solution.py:109
  5.0 1.6 %collective-permute-start.2 = (f32[8,128]{1,0:T(8,128)S(1)}, f32[8,128]{1,0:T(8,128)S(1)}, u32[]{:S(2)}, u32[]{:S(2)}) collective-permute-start(f32[8,128]{1,0:T(8,128)S(1)} %get-tuple-element.17.own), channel_id=1, source_target_pairs={{2,0},{3,1},{0,2},{1,3},{5,4},{4,5},{7,6},{6,7},{10,8},{11,9},{8,1... | collective-permute-start | bytes 12296 | tf_op jit(solution)/shard_map/ppermute | solution.py:326
  6.6 0.5 %collective-permute-start.1 = (f32[8,128]{1,0:T(8,128)S(1)}, f32[8,128]{1,0:T(8,128)S(1)}, u32[]{:S(2)}, u32[]{:S(2)}) collective-permute-start(f32[8,128]{1,0:T(8,128)S(1)} %get-tuple-element.17.own), channel_id=1, source_target_pairs={{1,0},{0,1},{3,2},{2,3},{6,4},{7,5},{4,6},{5,7},{9,8},{8,9},{11,10... | collective-permute-start | bytes 12296 | tf_op jit(solution)/shard_map/ppermute | solution.py:326
  7.1 3.3 %collective-permute-done.2.beside = f32[8,128]{1,0:T(8,128)S(1)} collective-permute-done((f32[8,128]{1,0:T(8,128)S(1)}, f32[8,128]{1,0:T(8,128)S(1)}, u32[]{:S(2)}, u32[]{:S(2)}) %collective-permute-start.2) | collective-permute-done | bytes 4128 | tf_op jit(solution)/shard_map/ppermute | solution.py:326
  10.4 0.1 collective-permute-done.1.near
  10.5 0.6 %shard_map.74 = (bf16[384,128]{1,0:T(8,128)(2,1)S(1)}, bf16[896,96]{1,0:T(8,128)(2,1)S(1)}, f32[128,8]{1,0:T(8,128)S(1)}) custom-call(f32[8,128]{1,0:T(8,128)S(1)} %get-tuple-element.17.own, f32[8,128]{1,0:T(8,128)S(1)} %collective-permute-done.1.near, f32[8,128]{1,0:T(8,128)S(1)} %collective-permute-done.2.beside), custom_call_target="tpu_custom_call" | custom-call | tf_op jit(solution)/shard_map/pallas_call | solution.py:70
  11.1 1.4 %collective-permute-done.3.rows.after = bf16[128,2048]{1,0:T(8,128)(2,1)S(1)} collective-permute-done((bf16[128,2048]{1,0:T(8,128)(2,1)}, bf16[128,2048]{1,0:T(8,128)(2,1)S(1)}, u32[]{:S(2)}, u32[]{:S(2)}) %collective-permute-start.3) | collective-permute-done | bytes 524320 | tf_op jit(solution)/shard_map/ppermute | solution.py:326
  12.6 0.3 shard_map.75.after
  12.8 2.1 %collective-permute-start.5 = (bf16[96,2048]{1,0:T(8,128)(2,1)S(1)}, bf16[96,2048]{1,0:T(8,128)(2,1)S(1)}, u32[]{:S(2)}, u32[]{:S(2)}) collective-permute-start(bf16[96,2048]{1,0:T(8,128)(2,1)S(1)} %shard_map.75.after), channel_id=1, source_target_pairs={{2,0},{3,1},{0,2},{1,3},{5,4},{4,5},{7,6},{6,7},{10,8},{11,9},{8,1... | collective-permute-start | bytes 1179656 | tf_op jit(solution)/shard_map/ppermute | solution.py:326
  14.9 0.0 copy-done
  14.9 0.0 copy-done.1
  14.9 0.0 copy-done.2
  14.9 2.5 %shard_map.76.after.near_out.refs_2_ = bf16[96,2048]{1,0:T(8,128)(2,1)S(1)} custom-call(bf16[128,2048]{1,0:T(8,128)(2,1)S(1)} %collective-permute-done.3.rows.after, bf16[384,128]{1,0:T(8,128)(2,1)S(1)} %get-tuple-element.20.place, f32[1,2048]{1,0:T(1,128)S(1)} %get-tuple-element.21.gain, bf16[2048,1024]{1,0:T(8,128)(2,1)S(1)} %bitcast.11, ...), custom_call_target="tpu_custom_call" | custom-call | flops 1207959552 | tf_op jit(solution)/shard_map/pallas_call | solution.py:70
  17.4 1.2 %collective-permute-done.rows = bf16[128,2048]{1,0:T(8,128)(2,1)S(1)} collective-permute-done((bf16[128,2048]{1,0:T(8,128)(2,1)}, bf16[128,2048]{1,0:T(8,128)(2,1)S(1)}, u32[]{:S(2)}, u32[]{:S(2)}) %collective-permute-start) | collective-permute-done | bytes 524320 | tf_op jit(solution)/shard_map/ppermute | solution.py:326
  18.6 0.3 shard_map.77.after
  18.9 1.6 %collective-permute-start.4 = (bf16[96,2048]{1,0:T(8,128)(2,1)S(1)}, bf16[96,2048]{1,0:T(8,128)(2,1)S(1)}, u32[]{:S(2)}, u32[]{:S(2)}) collective-permute-start(bf16[96,2048]{1,0:T(8,128)(2,1)S(1)} %shard_map.77.after), channel_id=1, source_target_pairs={{2,0},{3,1},{0,2},{1,3},{5,4},{4,5},{7,6},{6,7},{10,8},{11,9},{8,1... | collective-permute-start | bytes 1179656 | tf_op jit(solution)/shard_map/ppermute | solution.py:326
  20.5 0.2 collective-permute-done.5.rows
  20.7 2.3 %shard_map.78 = (bf16[96,1280]{1,0:T(8,128)(2,1)S(1)}, bf16[96,768]{1,0:T(8,128)(2,1)S(1)}) custom-call(bf16[96,2048]{1,0:T(8,128)(2,1)S(1)} %collective-permute-done.5.rows, f32[1,2048]{1,0:T(1,128)S(1)} %get-tuple-element.21.gain, bf16[2048,1024]{1,0:T(8,128)(2,1)S(1)} %bitcast.12, bf16[2048,1024]{1,0:T(8,128)(2,1)S(1)} %bitcast.16, ...), custom_call_target="tpu_custom_call" | custom-call | flops 1207959552 | tf_op jit(solution)/shard_map/pallas_call | solution.py:70
  23.0 2.1 %collective-permute-start.7 = (bf16[96,1280]{1,0:T(8,128)(2,1)S(1)}, bf16[96,1280]{1,0:T(8,128)(2,1)S(1)}, u32[]{:S(2)}, u32[]{:S(2)}) collective-permute-start(bf16[96,1280]{1,0:T(8,128)(2,1)S(1)} %get-tuple-element.22.after), channel_id=1, source_target_pairs={{2,0},{3,1},{0,2},{1,3},{5,4},{4,5},{7,6},{6,7},{10,8},{11,9},{8,1... | collective-permute-start | bytes 737288 | tf_op jit(solution)/shard_map/ppermute | solution.py:326
  25.0 1.4 %collective-permute-start.6 = (bf16[96,768]{1,0:T(8,128)(2,1)S(1)}, bf16[96,768]{1,0:T(8,128)(2,1)S(1)}, u32[]{:S(2)}, u32[]{:S(2)}) collective-permute-start(bf16[96,768]{1,0:T(8,128)(2,1)S(1)} %get-tuple-element.24), channel_id=1, source_target_pairs={{1,0},{0,1},{3,2},{2,3},{5,4},{4,5},{7,6},{6,7},{9,8},{8,9},{11,10... | collective-permute-start | bytes 442376 | tf_op jit(solution)/shard_map/ppermute | solution.py:326
  26.5 0.3 collective-permute-done.4.rows
  26.7 2.3 %shard_map.79 = (bf16[96,1280]{1,0:T(8,128)(2,1)S(1)}, bf16[96,768]{1,0:T(8,128)(2,1)S(1)}, bf16[96,768]{1,0:T(8,128)(2,1)S(1)}) custom-call(bf16[96,2048]{1,0:T(8,128)(2,1)S(1)} %collective-permute-done.4.rows, f32[1,2048]{1,0:T(1,128)S(1)} %get-tuple-element.21.gain, bf16[2048,1024]{1,0:T(8,128)(2,1)S(1)} %bitcast.13, bf16[2048,1024]{1,0:T(8,128)(2,1)S(1)} %bitcast.17, ...), custom_call_target="tpu_custom_call" | custom-call | flops 1207959552 | tf_op jit(solution)/shard_map/pallas_call | solution.py:70
  29.1 1.6 %collective-permute-start.8 = (bf16[96,1280]{1,0:T(8,128)(2,1)S(1)}, bf16[96,1280]{1,0:T(8,128)(2,1)S(1)}, u32[]{:S(2)}, u32[]{:S(2)}) collective-permute-start(bf16[96,1280]{1,0:T(8,128)(2,1)S(1)} %get-tuple-element.25), channel_id=1, source_target_pairs={{2,0},{3,1},{0,2},{1,3},{5,4},{4,5},{7,6},{6,7},{10,8},{11,9},{8,1... | collective-permute-start | bytes 737288 | tf_op jit(solution)/shard_map/ppermute | solution.py:326
  30.6 0.6 %collective-permute-start.9 = (bf16[96,768]{1,0:T(8,128)(2,1)S(1)}, bf16[96,768]{1,0:T(8,128)(2,1)S(1)}, u32[]{:S(2)}, u32[]{:S(2)}) collective-permute-start(bf16[96,768]{1,0:T(8,128)(2,1)S(1)} %get-tuple-element.26), channel_id=1, source_target_pairs={{1,0},{0,1},{3,2},{2,3},{5,4},{4,5},{7,6},{6,7},{9,8},{8,9},{11,10... | collective-permute-start | bytes 442376 | tf_op jit(solution)/shard_map/ppermute | solution.py:326
  31.2 0.0 collective-permute-done.7.refs_3_
  31.2 0.3 shard_map.80.refs_4_
  31.5 1.5 %collective-permute-start.10 = (bf16[128,1280]{1,0:T(8,128)(2,1)S(1)}, bf16[128,1280]{1,0:T(8,128)(2,1)S(1)}, u32[]{:S(2)}, u32[]{:S(2)}) collective-permute-start(bf16[128,1280]{1,0:T(8,128)(2,1)S(1)} %shard_map.80.refs_4_), channel_id=1, source_target_pairs={{1,0},{0,1},{3,2},{2,3},{6,4},{7,5},{4,6},{5,7},{9,8},{8,9},{11,10... | collective-permute-start | bytes 983048 | tf_op jit(solution)/shard_map/ppermute | solution.py:326
  33.0 0.0 collective-permute-done.6.refs_3_
  33.0 0.3 shard_map.81.after
  33.3 0.6 %collective-permute-start.11 = (bf16[128,768]{1,0:T(8,128)(2,1)S(1)}, bf16[128,768]{1,0:T(8,128)(2,1)S(1)}, u32[]{:S(2)}, u32[]{:S(2)}) collective-permute-start(bf16[128,768]{1,0:T(8,128)(2,1)S(1)} %shard_map.81.after), channel_id=1, source_target_pairs={{2,0},{3,1},{0,2},{1,3},{6,4},{7,5},{4,6},{5,7},{10,8},{11,9},{8,1... | collective-permute-start | bytes 589832 | tf_op jit(solution)/shard_map/ppermute | solution.py:326
  33.9 2.5 %shard_map.82.here = bf16[96,2048]{1,0:T(8,128)(2,1)S(1)} custom-call(bf16[128,2048]{1,0:T(8,128)(2,1)S(1)} %collective-permute-done.rows, bf16[384,128]{1,0:T(8,128)(2,1)S(1)} %get-tuple-element.20.place, f32[1,2048]{1,0:T(1,128)S(1)} %get-tuple-element.21.gain, bf16[2048,1024]{1,0:T(8,128)(2,1)S(1)} %bitcast.14, bf16[2048,1024]{1,0:T(8,128)(2,1)S(1)} %bitcast.18, ...), custom_call_target="tpu_custom_call" | custom-call | flops 1207959552 | tf_op jit(solution)/shard_map/pallas_call | solution.py:70
  36.4 1.6 %collective-permute-done.8.left = bf16[96,1280]{1,0:T(8,128)(2,1)S(1)} collective-permute-done((bf16[96,1280]{1,0:T(8,128)(2,1)S(1)}, bf16[96,1280]{1,0:T(8,128)(2,1)S(1)}, u32[]{:S(2)}, u32[]{:S(2)}) %collective-permute-start.8) | collective-permute-done | bytes 245792 | tf_op jit(solution)/shard_map/ppermute | solution.py:326
  38.0 0.4 shard_map.83.base
  38.4 0.0 collective-permute-done.9.slots_right
  38.4 0.9 %collective-permute-done.10.left = bf16[128,1280]{1,0:T(8,128)(2,1)S(1)} collective-permute-done((bf16[128,1280]{1,0:T(8,128)(2,1)S(1)}, bf16[128,1280]{1,0:T(8,128)(2,1)S(1)}, u32[]{:S(2)}, u32[]{:S(2)}) %collective-permute-start.10) | collective-permute-done | bytes 327712 | tf_op jit(solution)/shard_map/ppermute | solution.py:326
  39.3 0.9 %shard_map.84 = (bf16[128,2048]{1,0:T(8,128)(2,1)}, f32[128,768]{1,0:T(8,128)S(1)}) custom-call(f32[128,2048]{1,0:T(8,128)S(1)} %shard_map.83.base, bf16[896,96]{1,0:T(8,128)(2,1)S(1)} %get-tuple-element.18.refs_0_.place_t, f32[128,8]{1,0:T(8,128)S(1)} %get-tuple-element.19.refs_1_.weight_t, bf16[96,768]{1,0:T(8,128)(2,1)S(1)} %collective-permute-done.9.slots_right, ...), custom_call_target="tpu_custom_call" | custom-call | tf_op jit(solution)/shard_map/pallas_call | solution.py:302
  40.2 0.4 collective-permute-done.11.right
  40.6 0.8 %shard_map.85 = bf16[128,2048]{1,0:T(8,128)(2,1)} custom-call(bf16[128,2048]{1,0:T(8,128)(2,1)} %get-tuple-element.27._, f32[128,768]{1,0:T(8,128)S(1)} %get-tuple-element.28.rest, bf16[128,768]{1,0:T(8,128)(2,1)S(1)} %collective-permute-done.11.right), custom_call_target="tpu_custom_call", output_to_operand_aliasing={{}: (0, {})} | custom-call | tf_op jit(solution)/shard_map/pallas_call | solution.py:309
Async XLA Ops:
  0.0 12.6 %collective-permute-start.3 = (bf16[128,2048]{1,0:T(8,128)(2,1)}, bf16[128,2048]{1,0:T(8,128)(2,1)S(1)}, u32[]{:S(2)}, u32[]{:S(2)}) collective-permute-start(bf16[128,2048]{1,0:T(8,128)(2,1)} %bitcast.23), channel_id=1, source_target_pairs={{29,0},{28,1},{31,2},{30,3},{2,4},{3,5},{0,6},{1,7},{5,8},{4,9},{7... | collective-permute-start | bytes 1572872 | tf_op jit(solution)/shard_map/ppermute | solution.py:326
  2.4 16.2 %collective-permute-start = (bf16[128,2048]{1,0:T(8,128)(2,1)}, bf16[128,2048]{1,0:T(8,128)(2,1)S(1)}, u32[]{:S(2)}, u32[]{:S(2)}) collective-permute-start(bf16[128,2048]{1,0:T(8,128)(2,1)} %bitcast.24), channel_id=1, source_target_pairs={{28,0},{29,1},{30,2},{31,3},{0,4},{1,5},{2,6},{3,7},{4,8},{5,9},{6... | collective-permute-start | bytes 1572872 | tf_op jit(solution)/shard_map/ppermute | solution.py:326
  4.1 10.8 %copy-start = (bf16[1,2048,1024]{2,1,0:T(8,128)(2,1)S(1)}, bf16[1,2048,1024]{2,1,0:T(8,128)(2,1)}, u32[]{:S(2)}) copy-start(bf16[1,2048,1024]{2,1,0:T(8,128)(2,1)} %param.11) | copy-start | bytes 12582916
  4.1 10.8 %copy-start.1 = (bf16[1,2048,1024]{2,1,0:T(8,128)(2,1)S(1)}, bf16[1,2048,1024]{2,1,0:T(8,128)(2,1)}, u32[]{:S(2)}) copy-start(bf16[1,2048,1024]{2,1,0:T(8,128)(2,1)} %param.12) | copy-start | bytes 12582916
  4.1 10.8 %copy-start.2 = (bf16[1,1024,2048]{2,1,0:T(8,128)(2,1)S(1)}, bf16[1,1024,2048]{2,1,0:T(8,128)(2,1)}, u32[]{:S(2)}) copy-start(bf16[1,1024,2048]{2,1,0:T(8,128)(2,1)} %param.13) | copy-start | bytes 12582916
  5.0 5.4 %collective-permute-start.2 = (f32[8,128]{1,0:T(8,128)S(1)}, f32[8,128]{1,0:T(8,128)S(1)}, u32[]{:S(2)}, u32[]{:S(2)}) collective-permute-start(f32[8,128]{1,0:T(8,128)S(1)} %get-tuple-element.17.own), channel_id=1, source_target_pairs={{2,0},{3,1},{0,2},{1,3},{5,4},{4,5},{7,6},{6,7},{10,8},{11,9},{8,1... | collective-permute-start | bytes 12296 | tf_op jit(solution)/shard_map/ppermute | solution.py:326
  6.6 3.9 %collective-permute-start.1 = (f32[8,128]{1,0:T(8,128)S(1)}, f32[8,128]{1,0:T(8,128)S(1)}, u32[]{:S(2)}, u32[]{:S(2)}) collective-permute-start(f32[8,128]{1,0:T(8,128)S(1)} %get-tuple-element.17.own), channel_id=1, source_target_pairs={{1,0},{0,1},{3,2},{2,3},{6,4},{7,5},{4,6},{5,7},{9,8},{8,9},{11,10... | collective-permute-start | bytes 12296 | tf_op jit(solution)/shard_map/ppermute | solution.py:326
  12.8 7.8 %collective-permute-start.5 = (bf16[96,2048]{1,0:T(8,128)(2,1)S(1)}, bf16[96,2048]{1,0:T(8,128)(2,1)S(1)}, u32[]{:S(2)}, u32[]{:S(2)}) collective-permute-start(bf16[96,2048]{1,0:T(8,128)(2,1)S(1)} %shard_map.75.after), channel_id=1, source_target_pairs={{2,0},{3,1},{0,2},{1,3},{5,4},{4,5},{7,6},{6,7},{10,8},{11,9},{8,1... | collective-permute-start | bytes 1179656 | tf_op jit(solution)/shard_map/ppermute | solution.py:326
  18.9 7.8 %collective-permute-start.4 = (bf16[96,2048]{1,0:T(8,128)(2,1)S(1)}, bf16[96,2048]{1,0:T(8,128)(2,1)S(1)}, u32[]{:S(2)}, u32[]{:S(2)}) collective-permute-start(bf16[96,2048]{1,0:T(8,128)(2,1)S(1)} %shard_map.77.after), channel_id=1, source_target_pairs={{2,0},{3,1},{0,2},{1,3},{5,4},{4,5},{7,6},{6,7},{10,8},{11,9},{8,1... | collective-permute-start | bytes 1179656 | tf_op jit(solution)/shard_map/ppermute | solution.py:326
  23.0 8.2 %collective-permute-start.7 = (bf16[96,1280]{1,0:T(8,128)(2,1)S(1)}, bf16[96,1280]{1,0:T(8,128)(2,1)S(1)}, u32[]{:S(2)}, u32[]{:S(2)}) collective-permute-start(bf16[96,1280]{1,0:T(8,128)(2,1)S(1)} %get-tuple-element.22.after), channel_id=1, source_target_pairs={{2,0},{3,1},{0,2},{1,3},{5,4},{4,5},{7,6},{6,7},{10,8},{11,9},{8,1... | collective-permute-start | bytes 737288 | tf_op jit(solution)/shard_map/ppermute | solution.py:326
  25.0 8.0 %collective-permute-start.6 = (bf16[96,768]{1,0:T(8,128)(2,1)S(1)}, bf16[96,768]{1,0:T(8,128)(2,1)S(1)}, u32[]{:S(2)}, u32[]{:S(2)}) collective-permute-start(bf16[96,768]{1,0:T(8,128)(2,1)S(1)} %get-tuple-element.24), channel_id=1, source_target_pairs={{1,0},{0,1},{3,2},{2,3},{5,4},{4,5},{7,6},{6,7},{9,8},{8,9},{11,10... | collective-permute-start | bytes 442376 | tf_op jit(solution)/shard_map/ppermute | solution.py:326
  29.1 9.0 %collective-permute-start.8 = (bf16[96,1280]{1,0:T(8,128)(2,1)S(1)}, bf16[96,1280]{1,0:T(8,128)(2,1)S(1)}, u32[]{:S(2)}, u32[]{:S(2)}) collective-permute-start(bf16[96,1280]{1,0:T(8,128)(2,1)S(1)} %get-tuple-element.25), channel_id=1, source_target_pairs={{2,0},{3,1},{0,2},{1,3},{5,4},{4,5},{7,6},{6,7},{10,8},{11,9},{8,1... | collective-permute-start | bytes 737288 | tf_op jit(solution)/shard_map/ppermute | solution.py:326
  30.6 7.8 %collective-permute-start.9 = (bf16[96,768]{1,0:T(8,128)(2,1)S(1)}, bf16[96,768]{1,0:T(8,128)(2,1)S(1)}, u32[]{:S(2)}, u32[]{:S(2)}) collective-permute-start(bf16[96,768]{1,0:T(8,128)(2,1)S(1)} %get-tuple-element.26), channel_id=1, source_target_pairs={{1,0},{0,1},{3,2},{2,3},{5,4},{4,5},{7,6},{6,7},{9,8},{8,9},{11,10... | collective-permute-start | bytes 442376 | tf_op jit(solution)/shard_map/ppermute | solution.py:326
  31.5 7.8 %collective-permute-start.10 = (bf16[128,1280]{1,0:T(8,128)(2,1)S(1)}, bf16[128,1280]{1,0:T(8,128)(2,1)S(1)}, u32[]{:S(2)}, u32[]{:S(2)}) collective-permute-start(bf16[128,1280]{1,0:T(8,128)(2,1)S(1)} %shard_map.80.refs_4_), channel_id=1, source_target_pairs={{1,0},{0,1},{3,2},{2,3},{6,4},{7,5},{4,6},{5,7},{9,8},{8,9},{11,10... | collective-permute-start | bytes 983048 | tf_op jit(solution)/shard_map/ppermute | solution.py:326
  33.3 7.3 %collective-permute-start.11 = (bf16[128,768]{1,0:T(8,128)(2,1)S(1)}, bf16[128,768]{1,0:T(8,128)(2,1)S(1)}, u32[]{:S(2)}, u32[]{:S(2)}) collective-permute-start(bf16[128,768]{1,0:T(8,128)(2,1)S(1)} %shard_map.81.after), channel_id=1, source_target_pairs={{2,0},{3,1},{0,2},{1,3},{6,4},{7,5},{4,6},{5,7},{10,8},{11,9},{8,1... | collective-permute-start | bytes 589832 | tf_op jit(solution)/shard_map/ppermute | solution.py:326

commit v6 on v5

--- a/solution.py
+++ b/solution.py
@@ -220,24 +220,33 @@
 STRIP = 256
 
 
-def spread_body(which, count, first, *refs):
-    bases, (place_t, weight_t, *parts), out = refs[:count], refs[count:-2], refs[-1]
+def spread_body(which, first, carried, place_t, weight_t, *refs):
+    parts, (out, *copies) = refs[:2], refs[2 + carried + 1 :]
     size, width = weight_t.shape[0], out.shape[1]
     for at in range(0, width, STRIP):
-        strip = slice(at, at + STRIP)
-        terms = [base[:, strip].astype(jnp.float32) for base in bases]
+        terms = []
         for k, part in zip(which, parts):
             hit = place_t[k * size : (k + 1) * size, :]
             begin = at if part.shape[1] == width else first + at
             rows = jnp.dot(hit, part[:, begin : begin + STRIP], preferred_element_type=jnp.float32)
             terms.append(weight_t[:, k : k + 1] * rows)
-        out[:, strip] = sum(terms[1:], terms[0]).astype(out.dtype)
-
-
-def spread(which, bases, place_t, weight_t, parts, dtype, after, columns, flops=0):
-    outs = [like((weight_t.shape[0], columns.stop - columns.start), dtype)]
-    body = functools.partial(spread_body, which, len(bases), columns.start)
-    return call(body, outs, (*bases, place_t, weight_t, *parts, after), flops=flops)[0]
+        out[:, at : at + STRIP] = (terms[0] + terms[1]).astype(out.dtype)
+    for value, copy in zip(refs[2 : 2 + carried], copies):
+        copy[...] = value[...]
+
+
+def spread(which, place_t, weight_t, parts, columns, after, carried=()):
+    outs = [like((weight_t.shape[0], columns.stop - columns.start))] + [like(v.shape) for v in carried]
+    body = functools.partial(spread_body, which, columns.start, len(carried))
+    return call(body, outs, (place_t, weight_t, *parts, *carried, after))
+
+
+def again_body(value, after, out):
+    out[...] = value[...]
+
+
+def again(value, after):
+    return call(again_body, [like(value.shape)], (value, after))[0]
 
 
 def based_body(rows, place_t, weight_t, here, left, out):
@@ -265,28 +274,27 @@
     return copy
 
 
-def first_body(base, place_t, weight_t, slots_right, left, out, rest, here, done):
-    cut, size = left.shape[1], weight_t.shape[0]
+def first_body(base, left, out, rest, here, done):
+    cut = left.shape[1]
     copies = []
     for n, at in enumerate(range(0, cut, STRIP)):
         strip = slice(at, at + STRIP)
         copies.append(written(base[:, strip] + left[:, strip].astype(jnp.float32), here, out, at, done, n))
+    rest[...] = base[:, cut:]
+    for copy in copies:
+        copy.wait()
+
+
+def rest_body(_, rest, place_t, weight_t, slots_right, right, out, here, done):
+    cut, size = out.shape[1] - rest.shape[1], weight_t.shape[0]
     hit = place_t[BACK_RIGHT * size : (BACK_RIGHT + 1) * size, :]
     weight = weight_t[:, BACK_RIGHT : BACK_RIGHT + 1]
-    for at in range(0, rest.shape[1], STRIP):
-        strip = slice(at, at + STRIP)
-        rows = jnp.dot(hit, slots_right[:, strip], preferred_element_type=jnp.float32)
-        rest[:, strip] = base[:, cut + at : cut + at + STRIP] + weight * rows
-    for copy in copies:
-        copy.wait()
-
-
-def rest_body(_, rest, right, out, here, done):
-    cut = out.shape[1] - rest.shape[1]
     copies = []
     for n, at in enumerate(range(0, rest.shape[1], STRIP)):
         strip = slice(at, at + STRIP)
-        copies.append(written(rest[:, strip] + right[:, strip].astype(jnp.float32), here, out, cut + at, done, n))
+        rows = jnp.dot(hit, slots_right[:, strip], preferred_element_type=jnp.float32)
+        total = rest[:, strip] + weight * rows + right[:, strip].astype(jnp.float32)
+        copies.append(written(total, here, out, cut + at, done, n))
     for copy in copies:
         copy.wait()
 
@@ -302,18 +310,18 @@
     result, rest = pl.pallas_call(
         first_body,
         out_shape=[out, rest],
-        in_specs=[spec()] * 5,
+        in_specs=[spec()] * 2,
         out_specs=[spec(pltpu.HBM), spec()],
         **common,
-    )(base, place_t, weight_t, slots_right, left)
+    )(base, left)
     return pl.pallas_call(
         rest_body,
         out_shape=out,
-        in_specs=[spec(pltpu.HBM)] + [spec()] * 2,
+        in_specs=[spec(pltpu.HBM)] + [spec()] * 5,
         out_specs=spec(pltpu.HBM),
         input_output_aliases={0: 0},
         **common,
-    )(result, rest, right)
+    )(result, rest, place_t, weight_t, slots_right, right)
 
 
 def moved(value, back, flip):
@@ -358,9 +366,11 @@
     on_right = moved(far_right, 0, lambda s: side_flip(s) if s % 2 else near_flip(s))
     left_slots, right_slots, keep = sided(side_rows, gain, weights, near_out, far_left, cut)
     left_slots = moved(left_slots, 0, side_flip)
+    sums = functools.partial(spread, place_t=place_t, weight_t=weight_t)
+    (left,) = sums((LEFT_HERE, LEFT_ON), parts=(near_out, on_left), columns=slice(0, cut), after=keep)
+    (right,) = sums((RIGHT_HERE, RIGHT_ON), parts=(keep, on_right), columns=slice(cut, width), after=left)
+    right_slots = again(right_slots, right)
     right_slots = moved(right_slots, 0, lambda s: side_flip(s) if s % 2 else near_flip(s))
-    left = spread((LEFT_HERE, LEFT_ON), (), place_t, weight_t, (near_out, on_left), jnp.bfloat16, keep, slice(0, cut))
-    right = spread((RIGHT_HERE, RIGHT_ON), (), place_t, weight_t, (keep, on_right), jnp.bfloat16, left, slice(cut, width))
     from_left = moved(left, 0, near_flip)
     from_right = moved(right, 0, lambda s: near_flip(s) if s % 2 else side_flip(s))
     here = tokens(OWN_HERE, rows, place, gain, weights, right)

time: 41.5 us -> 40.8 us (0.983)
  waiting for transfers between devices: 9.41 us -> 7.88 us
  starting transfers between devices: 17.6 us -> 18.3 us
    ppermute x12, waiting for transfers between devices: 9.41 us -> 7.88 us  [moved(): return lax.ppermute(value, ('section', 'expert'), pairs)]
    ppermute x12, starting transfers between devices: 17.6 us -> 18.3 us  [moved(): return lax.ppermute(value, ('section', 'expert'), pairs)]
    pallas_call x10 -> x11, Pallas kernels: 11.7 us -> 11.7 us  [call(): pl.pallas_call(body, out_shape=outs, in_specs=[spec()] * len(ins), out_sp...]
  transfers between devices with their start and end apart: 12 -> 12, of which waited for: 9 -> 10; matrix products, arithmetic and copies ran while one was open for 0% -> 0% of each run, Pallas kernels for 33% -> 33%
where the time goes in v6:
time: 40.8 us; the launch traced here: 40.7 us
  starting transfers between devices  18.3 us (45%)
  Pallas kernels  14.3 us (35%)
  waiting for transfers between devices  7.88 us (19%)
    ppermute x12, starting transfers between devices, moved(): return lax.ppermute(value, ('section', 'expert'), pairs)  18.3 us
    pallas_call x11, Pallas kernels, call(): pl.pallas_call(body, out_shape=outs, in_specs=[spec()] * len(ins), out_sp...  11.7 us
    ppermute x12, waiting for transfers between devices, moved(): return lax.ppermute(value, ('section', 'expert'), pairs)  7.88 us
    pallas_call x1, Pallas kernels, last(): pl.pallas_call(rest_body, out_shape=out, in_specs=[spec(pltpu.HBM)] + [sp...  0.92 us
    pallas_call x1, Pallas kernels, tabled(): pl.pallas_call(table_body, out_shape=[like((8, ids.shape[1]), jnp.float32...  0.91 us
  transfers between devices with their start and end apart: 12, of which 10 were waited for; matrix products, arithmetic and copies ran while one was open for 0% of the time, Pallas kernels for 33%

profile of v6, /device:TPU:0, one launch (start us, length us, event | category | flops | bytes accessed | tf_op | source)
XLA Modules:
  0.0 40.7 jit_solution(13903221994353265843)
XLA Ops:
  0.0 2.4 %collective-permute-start.3 = (bf16[128,2048]{1,0:T(8,128)(2,1)}, bf16[128,2048]{1,0:T(8,128)(2,1)S(1)}, u32[]{:S(2)}, u32[]{:S(2)}) collective-permute-start(bf16[128,2048]{1,0:T(8,128)(2,1)} %bitcast.23), channel_id=1, source_target_pairs={{29,0},{28,1},{31,2},{30,3},{2,4},{3,5},{0,6},{1,7},{5,8},{4,9},{7... | collective-permute-start | bytes 1572872 | tf_op jit(solution)/shard_map/ppermute | solution.py:334
  2.4 1.7 %collective-permute-start = (bf16[128,2048]{1,0:T(8,128)(2,1)}, bf16[128,2048]{1,0:T(8,128)(2,1)S(1)}, u32[]{:S(2)}, u32[]{:S(2)}) collective-permute-start(bf16[128,2048]{1,0:T(8,128)(2,1)} %bitcast.24), channel_id=1, source_target_pairs={{28,0},{29,1},{30,2},{31,3},{0,4},{1,5},{2,6},{3,7},{4,8},{5,9},{6... | collective-permute-start | bytes 1572872 | tf_op jit(solution)/shard_map/ppermute | solution.py:334
  4.1 0.0 copy-start
  4.1 0.0 copy-start.1
  4.1 0.0 copy-start.2
  4.1 0.9 %shard_map.73 = (f32[8,128]{1,0:T(8,128)S(1)}, f32[1,2048]{1,0:T(1,128)S(1)}) custom-call(s32[2,128]{1,0:T(2,128)} %bitcast.25, f32[2,128]{1,0:T(2,128)} %bitcast.26, f32[1,2048]{1,0:T(1,128)} %gain.1), custom_call_target="tpu_custom_call" | custom-call | flops 20000000000 | tf_op jit(solution)/shard_map/pallas_call | solution.py:109
  5.0 1.6 %collective-permute-start.2 = (f32[8,128]{1,0:T(8,128)S(1)}, f32[8,128]{1,0:T(8,128)S(1)}, u32[]{:S(2)}, u32[]{:S(2)}) collective-permute-start(f32[8,128]{1,0:T(8,128)S(1)} %get-tuple-element.17.own), channel_id=1, source_target_pairs={{2,0},{3,1},{0,2},{1,3},{5,4},{4,5},{7,6},{6,7},{10,8},{11,9},{8,1... | collective-permute-start | bytes 12296 | tf_op jit(solution)/shard_map/ppermute | solution.py:334
  6.6 0.5 %collective-permute-start.1 = (f32[8,128]{1,0:T(8,128)S(1)}, f32[8,128]{1,0:T(8,128)S(1)}, u32[]{:S(2)}, u32[]{:S(2)}) collective-permute-start(f32[8,128]{1,0:T(8,128)S(1)} %get-tuple-element.17.own), channel_id=1, source_target_pairs={{1,0},{0,1},{3,2},{2,3},{6,4},{7,5},{4,6},{5,7},{9,8},{8,9},{11,10... | collective-permute-start | bytes 12296 | tf_op jit(solution)/shard_map/ppermute | solution.py:334
  7.1 3.3 %collective-permute-done.2.beside = f32[8,128]{1,0:T(8,128)S(1)} collective-permute-done((f32[8,128]{1,0:T(8,128)S(1)}, f32[8,128]{1,0:T(8,128)S(1)}, u32[]{:S(2)}, u32[]{:S(2)}) %collective-permute-start.2) | collective-permute-done | bytes 4128 | tf_op jit(solution)/shard_map/ppermute | solution.py:334
  10.4 0.1 collective-permute-done.1.near
  10.5 0.6 %shard_map.74 = (bf16[384,128]{1,0:T(8,128)(2,1)S(1)}, bf16[896,96]{1,0:T(8,128)(2,1)S(1)}, f32[128,8]{1,0:T(8,128)S(1)}) custom-call(f32[8,128]{1,0:T(8,128)S(1)} %get-tuple-element.17.own, f32[8,128]{1,0:T(8,128)S(1)} %collective-permute-done.1.near, f32[8,128]{1,0:T(8,128)S(1)} %collective-permute-done.2.beside), custom_call_target="tpu_custom_call" | custom-call | tf_op jit(solution)/shard_map/pallas_call | solution.py:70
  11.1 1.4 %collective-permute-done.3.rows.after = bf16[128,2048]{1,0:T(8,128)(2,1)S(1)} collective-permute-done((bf16[128,2048]{1,0:T(8,128)(2,1)}, bf16[128,2048]{1,0:T(8,128)(2,1)S(1)}, u32[]{:S(2)}, u32[]{:S(2)}) %collective-permute-start.3) | collective-permute-done | bytes 524320 | tf_op jit(solution)/shard_map/ppermute | solution.py:334
  12.6 0.3 shard_map.75.after
  12.8 2.1 %collective-permute-start.5 = (bf16[96,2048]{1,0:T(8,128)(2,1)S(1)}, bf16[96,2048]{1,0:T(8,128)(2,1)S(1)}, u32[]{:S(2)}, u32[]{:S(2)}) collective-permute-start(bf16[96,2048]{1,0:T(8,128)(2,1)S(1)} %shard_map.75.after), channel_id=1, source_target_pairs={{2,0},{3,1},{0,2},{1,3},{5,4},{4,5},{7,6},{6,7},{10,8},{11,9},{8,1... | collective-permute-start | bytes 1179656 | tf_op jit(solution)/shard_map/ppermute | solution.py:334
  14.9 0.0 copy-done
  14.9 0.0 copy-done.1
  14.9 0.0 copy-done.2
  14.9 2.5 %shard_map.76.after.near_out.refs_0_ = bf16[96,2048]{1,0:T(8,128)(2,1)S(1)} custom-call(bf16[128,2048]{1,0:T(8,128)(2,1)S(1)} %collective-permute-done.3.rows.after, bf16[384,128]{1,0:T(8,128)(2,1)S(1)} %get-tuple-element.20.place, f32[1,2048]{1,0:T(1,128)S(1)} %get-tuple-element.21.gain, bf16[2048,1024]{1,0:T(8,128)(2,1)S(1)} %bitcast.11, ...), custom_call_target="tpu_custom_call" | custom-call | flops 1207959552 | tf_op jit(solution)/shard_map/pallas_call | solution.py:70
  17.4 1.2 %collective-permute-done.rows = bf16[128,2048]{1,0:T(8,128)(2,1)S(1)} collective-permute-done((bf16[128,2048]{1,0:T(8,128)(2,1)}, bf16[128,2048]{1,0:T(8,128)(2,1)S(1)}, u32[]{:S(2)}, u32[]{:S(2)}) %collective-permute-start) | collective-permute-done | bytes 524320 | tf_op jit(solution)/shard_map/ppermute | solution.py:334
  18.6 0.3 shard_map.77.after
  18.9 1.6 %collective-permute-start.4 = (bf16[96,2048]{1,0:T(8,128)(2,1)S(1)}, bf16[96,2048]{1,0:T(8,128)(2,1)S(1)}, u32[]{:S(2)}, u32[]{:S(2)}) collective-permute-start(bf16[96,2048]{1,0:T(8,128)(2,1)S(1)} %shard_map.77.after), channel_id=1, source_target_pairs={{2,0},{3,1},{0,2},{1,3},{5,4},{4,5},{7,6},{6,7},{10,8},{11,9},{8,1... | collective-permute-start | bytes 1179656 | tf_op jit(solution)/shard_map/ppermute | solution.py:334
  20.5 0.2 collective-permute-done.5.rows
  20.7 2.3 %shard_map.78 = (bf16[96,1280]{1,0:T(8,128)(2,1)S(1)}, bf16[96,768]{1,0:T(8,128)(2,1)S(1)}) custom-call(bf16[96,2048]{1,0:T(8,128)(2,1)S(1)} %collective-permute-done.5.rows, f32[1,2048]{1,0:T(1,128)S(1)} %get-tuple-element.21.gain, bf16[2048,1024]{1,0:T(8,128)(2,1)S(1)} %bitcast.12, bf16[2048,1024]{1,0:T(8,128)(2,1)S(1)} %bitcast.16, ...), custom_call_target="tpu_custom_call" | custom-call | flops 1207959552 | tf_op jit(solution)/shard_map/pallas_call | solution.py:70
  23.0 2.1 %collective-permute-start.7 = (bf16[96,1280]{1,0:T(8,128)(2,1)S(1)}, bf16[96,1280]{1,0:T(8,128)(2,1)S(1)}, u32[]{:S(2)}, u32[]{:S(2)}) collective-permute-start(bf16[96,1280]{1,0:T(8,128)(2,1)S(1)} %get-tuple-element.22.after), channel_id=1, source_target_pairs={{2,0},{3,1},{0,2},{1,3},{5,4},{4,5},{7,6},{6,7},{10,8},{11,9},{8,1... | collective-permute-start | bytes 737288 | tf_op jit(solution)/shard_map/ppermute | solution.py:334
  25.0 1.4 %collective-permute-start.6 = (bf16[96,768]{1,0:T(8,128)(2,1)S(1)}, bf16[96,768]{1,0:T(8,128)(2,1)S(1)}, u32[]{:S(2)}, u32[]{:S(2)}) collective-permute-start(bf16[96,768]{1,0:T(8,128)(2,1)S(1)} %get-tuple-element.24), channel_id=1, source_target_pairs={{1,0},{0,1},{3,2},{2,3},{5,4},{4,5},{7,6},{6,7},{9,8},{8,9},{11,10... | collective-permute-start | bytes 442376 | tf_op jit(solution)/shard_map/ppermute | solution.py:334
  26.5 0.2 collective-permute-done.4.rows
  26.7 2.3 %shard_map.79 = (bf16[96,1280]{1,0:T(8,128)(2,1)S(1)}, bf16[96,768]{1,0:T(8,128)(2,1)S(1)}, bf16[96,768]{1,0:T(8,128)(2,1)S(1)}) custom-call(bf16[96,2048]{1,0:T(8,128)(2,1)S(1)} %collective-permute-done.4.rows, f32[1,2048]{1,0:T(1,128)S(1)} %get-tuple-element.21.gain, bf16[2048,1024]{1,0:T(8,128)(2,1)S(1)} %bitcast.13, bf16[2048,1024]{1,0:T(8,128)(2,1)S(1)} %bitcast.17, ...), custom_call_target="tpu_custom_call" | custom-call | flops 1207959552 | tf_op jit(solution)/shard_map/pallas_call | solution.py:70
  29.0 1.6 %collective-permute-start.8 = (bf16[96,1280]{1,0:T(8,128)(2,1)S(1)}, bf16[96,1280]{1,0:T(8,128)(2,1)S(1)}, u32[]{:S(2)}, u32[]{:S(2)}) collective-permute-start(bf16[96,1280]{1,0:T(8,128)(2,1)S(1)} %get-tuple-element.25), channel_id=1, source_target_pairs={{2,0},{3,1},{0,2},{1,3},{5,4},{4,5},{7,6},{6,7},{10,8},{11,9},{8,1... | collective-permute-start | bytes 737288 | tf_op jit(solution)/shard_map/ppermute | solution.py:334
  30.6 0.0 collective-permute-done.7.refs_1_
  30.6 0.3 shard_map.80.refs_2_
  30.9 1.3 %collective-permute-start.9 = (bf16[128,1280]{1,0:T(8,128)(2,1)S(1)}, bf16[128,1280]{1,0:T(8,128)(2,1)S(1)}, u32[]{:S(2)}, u32[]{:S(2)}) collective-permute-start(bf16[128,1280]{1,0:T(8,128)(2,1)S(1)} %shard_map.80.refs_2_), channel_id=1, source_target_pairs={{1,0},{0,1},{3,2},{2,3},{6,4},{7,5},{4,6},{5,7},{9,8},{8,9},{11,10... | collective-permute-start | bytes 983048 | tf_op jit(solution)/shard_map/ppermute | solution.py:334
  32.2 0.0 collective-permute-done.6.refs_1_
  32.2 0.3 shard_map.81.after
  32.5 1.5 %collective-permute-start.11 = (bf16[128,768]{1,0:T(8,128)(2,1)S(1)}, bf16[128,768]{1,0:T(8,128)(2,1)S(1)}, u32[]{:S(2)}, u32[]{:S(2)}) collective-permute-start(bf16[128,768]{1,0:T(8,128)(2,1)S(1)} %shard_map.81.after), channel_id=1, source_target_pairs={{2,0},{3,1},{0,2},{1,3},{6,4},{7,5},{4,6},{5,7},{10,8},{11,9},{8,1... | collective-permute-start | bytes 589832 | tf_op jit(solution)/shard_map/ppermute | solution.py:334
  34.0 0.7 %collective-permute-start.10 = (bf16[96,768]{1,0:T(8,128)(2,1)S(1)}, bf16[96,768]{1,0:T(8,128)(2,1)S(1)}, u32[]{:S(2)}, u32[]{:S(2)}) collective-permute-start(bf16[96,768]{1,0:T(8,128)(2,1)S(1)} %shard_map.85), channel_id=1, source_target_pairs={{1,0},{0,1},{3,2},{2,3},{5,4},{4,5},{7,6},{6,7},{9,8},{8,9},{11,10... | collective-permute-start | bytes 442376 | tf_op jit(solution)/shard_map/ppermute | solution.py:334
  34.7 2.5 %shard_map.82.here = bf16[96,2048]{1,0:T(8,128)(2,1)S(1)} custom-call(bf16[128,2048]{1,0:T(8,128)(2,1)S(1)} %collective-permute-done.rows, bf16[384,128]{1,0:T(8,128)(2,1)S(1)} %get-tuple-element.20.place, f32[1,2048]{1,0:T(1,128)S(1)} %get-tuple-element.21.gain, bf16[2048,1024]{1,0:T(8,128)(2,1)S(1)} %bitcast.14, bf16[2048,1024]{1,0:T(8,128)(2,1)S(1)} %bitcast.18, ...), custom_call_target="tpu_custom_call" | custom-call | flops 1207959552 | tf_op jit(solution)/shard_map/pallas_call | solution.py:70
  37.2 0.4 %collective-permute-done.8.left = bf16[96,1280]{1,0:T(8,128)(2,1)S(1)} collective-permute-done((bf16[96,1280]{1,0:T(8,128)(2,1)S(1)}, bf16[96,1280]{1,0:T(8,128)(2,1)S(1)}, u32[]{:S(2)}, u32[]{:S(2)}) %collective-permute-start.8) | collective-permute-done | bytes 245792 | tf_op jit(solution)/shard_map/ppermute | solution.py:334
  37.6 0.4 shard_map.83.base
  38.0 0.1 collective-permute-done.9.left
  38.1 0.8 %shard_map.84 = (bf16[128,2048]{1,0:T(8,128)(2,1)}, f32[128,768]{1,0:T(8,128)S(1)}) custom-call(f32[128,2048]{1,0:T(8,128)S(1)} %shard_map.83.base, bf16[128,1280]{1,0:T(8,128)(2,1)S(1)} %collective-permute-done.9.left), custom_call_target="tpu_custom_call" | custom-call | tf_op jit(solution)/shard_map/pallas_call | solution.py:310
  38.9 0.8 %collective-permute-done.10.slots_right = bf16[96,768]{1,0:T(8,128)(2,1)S(1)} collective-permute-done((bf16[96,768]{1,0:T(8,128)(2,1)S(1)}, bf16[96,768]{1,0:T(8,128)(2,1)S(1)}, u32[]{:S(2)}, u32[]{:S(2)}) %collective-permute-start.10) | collective-permute-done | bytes 147488 | tf_op jit(solution)/shard_map/ppermute | solution.py:334
  39.7 0.1 collective-permute-done.11.right
  39.7 0.9 %shard_map.86 = bf16[128,2048]{1,0:T(8,128)(2,1)} custom-call(bf16[128,2048]{1,0:T(8,128)(2,1)} %get-tuple-element.26._, f32[128,768]{1,0:T(8,128)S(1)} %get-tuple-element.27.rest, bf16[896,96]{1,0:T(8,128)(2,1)S(1)} %get-tuple-element.18.place_t, f32[128,8]{1,0:T(8,128)S(1)} %get-tuple-element.19.weight_t, ...), custom_call_target="tpu_custom_call", output_to_operand_aliasing={{}: (0, {})} | custom-call | tf_op jit(solution)/shard_map/pallas_call | solution.py:317
  (1 shorter events, 0.0 us)
Async XLA Ops:
  0.0 12.6 %collective-permute-start.3 = (bf16[128,2048]{1,0:T(8,128)(2,1)}, bf16[128,2048]{1,0:T(8,128)(2,1)S(1)}, u32[]{:S(2)}, u32[]{:S(2)}) collective-permute-start(bf16[128,2048]{1,0:T(8,128)(2,1)} %bitcast.23), channel_id=1, source_target_pairs={{29,0},{28,1},{31,2},{30,3},{2,4},{3,5},{0,6},{1,7},{5,8},{4,9},{7... | collective-permute-start | bytes 1572872 | tf_op jit(solution)/shard_map/ppermute | solution.py:334
  2.4 16.2 %collective-permute-start = (bf16[128,2048]{1,0:T(8,128)(2,1)}, bf16[128,2048]{1,0:T(8,128)(2,1)S(1)}, u32[]{:S(2)}, u32[]{:S(2)}) collective-permute-start(bf16[128,2048]{1,0:T(8,128)(2,1)} %bitcast.24), channel_id=1, source_target_pairs={{28,0},{29,1},{30,2},{31,3},{0,4},{1,5},{2,6},{3,7},{4,8},{5,9},{6... | collective-permute-start | bytes 1572872 | tf_op jit(solution)/shard_map/ppermute | solution.py:334
  4.1 10.8 %copy-start = (bf16[1,2048,1024]{2,1,0:T(8,128)(2,1)S(1)}, bf16[1,2048,1024]{2,1,0:T(8,128)(2,1)}, u32[]{:S(2)}) copy-start(bf16[1,2048,1024]{2,1,0:T(8,128)(2,1)} %param.11) | copy-start | bytes 12582916
  4.1 10.8 %copy-start.1 = (bf16[1,2048,1024]{2,1,0:T(8,128)(2,1)S(1)}, bf16[1,2048,1024]{2,1,0:T(8,128)(2,1)}, u32[]{:S(2)}) copy-start(bf16[1,2048,1024]{2,1,0:T(8,128)(2,1)} %param.12) | copy-start | bytes 12582916
  4.1 10.8 %copy-start.2 = (bf16[1,1024,2048]{2,1,0:T(8,128)(2,1)S(1)}, bf16[1,1024,2048]{2,1,0:T(8,128)(2,1)}, u32[]{:S(2)}) copy-start(bf16[1,1024,2048]{2,1,0:T(8,128)(2,1)} %param.13) | copy-start | bytes 12582916
  5.0 5.4 %collective-permute-start.2 = (f32[8,128]{1,0:T(8,128)S(1)}, f32[8,128]{1,0:T(8,128)S(1)}, u32[]{:S(2)}, u32[]{:S(2)}) collective-permute-start(f32[8,128]{1,0:T(8,128)S(1)} %get-tuple-element.17.own), channel_id=1, source_target_pairs={{2,0},{3,1},{0,2},{1,3},{5,4},{4,5},{7,6},{6,7},{10,8},{11,9},{8,1... | collective-permute-start | bytes 12296 | tf_op jit(solution)/shard_map/ppermute | solution.py:334
  6.6 3.9 %collective-permute-start.1 = (f32[8,128]{1,0:T(8,128)S(1)}, f32[8,128]{1,0:T(8,128)S(1)}, u32[]{:S(2)}, u32[]{:S(2)}) collective-permute-start(f32[8,128]{1,0:T(8,128)S(1)} %get-tuple-element.17.own), channel_id=1, source_target_pairs={{1,0},{0,1},{3,2},{2,3},{6,4},{7,5},{4,6},{5,7},{9,8},{8,9},{11,10... | collective-permute-start | bytes 12296 | tf_op jit(solution)/shard_map/ppermute | solution.py:334
  12.8 7.8 %collective-permute-start.5 = (bf16[96,2048]{1,0:T(8,128)(2,1)S(1)}, bf16[96,2048]{1,0:T(8,128)(2,1)S(1)}, u32[]{:S(2)}, u32[]{:S(2)}) collective-permute-start(bf16[96,2048]{1,0:T(8,128)(2,1)S(1)} %shard_map.75.after), channel_id=1, source_target_pairs={{2,0},{3,1},{0,2},{1,3},{5,4},{4,5},{7,6},{6,7},{10,8},{11,9},{8,1... | collective-permute-start | bytes 1179656 | tf_op jit(solution)/shard_map/ppermute | solution.py:334
  18.9 7.8 %collective-permute-start.4 = (bf16[96,2048]{1,0:T(8,128)(2,1)S(1)}, bf16[96,2048]{1,0:T(8,128)(2,1)S(1)}, u32[]{:S(2)}, u32[]{:S(2)}) collective-permute-start(bf16[96,2048]{1,0:T(8,128)(2,1)S(1)} %shard_map.77.after), channel_id=1, source_target_pairs={{2,0},{3,1},{0,2},{1,3},{5,4},{4,5},{7,6},{6,7},{10,8},{11,9},{8,1... | collective-permute-start | bytes 1179656 | tf_op jit(solution)/shard_map/ppermute | solution.py:334
  23.0 7.6 %collective-permute-start.7 = (bf16[96,1280]{1,0:T(8,128)(2,1)S(1)}, bf16[96,1280]{1,0:T(8,128)(2,1)S(1)}, u32[]{:S(2)}, u32[]{:S(2)}) collective-permute-start(bf16[96,1280]{1,0:T(8,128)(2,1)S(1)} %get-tuple-element.22.after), channel_id=1, source_target_pairs={{2,0},{3,1},{0,2},{1,3},{5,4},{4,5},{7,6},{6,7},{10,8},{11,9},{8,1... | collective-permute-start | bytes 737288 | tf_op jit(solution)/shard_map/ppermute | solution.py:334
  25.0 7.2 %collective-permute-start.6 = (bf16[96,768]{1,0:T(8,128)(2,1)S(1)}, bf16[96,768]{1,0:T(8,128)(2,1)S(1)}, u32[]{:S(2)}, u32[]{:S(2)}) collective-permute-start(bf16[96,768]{1,0:T(8,128)(2,1)S(1)} %get-tuple-element.24), channel_id=1, source_target_pairs={{1,0},{0,1},{3,2},{2,3},{5,4},{4,5},{7,6},{6,7},{9,8},{8,9},{11,10... | collective-permute-start | bytes 442376 | tf_op jit(solution)/shard_map/ppermute | solution.py:334
  29.0 8.6 %collective-permute-start.8 = (bf16[96,1280]{1,0:T(8,128)(2,1)S(1)}, bf16[96,1280]{1,0:T(8,128)(2,1)S(1)}, u32[]{:S(2)}, u32[]{:S(2)}) collective-permute-start(bf16[96,1280]{1,0:T(8,128)(2,1)S(1)} %get-tuple-element.25), channel_id=1, source_target_pairs={{2,0},{3,1},{0,2},{1,3},{5,4},{4,5},{7,6},{6,7},{10,8},{11,9},{8,1... | collective-permute-start | bytes 737288 | tf_op jit(solution)/shard_map/ppermute | solution.py:334
  30.9 7.1 %collective-permute-start.9 = (bf16[128,1280]{1,0:T(8,128)(2,1)S(1)}, bf16[128,1280]{1,0:T(8,128)(2,1)S(1)}, u32[]{:S(2)}, u32[]{:S(2)}) collective-permute-start(bf16[128,1280]{1,0:T(8,128)(2,1)S(1)} %shard_map.80.refs_2_), channel_id=1, source_target_pairs={{1,0},{0,1},{3,2},{2,3},{6,4},{7,5},{4,6},{5,7},{9,8},{8,9},{11,10... | collective-permute-start | bytes 983048 | tf_op jit(solution)/shard_map/ppermute | solution.py:334
  32.5 7.2 %collective-permute-start.11 = (bf16[128,768]{1,0:T(8,128)(2,1)S(1)}, bf16[128,768]{1,0:T(8,128)(2,1)S(1)}, u32[]{:S(2)}, u32[]{:S(2)}) collective-permute-start(bf16[128,768]{1,0:T(8,128)(2,1)S(1)} %shard_map.81.after), channel_id=1, source_target_pairs={{2,0},{3,1},{0,2},{1,3},{6,4},{7,5},{4,6},{5,7},{10,8},{11,9},{8,1... | collective-permute-start | bytes 589832 | tf_op jit(solution)/shard_map/ppermute | solution.py:334
  34.0 5.6 %collective-permute-start.10 = (bf16[96,768]{1,0:T(8,128)(2,1)S(1)}, bf16[96,768]{1,0:T(8,128)(2,1)S(1)}, u32[]{:S(2)}, u32[]{:S(2)}) collective-permute-start(bf16[96,768]{1,0:T(8,128)(2,1)S(1)} %shard_map.85), channel_id=1, source_target_pairs={{1,0},{0,1},{3,2},{2,3},{5,4},{4,5},{7,6},{6,7},{9,8},{8,9},{11,10... | collective-permute-start | bytes 442376 | tf_op jit(solution)/shard_map/ppermute | solution.py:334

commit v7 on v6

--- a/solution.py
+++ b/solution.py
@@ -343,7 +343,7 @@
 
 
 LONG = 20_000_000_000
-CUT = 5
+CUT = 4
 
 
 def local_square(acts, routes, gates, norm_gain, gate_w, up_w, down_w):

time: 40.8 us -> 40.7 us (level)
  starting transfers between devices: 18.3 us -> 17.6 us
  waiting for transfers between devices: 7.88 us -> 8.48 us
    ppermute x12, starting transfers between devices: 18.3 us -> 17.6 us  [moved(): return lax.ppermute(value, ('section', 'expert'), pairs)]
    ppermute x12, waiting for transfers between devices: 7.88 us -> 8.48 us  [moved(): return lax.ppermute(value, ('section', 'expert'), pairs)]
  transfers between devices with their start and end apart: 12 -> 12, of which waited for: 10 -> 8; matrix products, arithmetic and copies ran while one was open for 0% -> 0% of each run, Pallas kernels for 33% -> 33%
where the time goes in v7:
time: 40.7 us; the launch traced here: 40.6 us
  starting transfers between devices  17.6 us (43%)
  Pallas kernels  14.4 us (35%)
  waiting for transfers between devices  8.48 us (21%)
    ppermute x12, starting transfers between devices, moved(): return lax.ppermute(value, ('section', 'expert'), pairs)  17.6 us
    pallas_call x11, Pallas kernels, call(): pl.pallas_call(body, out_shape=outs, in_specs=[spec()] * len(ins), out_sp...  11.7 us
    ppermute x12, waiting for transfers between devices, moved(): return lax.ppermute(value, ('section', 'expert'), pairs)  8.48 us
    pallas_call x1, Pallas kernels, last(): pl.pallas_call(rest_body, out_shape=out, in_specs=[spec(pltpu.HBM)] + [sp...  0.94 us
    pallas_call x1, Pallas kernels, tabled(): pl.pallas_call(table_body, out_shape=[like((8, ids.shape[1]), jnp.float32...  0.91 us
  transfers between devices with their start and end apart: 12, of which 8 were waited for; matrix products, arithmetic and copies ran while one was open for 0% of the time, Pallas kernels for 33%

profile of v7, /device:TPU:0, one launch (start us, length us, event | category | flops | bytes accessed | tf_op | source)
XLA Modules:
  0.0 40.6 jit_solution(11890092350328648694)
XLA Ops:
  0.0 2.4 %collective-permute-start.3 = (bf16[128,2048]{1,0:T(8,128)(2,1)}, bf16[128,2048]{1,0:T(8,128)(2,1)S(1)}, u32[]{:S(2)}, u32[]{:S(2)}) collective-permute-start(bf16[128,2048]{1,0:T(8,128)(2,1)} %bitcast.23), channel_id=1, source_target_pairs={{29,0},{28,1},{31,2},{30,3},{2,4},{3,5},{0,6},{1,7},{5,8},{4,9},{7... | collective-permute-start | bytes 1572872 | tf_op jit(solution)/shard_map/ppermute | solution.py:334
  2.4 1.7 %collective-permute-start = (bf16[128,2048]{1,0:T(8,128)(2,1)}, bf16[128,2048]{1,0:T(8,128)(2,1)S(1)}, u32[]{:S(2)}, u32[]{:S(2)}) collective-permute-start(bf16[128,2048]{1,0:T(8,128)(2,1)} %bitcast.24), channel_id=1, source_target_pairs={{28,0},{29,1},{30,2},{31,3},{0,4},{1,5},{2,6},{3,7},{4,8},{5,9},{6... | collective-permute-start | bytes 1572872 | tf_op jit(solution)/shard_map/ppermute | solution.py:334
  4.1 0.0 copy-start
  4.1 0.0 copy-start.1
  4.1 0.0 copy-start.2
  4.1 0.9 %shard_map.73 = (f32[8,128]{1,0:T(8,128)S(1)}, f32[1,2048]{1,0:T(1,128)S(1)}) custom-call(s32[2,128]{1,0:T(2,128)} %bitcast.25, f32[2,128]{1,0:T(2,128)} %bitcast.26, f32[1,2048]{1,0:T(1,128)} %gain.1), custom_call_target="tpu_custom_call" | custom-call | flops 20000000000 | tf_op jit(solution)/shard_map/pallas_call | solution.py:109
  5.0 1.6 %collective-permute-start.2 = (f32[8,128]{1,0:T(8,128)S(1)}, f32[8,128]{1,0:T(8,128)S(1)}, u32[]{:S(2)}, u32[]{:S(2)}) collective-permute-start(f32[8,128]{1,0:T(8,128)S(1)} %get-tuple-element.17.own), channel_id=1, source_target_pairs={{2,0},{3,1},{0,2},{1,3},{5,4},{4,5},{7,6},{6,7},{10,8},{11,9},{8,1... | collective-permute-start | bytes 12296 | tf_op jit(solution)/shard_map/ppermute | solution.py:334
  6.6 0.5 %collective-permute-start.1 = (f32[8,128]{1,0:T(8,128)S(1)}, f32[8,128]{1,0:T(8,128)S(1)}, u32[]{:S(2)}, u32[]{:S(2)}) collective-permute-start(f32[8,128]{1,0:T(8,128)S(1)} %get-tuple-element.17.own), channel_id=1, source_target_pairs={{1,0},{0,1},{3,2},{2,3},{6,4},{7,5},{4,6},{5,7},{9,8},{8,9},{11,10... | collective-permute-start | bytes 12296 | tf_op jit(solution)/shard_map/ppermute | solution.py:334
  7.1 3.3 %collective-permute-done.2.beside = f32[8,128]{1,0:T(8,128)S(1)} collective-permute-done((f32[8,128]{1,0:T(8,128)S(1)}, f32[8,128]{1,0:T(8,128)S(1)}, u32[]{:S(2)}, u32[]{:S(2)}) %collective-permute-start.2) | collective-permute-done | bytes 4128 | tf_op jit(solution)/shard_map/ppermute | solution.py:334
  10.4 0.1 collective-permute-done.1.near
  10.5 0.6 %shard_map.74 = (bf16[384,128]{1,0:T(8,128)(2,1)S(1)}, bf16[896,96]{1,0:T(8,128)(2,1)S(1)}, f32[128,8]{1,0:T(8,128)S(1)}) custom-call(f32[8,128]{1,0:T(8,128)S(1)} %get-tuple-element.17.own, f32[8,128]{1,0:T(8,128)S(1)} %collective-permute-done.1.near, f32[8,128]{1,0:T(8,128)S(1)} %collective-permute-done.2.beside), custom_call_target="tpu_custom_call" | custom-call | tf_op jit(solution)/shard_map/pallas_call | solution.py:70
  11.1 1.4 %collective-permute-done.3.rows.after = bf16[128,2048]{1,0:T(8,128)(2,1)S(1)} collective-permute-done((bf16[128,2048]{1,0:T(8,128)(2,1)}, bf16[128,2048]{1,0:T(8,128)(2,1)S(1)}, u32[]{:S(2)}, u32[]{:S(2)}) %collective-permute-start.3) | collective-permute-done | bytes 524320 | tf_op jit(solution)/shard_map/ppermute | solution.py:334
  12.6 0.3 shard_map.75.after
  12.8 2.1 %collective-permute-start.5 = (bf16[96,2048]{1,0:T(8,128)(2,1)S(1)}, bf16[96,2048]{1,0:T(8,128)(2,1)S(1)}, u32[]{:S(2)}, u32[]{:S(2)}) collective-permute-start(bf16[96,2048]{1,0:T(8,128)(2,1)S(1)} %shard_map.75.after), channel_id=1, source_target_pairs={{2,0},{3,1},{0,2},{1,3},{5,4},{4,5},{7,6},{6,7},{10,8},{11,9},{8,1... | collective-permute-start | bytes 1179656 | tf_op jit(solution)/shard_map/ppermute | solution.py:334
  14.9 0.0 copy-done
  14.9 0.0 copy-done.1
  14.9 0.0 copy-done.2
  14.9 2.5 %shard_map.76.after.near_out.refs_0_ = bf16[96,2048]{1,0:T(8,128)(2,1)S(1)} custom-call(bf16[128,2048]{1,0:T(8,128)(2,1)S(1)} %collective-permute-done.3.rows.after, bf16[384,128]{1,0:T(8,128)(2,1)S(1)} %get-tuple-element.20.place, f32[1,2048]{1,0:T(1,128)S(1)} %get-tuple-element.21.gain, bf16[2048,1024]{1,0:T(8,128)(2,1)S(1)} %bitcast.11, ...), custom_call_target="tpu_custom_call" | custom-call | flops 1207959552 | tf_op jit(solution)/shard_map/pallas_call | solution.py:70
  17.4 1.2 %collective-permute-done.rows = bf16[128,2048]{1,0:T(8,128)(2,1)S(1)} collective-permute-done((bf16[128,2048]{1,0:T(8,128)(2,1)}, bf16[128,2048]{1,0:T(8,128)(2,1)S(1)}, u32[]{:S(2)}, u32[]{:S(2)}) %collective-permute-start) | collective-permute-done | bytes 524320 | tf_op jit(solution)/shard_map/ppermute | solution.py:334
  18.6 0.3 shard_map.77.after
  18.9 1.6 %collective-permute-start.4 = (bf16[96,2048]{1,0:T(8,128)(2,1)S(1)}, bf16[96,2048]{1,0:T(8,128)(2,1)S(1)}, u32[]{:S(2)}, u32[]{:S(2)}) collective-permute-start(bf16[96,2048]{1,0:T(8,128)(2,1)S(1)} %shard_map.77.after), channel_id=1, source_target_pairs={{2,0},{3,1},{0,2},{1,3},{5,4},{4,5},{7,6},{6,7},{10,8},{11,9},{8,1... | collective-permute-start | bytes 1179656 | tf_op jit(solution)/shard_map/ppermute | solution.py:334
  20.5 0.2 collective-permute-done.5.rows
  20.7 2.3 %shard_map.78 = (bf16[96,1024]{1,0:T(8,128)(2,1)S(1)}, bf16[96,1024]{1,0:T(8,128)(2,1)S(1)}) custom-call(bf16[96,2048]{1,0:T(8,128)(2,1)S(1)} %collective-permute-done.5.rows, f32[1,2048]{1,0:T(1,128)S(1)} %get-tuple-element.21.gain, bf16[2048,1024]{1,0:T(8,128)(2,1)S(1)} %bitcast.12, bf16[2048,1024]{1,0:T(8,128)(2,1)S(1)} %bitcast.16, ...), custom_call_target="tpu_custom_call" | custom-call | flops 1207959552 | tf_op jit(solution)/shard_map/pallas_call | solution.py:70
  23.0 2.1 %collective-permute-start.7 = (bf16[96,1024]{1,0:T(8,128)(2,1)S(1)}, bf16[96,1024]{1,0:T(8,128)(2,1)S(1)}, u32[]{:S(2)}, u32[]{:S(2)}) collective-permute-start(bf16[96,1024]{1,0:T(8,128)(2,1)S(1)} %get-tuple-element.22.after), channel_id=1, source_target_pairs={{2,0},{3,1},{0,2},{1,3},{5,4},{4,5},{7,6},{6,7},{10,8},{11,9},{8,1... | collective-permute-start | bytes 589832 | tf_op jit(solution)/shard_map/ppermute | solution.py:334
  25.0 1.4 %collective-permute-start.6 = (bf16[96,1024]{1,0:T(8,128)(2,1)S(1)}, bf16[96,1024]{1,0:T(8,128)(2,1)S(1)}, u32[]{:S(2)}, u32[]{:S(2)}) collective-permute-start(bf16[96,1024]{1,0:T(8,128)(2,1)S(1)} %get-tuple-element.24), channel_id=1, source_target_pairs={{1,0},{0,1},{3,2},{2,3},{5,4},{4,5},{7,6},{6,7},{9,8},{8,9},{11,10... | collective-permute-start | bytes 589832 | tf_op jit(solution)/shard_map/ppermute | solution.py:334
  26.5 0.2 collective-permute-done.4.rows
  26.7 2.3 %shard_map.79 = (bf16[96,1024]{1,0:T(8,128)(2,1)S(1)}, bf16[96,1024]{1,0:T(8,128)(2,1)S(1)}, bf16[96,1024]{1,0:T(8,128)(2,1)S(1)}) custom-call(bf16[96,2048]{1,0:T(8,128)(2,1)S(1)} %collective-permute-done.4.rows, f32[1,2048]{1,0:T(1,128)S(1)} %get-tuple-element.21.gain, bf16[2048,1024]{1,0:T(8,128)(2,1)S(1)} %bitcast.13, bf16[2048,1024]{1,0:T(8,128)(2,1)S(1)} %bitcast.17, ...), custom_call_target="tpu_custom_call" | custom-call | flops 1207959552 | tf_op jit(solution)/shard_map/pallas_call | solution.py:70
  29.1 1.6 %collective-permute-start.8 = (bf16[96,1024]{1,0:T(8,128)(2,1)S(1)}, bf16[96,1024]{1,0:T(8,128)(2,1)S(1)}, u32[]{:S(2)}, u32[]{:S(2)}) collective-permute-start(bf16[96,1024]{1,0:T(8,128)(2,1)S(1)} %get-tuple-element.25), channel_id=1, source_target_pairs={{2,0},{3,1},{0,2},{1,3},{5,4},{4,5},{7,6},{6,7},{10,8},{11,9},{8,1... | collective-permute-start | bytes 589832 | tf_op jit(solution)/shard_map/ppermute | solution.py:334
  30.6 0.0 collective-permute-done.7.refs_1_
  30.6 0.3 shard_map.80.refs_2_
  30.9 0.6 %collective-permute-start.9 = (bf16[128,1024]{1,0:T(8,128)(2,1)S(1)}, bf16[128,1024]{1,0:T(8,128)(2,1)S(1)}, u32[]{:S(2)}, u32[]{:S(2)}) collective-permute-start(bf16[128,1024]{1,0:T(8,128)(2,1)S(1)} %shard_map.80.refs_2_), channel_id=1, source_target_pairs={{1,0},{0,1},{3,2},{2,3},{6,4},{7,5},{4,6},{5,7},{9,8},{8,9},{11,10... | collective-permute-start | bytes 786440 | tf_op jit(solution)/shard_map/ppermute | solution.py:334
  31.5 1.3 %collective-permute-done.6.refs_1_ = bf16[96,1024]{1,0:T(8,128)(2,1)S(1)} collective-permute-done((bf16[96,1024]{1,0:T(8,128)(2,1)S(1)}, bf16[96,1024]{1,0:T(8,128)(2,1)S(1)}, u32[]{:S(2)}, u32[]{:S(2)}) %collective-permute-start.6) | collective-permute-done | bytes 196640 | tf_op jit(solution)/shard_map/ppermute | solution.py:334
  32.8 0.3 shard_map.81.after
  33.1 0.1 collective-permute-start.11
  33.2 2.0 %collective-permute-start.10 = (bf16[96,1024]{1,0:T(8,128)(2,1)S(1)}, bf16[96,1024]{1,0:T(8,128)(2,1)S(1)}, u32[]{:S(2)}, u32[]{:S(2)}) collective-permute-start(bf16[96,1024]{1,0:T(8,128)(2,1)S(1)} %shard_map.85), channel_id=1, source_target_pairs={{1,0},{0,1},{3,2},{2,3},{5,4},{4,5},{7,6},{6,7},{9,8},{8,9},{11,10... | collective-permute-start | bytes 589832 | tf_op jit(solution)/shard_map/ppermute | solution.py:334
  35.3 2.5 %shard_map.82.here = bf16[96,2048]{1,0:T(8,128)(2,1)S(1)} custom-call(bf16[128,2048]{1,0:T(8,128)(2,1)S(1)} %collective-permute-done.rows, bf16[384,128]{1,0:T(8,128)(2,1)S(1)} %get-tuple-element.20.place, f32[1,2048]{1,0:T(1,128)S(1)} %get-tuple-element.21.gain, bf16[2048,1024]{1,0:T(8,128)(2,1)S(1)} %bitcast.14, bf16[2048,1024]{1,0:T(8,128)(2,1)S(1)} %bitcast.18, ...), custom_call_target="tpu_custom_call" | custom-call | flops 1207959552 | tf_op jit(solution)/shard_map/pallas_call | solution.py:70
  37.8 0.0 collective-permute-done.8.left
  37.8 0.4 shard_map.83.base
  38.2 0.0 collective-permute-done.9.left
  38.2 0.8 %shard_map.84 = (bf16[128,2048]{1,0:T(8,128)(2,1)}, f32[128,1024]{1,0:T(8,128)S(1)}) custom-call(f32[128,2048]{1,0:T(8,128)S(1)} %shard_map.83.base, bf16[128,1024]{1,0:T(8,128)(2,1)S(1)} %collective-permute-done.9.left), custom_call_target="tpu_custom_call" | custom-call | tf_op jit(solution)/shard_map/pallas_call | solution.py:310
  39.0 0.6 %collective-permute-done.10.slots_right = bf16[96,1024]{1,0:T(8,128)(2,1)S(1)} collective-permute-done((bf16[96,1024]{1,0:T(8,128)(2,1)S(1)}, bf16[96,1024]{1,0:T(8,128)(2,1)S(1)}, u32[]{:S(2)}, u32[]{:S(2)}) %collective-permute-start.10) | collective-permute-done | bytes 196640 | tf_op jit(solution)/shard_map/ppermute | solution.py:334
  39.6 0.0 collective-permute-done.11.right
  39.6 0.9 %shard_map.86 = bf16[128,2048]{1,0:T(8,128)(2,1)} custom-call(bf16[128,2048]{1,0:T(8,128)(2,1)} %get-tuple-element.26._, f32[128,1024]{1,0:T(8,128)S(1)} %get-tuple-element.27.rest, bf16[896,96]{1,0:T(8,128)(2,1)S(1)} %get-tuple-element.18.place_t, f32[128,8]{1,0:T(8,128)S(1)} %get-tuple-element.19.weight_t, ...), custom_call_target="tpu_custom_call", output_to_operand_aliasing={{}: (0, {})} | custom-call | tf_op jit(solution)/shard_map/pallas_call | solution.py:317
  (1 shorter events, 0.0 us)
Async XLA Ops:
  0.0 12.6 %collective-permute-start.3 = (bf16[128,2048]{1,0:T(8,128)(2,1)}, bf16[128,2048]{1,0:T(8,128)(2,1)S(1)}, u32[]{:S(2)}, u32[]{:S(2)}) collective-permute-start(bf16[128,2048]{1,0:T(8,128)(2,1)} %bitcast.23), channel_id=1, source_target_pairs={{29,0},{28,1},{31,2},{30,3},{2,4},{3,5},{0,6},{1,7},{5,8},{4,9},{7... | collective-permute-start | bytes 1572872 | tf_op jit(solution)/shard_map/ppermute | solution.py:334
  2.4 16.2 %collective-permute-start = (bf16[128,2048]{1,0:T(8,128)(2,1)}, bf16[128,2048]{1,0:T(8,128)(2,1)S(1)}, u32[]{:S(2)}, u32[]{:S(2)}) collective-permute-start(bf16[128,2048]{1,0:T(8,128)(2,1)} %bitcast.24), channel_id=1, source_target_pairs={{28,0},{29,1},{30,2},{31,3},{0,4},{1,5},{2,6},{3,7},{4,8},{5,9},{6... | collective-permute-start | bytes 1572872 | tf_op jit(solution)/shard_map/ppermute | solution.py:334
  4.1 10.8 %copy-start = (bf16[1,2048,1024]{2,1,0:T(8,128)(2,1)S(1)}, bf16[1,2048,1024]{2,1,0:T(8,128)(2,1)}, u32[]{:S(2)}) copy-start(bf16[1,2048,1024]{2,1,0:T(8,128)(2,1)} %param.11) | copy-start | bytes 12582916
  4.1 10.8 %copy-start.1 = (bf16[1,2048,1024]{2,1,0:T(8,128)(2,1)S(1)}, bf16[1,2048,1024]{2,1,0:T(8,128)(2,1)}, u32[]{:S(2)}) copy-start(bf16[1,2048,1024]{2,1,0:T(8,128)(2,1)} %param.12) | copy-start | bytes 12582916
  4.1 10.8 %copy-start.2 = (bf16[1,1024,2048]{2,1,0:T(8,128)(2,1)S(1)}, bf16[1,1024,2048]{2,1,0:T(8,128)(2,1)}, u32[]{:S(2)}) copy-start(bf16[1,1024,2048]{2,1,0:T(8,128)(2,1)} %param.13) | copy-start | bytes 12582916
  5.0 5.4 %collective-permute-start.2 = (f32[8,128]{1,0:T(8,128)S(1)}, f32[8,128]{1,0:T(8,128)S(1)}, u32[]{:S(2)}, u32[]{:S(2)}) collective-permute-start(f32[8,128]{1,0:T(8,128)S(1)} %get-tuple-element.17.own), channel_id=1, source_target_pairs={{2,0},{3,1},{0,2},{1,3},{5,4},{4,5},{7,6},{6,7},{10,8},{11,9},{8,1... | collective-permute-start | bytes 12296 | tf_op jit(solution)/shard_map/ppermute | solution.py:334
  6.6 3.9 %collective-permute-start.1 = (f32[8,128]{1,0:T(8,128)S(1)}, f32[8,128]{1,0:T(8,128)S(1)}, u32[]{:S(2)}, u32[]{:S(2)}) collective-permute-start(f32[8,128]{1,0:T(8,128)S(1)} %get-tuple-element.17.own), channel_id=1, source_target_pairs={{1,0},{0,1},{3,2},{2,3},{6,4},{7,5},{4,6},{5,7},{9,8},{8,9},{11,10... | collective-permute-start | bytes 12296 | tf_op jit(solution)/shard_map/ppermute | solution.py:334
  12.8 7.8 %collective-permute-start.5 = (bf16[96,2048]{1,0:T(8,128)(2,1)S(1)}, bf16[96,2048]{1,0:T(8,128)(2,1)S(1)}, u32[]{:S(2)}, u32[]{:S(2)}) collective-permute-start(bf16[96,2048]{1,0:T(8,128)(2,1)S(1)} %shard_map.75.after), channel_id=1, source_target_pairs={{2,0},{3,1},{0,2},{1,3},{5,4},{4,5},{7,6},{6,7},{10,8},{11,9},{8,1... | collective-permute-start | bytes 1179656 | tf_op jit(solution)/shard_map/ppermute | solution.py:334
  18.9 7.8 %collective-permute-start.4 = (bf16[96,2048]{1,0:T(8,128)(2,1)S(1)}, bf16[96,2048]{1,0:T(8,128)(2,1)S(1)}, u32[]{:S(2)}, u32[]{:S(2)}) collective-permute-start(bf16[96,2048]{1,0:T(8,128)(2,1)S(1)} %shard_map.77.after), channel_id=1, source_target_pairs={{2,0},{3,1},{0,2},{1,3},{5,4},{4,5},{7,6},{6,7},{10,8},{11,9},{8,1... | collective-permute-start | bytes 1179656 | tf_op jit(solution)/shard_map/ppermute | solution.py:334
  23.0 7.6 %collective-permute-start.7 = (bf16[96,1024]{1,0:T(8,128)(2,1)S(1)}, bf16[96,1024]{1,0:T(8,128)(2,1)S(1)}, u32[]{:S(2)}, u32[]{:S(2)}) collective-permute-start(bf16[96,1024]{1,0:T(8,128)(2,1)S(1)} %get-tuple-element.22.after), channel_id=1, source_target_pairs={{2,0},{3,1},{0,2},{1,3},{5,4},{4,5},{7,6},{6,7},{10,8},{11,9},{8,1... | collective-permute-start | bytes 589832 | tf_op jit(solution)/shard_map/ppermute | solution.py:334
  25.0 7.8 %collective-permute-start.6 = (bf16[96,1024]{1,0:T(8,128)(2,1)S(1)}, bf16[96,1024]{1,0:T(8,128)(2,1)S(1)}, u32[]{:S(2)}, u32[]{:S(2)}) collective-permute-start(bf16[96,1024]{1,0:T(8,128)(2,1)S(1)} %get-tuple-element.24), channel_id=1, source_target_pairs={{1,0},{0,1},{3,2},{2,3},{5,4},{4,5},{7,6},{6,7},{9,8},{8,9},{11,10... | collective-permute-start | bytes 589832 | tf_op jit(solution)/shard_map/ppermute | solution.py:334
  29.1 8.7 %collective-permute-start.8 = (bf16[96,1024]{1,0:T(8,128)(2,1)S(1)}, bf16[96,1024]{1,0:T(8,128)(2,1)S(1)}, u32[]{:S(2)}, u32[]{:S(2)}) collective-permute-start(bf16[96,1024]{1,0:T(8,128)(2,1)S(1)} %get-tuple-element.25), channel_id=1, source_target_pairs={{2,0},{3,1},{0,2},{1,3},{5,4},{4,5},{7,6},{6,7},{10,8},{11,9},{8,1... | collective-permute-start | bytes 589832 | tf_op jit(solution)/shard_map/ppermute | solution.py:334
  30.9 7.2 %collective-permute-start.9 = (bf16[128,1024]{1,0:T(8,128)(2,1)S(1)}, bf16[128,1024]{1,0:T(8,128)(2,1)S(1)}, u32[]{:S(2)}, u32[]{:S(2)}) collective-permute-start(bf16[128,1024]{1,0:T(8,128)(2,1)S(1)} %shard_map.80.refs_2_), channel_id=1, source_target_pairs={{1,0},{0,1},{3,2},{2,3},{6,4},{7,5},{4,6},{5,7},{9,8},{8,9},{11,10... | collective-permute-start | bytes 786440 | tf_op jit(solution)/shard_map/ppermute | solution.py:334
  33.1 6.5 %collective-permute-start.11 = (bf16[128,1024]{1,0:T(8,128)(2,1)S(1)}, bf16[128,1024]{1,0:T(8,128)(2,1)S(1)}, u32[]{:S(2)}, u32[]{:S(2)}) collective-permute-start(bf16[128,1024]{1,0:T(8,128)(2,1)S(1)} %shard_map.81.after), channel_id=1, source_target_pairs={{2,0},{3,1},{0,2},{1,3},{6,4},{7,5},{4,6},{5,7},{10,8},{11,9},{8,1... | collective-permute-start | bytes 786440 | tf_op jit(solution)/shard_map/ppermute | solution.py:334
  33.2 6.4 %collective-permute-start.10 = (bf16[96,1024]{1,0:T(8,128)(2,1)S(1)}, bf16[96,1024]{1,0:T(8,128)(2,1)S(1)}, u32[]{:S(2)}, u32[]{:S(2)}) collective-permute-start(bf16[96,1024]{1,0:T(8,128)(2,1)S(1)} %shard_map.85), channel_id=1, source_target_pairs={{1,0},{0,1},{3,2},{2,3},{5,4},{4,5},{7,6},{6,7},{9,8},{8,9},{11,10... | collective-permute-start | bytes 589832 | tf_op jit(solution)/shard_map/ppermute | solution.py:334

commit v8 on v6

--- a/solution.py
+++ b/solution.py
@@ -274,26 +274,25 @@
     return copy
 
 
-def first_body(base, left, out, rest, here, done):
+def first_body(base, left, out, here, done):
     cut = left.shape[1]
     copies = []
     for n, at in enumerate(range(0, cut, STRIP)):
         strip = slice(at, at + STRIP)
         copies.append(written(base[:, strip] + left[:, strip].astype(jnp.float32), here, out, at, done, n))
-    rest[...] = base[:, cut:]
     for copy in copies:
         copy.wait()
 
 
-def rest_body(_, rest, place_t, weight_t, slots_right, right, out, here, done):
-    cut, size = out.shape[1] - rest.shape[1], weight_t.shape[0]
+def rest_body(_, base, place_t, weight_t, slots_right, right, out, here, done):
+    cut, size = out.shape[1] - right.shape[1], weight_t.shape[0]
     hit = place_t[BACK_RIGHT * size : (BACK_RIGHT + 1) * size, :]
     weight = weight_t[:, BACK_RIGHT : BACK_RIGHT + 1]
     copies = []
-    for n, at in enumerate(range(0, rest.shape[1], STRIP)):
+    for n, at in enumerate(range(0, right.shape[1], STRIP)):
         strip = slice(at, at + STRIP)
         rows = jnp.dot(hit, slots_right[:, strip], preferred_element_type=jnp.float32)
-        total = rest[:, strip] + weight * rows + right[:, strip].astype(jnp.float32)
+        total = base[:, cut + at : cut + at + STRIP] + weight * rows + right[:, strip].astype(jnp.float32)
         copies.append(written(total, here, out, cut + at, done, n))
     for copy in copies:
         copy.wait()
@@ -301,17 +300,16 @@
 
 def last(base, place_t, weight_t, slots_right, left, right, dtype):
     out = like(base.shape, dtype)
-    rest = like(right.shape, jnp.float32)
     common = dict(
         scratch_shapes=[VMEM(out.shape, dtype), pltpu.SemaphoreType.DMA((base.shape[1] // STRIP,))],
         compiler_params=pltpu.CompilerParams(vmem_limit_bytes=8 << 20),
         cost_estimate=pl.CostEstimate(flops=0, bytes_accessed=0, transcendentals=0),
     )
-    result, rest = pl.pallas_call(
+    result = pl.pallas_call(
         first_body,
-        out_shape=[out, rest],
+        out_shape=out,
         in_specs=[spec()] * 2,
-        out_specs=[spec(pltpu.HBM), spec()],
+        out_specs=spec(pltpu.HBM),
         **common,
     )(base, left)
     return pl.pallas_call(
@@ -321,7 +319,7 @@
         out_specs=spec(pltpu.HBM),
         input_output_aliases={0: 0},
         **common,
-    )(result, rest, place_t, weight_t, slots_right, right)
+    )(result, base, place_t, weight_t, slots_right, right)
 
 
 def moved(value, back, flip):

time: 40.8 us -> 40.8 us (level)
  no operation moved by 1% of the time
where the time goes in v8:
time: 40.8 us; the launch traced here: 40.7 us
  starting transfers between devices  18.3 us (45%)
  Pallas kernels  14.3 us (35%)
  waiting for transfers between devices  7.88 us (19%)
    ppermute x12, starting transfers between devices, moved(): return lax.ppermute(value, ('section', 'expert'), pairs)  18.3 us
    pallas_call x11, Pallas kernels, call(): pl.pallas_call(body, out_shape=outs, in_specs=[spec()] * len(ins), out_sp...  11.7 us
    ppermute x12, waiting for transfers between devices, moved(): return lax.ppermute(value, ('section', 'expert'), pairs)  7.88 us
    pallas_call x1, Pallas kernels, last(): pl.pallas_call(rest_body, out_shape=out, in_specs=[spec(pltpu.HBM)] + [sp...  0.92 us
    pallas_call x1, Pallas kernels, tabled(): pl.pallas_call(table_body, out_shape=[like((8, ids.shape[1]), jnp.float32...  0.91 us
  transfers between devices with their start and end apart: 12, of which 10 were waited for; matrix products, arithmetic and copies ran while one was open for 0% of the time, Pallas kernels for 33%

profile of v8, /device:TPU:0, one launch (start us, length us, event | category | flops | bytes accessed | tf_op | source)
XLA Modules:
  0.0 40.7 jit_solution(4207243711810063810)
XLA Ops:
  0.0 2.4 %collective-permute-start.3 = (bf16[128,2048]{1,0:T(8,128)(2,1)}, bf16[128,2048]{1,0:T(8,128)(2,1)S(1)}, u32[]{:S(2)}, u32[]{:S(2)}) collective-permute-start(bf16[128,2048]{1,0:T(8,128)(2,1)} %bitcast.23), channel_id=1, source_target_pairs={{29,0},{28,1},{31,2},{30,3},{2,4},{3,5},{0,6},{1,7},{5,8},{4,9},{7... | collective-permute-start | bytes 1572872 | tf_op jit(solution)/shard_map/ppermute | solution.py:332
  2.4 1.7 %collective-permute-start = (bf16[128,2048]{1,0:T(8,128)(2,1)}, bf16[128,2048]{1,0:T(8,128)(2,1)S(1)}, u32[]{:S(2)}, u32[]{:S(2)}) collective-permute-start(bf16[128,2048]{1,0:T(8,128)(2,1)} %bitcast.24), channel_id=1, source_target_pairs={{28,0},{29,1},{30,2},{31,3},{0,4},{1,5},{2,6},{3,7},{4,8},{5,9},{6... | collective-permute-start | bytes 1572872 | tf_op jit(solution)/shard_map/ppermute | solution.py:332
  4.1 0.0 copy-start
  4.1 0.0 copy-start.1
  4.1 0.0 copy-start.2
  4.1 0.9 %shard_map.73 = (f32[8,128]{1,0:T(8,128)S(1)}, f32[1,2048]{1,0:T(1,128)S(1)}) custom-call(s32[2,128]{1,0:T(2,128)} %bitcast.25, f32[2,128]{1,0:T(2,128)} %bitcast.26, f32[1,2048]{1,0:T(1,128)} %gain.1), custom_call_target="tpu_custom_call" | custom-call | flops 20000000000 | tf_op jit(solution)/shard_map/pallas_call | solution.py:109
  5.0 1.6 %collective-permute-start.2 = (f32[8,128]{1,0:T(8,128)S(1)}, f32[8,128]{1,0:T(8,128)S(1)}, u32[]{:S(2)}, u32[]{:S(2)}) collective-permute-start(f32[8,128]{1,0:T(8,128)S(1)} %get-tuple-element.15.own), channel_id=1, source_target_pairs={{2,0},{3,1},{0,2},{1,3},{5,4},{4,5},{7,6},{6,7},{10,8},{11,9},{8,1... | collective-permute-start | bytes 12296 | tf_op jit(solution)/shard_map/ppermute | solution.py:332
  6.6 0.5 %collective-permute-start.1 = (f32[8,128]{1,0:T(8,128)S(1)}, f32[8,128]{1,0:T(8,128)S(1)}, u32[]{:S(2)}, u32[]{:S(2)}) collective-permute-start(f32[8,128]{1,0:T(8,128)S(1)} %get-tuple-element.15.own), channel_id=1, source_target_pairs={{1,0},{0,1},{3,2},{2,3},{6,4},{7,5},{4,6},{5,7},{9,8},{8,9},{11,10... | collective-permute-start | bytes 12296 | tf_op jit(solution)/shard_map/ppermute | solution.py:332
  7.1 3.3 %collective-permute-done.2.beside = f32[8,128]{1,0:T(8,128)S(1)} collective-permute-done((f32[8,128]{1,0:T(8,128)S(1)}, f32[8,128]{1,0:T(8,128)S(1)}, u32[]{:S(2)}, u32[]{:S(2)}) %collective-permute-start.2) | collective-permute-done | bytes 4128 | tf_op jit(solution)/shard_map/ppermute | solution.py:332
  10.4 0.1 collective-permute-done.1.near
  10.5 0.6 %shard_map.74 = (bf16[384,128]{1,0:T(8,128)(2,1)S(1)}, bf16[896,96]{1,0:T(8,128)(2,1)S(1)}, f32[128,8]{1,0:T(8,128)S(1)}) custom-call(f32[8,128]{1,0:T(8,128)S(1)} %get-tuple-element.15.own, f32[8,128]{1,0:T(8,128)S(1)} %collective-permute-done.1.near, f32[8,128]{1,0:T(8,128)S(1)} %collective-permute-done.2.beside), custom_call_target="tpu_custom_call" | custom-call | tf_op jit(solution)/shard_map/pallas_call | solution.py:70
  11.1 1.4 %collective-permute-done.3.rows.after = bf16[128,2048]{1,0:T(8,128)(2,1)S(1)} collective-permute-done((bf16[128,2048]{1,0:T(8,128)(2,1)}, bf16[128,2048]{1,0:T(8,128)(2,1)S(1)}, u32[]{:S(2)}, u32[]{:S(2)}) %collective-permute-start.3) | collective-permute-done | bytes 524320 | tf_op jit(solution)/shard_map/ppermute | solution.py:332
  12.6 0.3 shard_map.75.after
  12.8 2.1 %collective-permute-start.5 = (bf16[96,2048]{1,0:T(8,128)(2,1)S(1)}, bf16[96,2048]{1,0:T(8,128)(2,1)S(1)}, u32[]{:S(2)}, u32[]{:S(2)}) collective-permute-start(bf16[96,2048]{1,0:T(8,128)(2,1)S(1)} %shard_map.75.after), channel_id=1, source_target_pairs={{2,0},{3,1},{0,2},{1,3},{5,4},{4,5},{7,6},{6,7},{10,8},{11,9},{8,1... | collective-permute-start | bytes 1179656 | tf_op jit(solution)/shard_map/ppermute | solution.py:332
  14.9 0.0 copy-done
  14.9 0.0 copy-done.1
  14.9 0.0 copy-done.2
  14.9 2.5 %shard_map.76.after.near_out.refs_0_ = bf16[96,2048]{1,0:T(8,128)(2,1)S(1)} custom-call(bf16[128,2048]{1,0:T(8,128)(2,1)S(1)} %collective-permute-done.3.rows.after, bf16[384,128]{1,0:T(8,128)(2,1)S(1)} %get-tuple-element.18.place, f32[1,2048]{1,0:T(1,128)S(1)} %get-tuple-element.19.gain, bf16[2048,1024]{1,0:T(8,128)(2,1)S(1)} %bitcast.11, ...), custom_call_target="tpu_custom_call" | custom-call | flops 1207959552 | tf_op jit(solution)/shard_map/pallas_call | solution.py:70
  17.4 1.2 %collective-permute-done.rows = bf16[128,2048]{1,0:T(8,128)(2,1)S(1)} collective-permute-done((bf16[128,2048]{1,0:T(8,128)(2,1)}, bf16[128,2048]{1,0:T(8,128)(2,1)S(1)}, u32[]{:S(2)}, u32[]{:S(2)}) %collective-permute-start) | collective-permute-done | bytes 524320 | tf_op jit(solution)/shard_map/ppermute | solution.py:332
  18.6 0.3 shard_map.77.after
  18.9 1.6 %collective-permute-start.4 = (bf16[96,2048]{1,0:T(8,128)(2,1)S(1)}, bf16[96,2048]{1,0:T(8,128)(2,1)S(1)}, u32[]{:S(2)}, u32[]{:S(2)}) collective-permute-start(bf16[96,2048]{1,0:T(8,128)(2,1)S(1)} %shard_map.77.after), channel_id=1, source_target_pairs={{2,0},{3,1},{0,2},{1,3},{5,4},{4,5},{7,6},{6,7},{10,8},{11,9},{8,1... | collective-permute-start | bytes 1179656 | tf_op jit(solution)/shard_map/ppermute | solution.py:332
  20.5 0.2 collective-permute-done.5.rows
  20.7 2.3 %shard_map.78 = (bf16[96,1280]{1,0:T(8,128)(2,1)S(1)}, bf16[96,768]{1,0:T(8,128)(2,1)S(1)}) custom-call(bf16[96,2048]{1,0:T(8,128)(2,1)S(1)} %collective-permute-done.5.rows, f32[1,2048]{1,0:T(1,128)S(1)} %get-tuple-element.19.gain, bf16[2048,1024]{1,0:T(8,128)(2,1)S(1)} %bitcast.12, bf16[2048,1024]{1,0:T(8,128)(2,1)S(1)} %bitcast.16, ...), custom_call_target="tpu_custom_call" | custom-call | flops 1207959552 | tf_op jit(solution)/shard_map/pallas_call | solution.py:70
  23.0 2.1 %collective-permute-start.7 = (bf16[96,1280]{1,0:T(8,128)(2,1)S(1)}, bf16[96,1280]{1,0:T(8,128)(2,1)S(1)}, u32[]{:S(2)}, u32[]{:S(2)}) collective-permute-start(bf16[96,1280]{1,0:T(8,128)(2,1)S(1)} %get-tuple-element.20.after), channel_id=1, source_target_pairs={{2,0},{3,1},{0,2},{1,3},{5,4},{4,5},{7,6},{6,7},{10,8},{11,9},{8,1... | collective-permute-start | bytes 737288 | tf_op jit(solution)/shard_map/ppermute | solution.py:332
  25.0 1.4 %collective-permute-start.6 = (bf16[96,768]{1,0:T(8,128)(2,1)S(1)}, bf16[96,768]{1,0:T(8,128)(2,1)S(1)}, u32[]{:S(2)}, u32[]{:S(2)}) collective-permute-start(bf16[96,768]{1,0:T(8,128)(2,1)S(1)} %get-tuple-element.22), channel_id=1, source_target_pairs={{1,0},{0,1},{3,2},{2,3},{5,4},{4,5},{7,6},{6,7},{9,8},{8,9},{11,10... | collective-permute-start | bytes 442376 | tf_op jit(solution)/shard_map/ppermute | solution.py:332
  26.5 0.2 collective-permute-done.4.rows
  26.7 2.3 %shard_map.79 = (bf16[96,1280]{1,0:T(8,128)(2,1)S(1)}, bf16[96,768]{1,0:T(8,128)(2,1)S(1)}, bf16[96,768]{1,0:T(8,128)(2,1)S(1)}) custom-call(bf16[96,2048]{1,0:T(8,128)(2,1)S(1)} %collective-permute-done.4.rows, f32[1,2048]{1,0:T(1,128)S(1)} %get-tuple-element.19.gain, bf16[2048,1024]{1,0:T(8,128)(2,1)S(1)} %bitcast.13, bf16[2048,1024]{1,0:T(8,128)(2,1)S(1)} %bitcast.17, ...), custom_call_target="tpu_custom_call" | custom-call | flops 1207959552 | tf_op jit(solution)/shard_map/pallas_call | solution.py:70
  29.0 1.6 %collective-permute-start.8 = (bf16[96,1280]{1,0:T(8,128)(2,1)S(1)}, bf16[96,1280]{1,0:T(8,128)(2,1)S(1)}, u32[]{:S(2)}, u32[]{:S(2)}) collective-permute-start(bf16[96,1280]{1,0:T(8,128)(2,1)S(1)} %get-tuple-element.23), channel_id=1, source_target_pairs={{2,0},{3,1},{0,2},{1,3},{5,4},{4,5},{7,6},{6,7},{10,8},{11,9},{8,1... | collective-permute-start | bytes 737288 | tf_op jit(solution)/shard_map/ppermute | solution.py:332
  30.6 0.0 collective-permute-done.7.refs_1_
  30.6 0.3 shard_map.80.refs_2_
  30.9 1.3 %collective-permute-start.9 = (bf16[128,1280]{1,0:T(8,128)(2,1)S(1)}, bf16[128,1280]{1,0:T(8,128)(2,1)S(1)}, u32[]{:S(2)}, u32[]{:S(2)}) collective-permute-start(bf16[128,1280]{1,0:T(8,128)(2,1)S(1)} %shard_map.80.refs_2_), channel_id=1, source_target_pairs={{1,0},{0,1},{3,2},{2,3},{6,4},{7,5},{4,6},{5,7},{9,8},{8,9},{11,10... | collective-permute-start | bytes 983048 | tf_op jit(solution)/shard_map/ppermute | solution.py:332
  32.2 0.0 collective-permute-done.6.refs_1_
  32.2 0.3 shard_map.81.after
  32.5 1.5 %collective-permute-start.11 = (bf16[128,768]{1,0:T(8,128)(2,1)S(1)}, bf16[128,768]{1,0:T(8,128)(2,1)S(1)}, u32[]{:S(2)}, u32[]{:S(2)}) collective-permute-start(bf16[128,768]{1,0:T(8,128)(2,1)S(1)} %shard_map.81.after), channel_id=1, source_target_pairs={{2,0},{3,1},{0,2},{1,3},{6,4},{7,5},{4,6},{5,7},{10,8},{11,9},{8,1... | collective-permute-start | bytes 589832 | tf_op jit(solution)/shard_map/ppermute | solution.py:332
  34.0 0.7 %collective-permute-start.10 = (bf16[96,768]{1,0:T(8,128)(2,1)S(1)}, bf16[96,768]{1,0:T(8,128)(2,1)S(1)}, u32[]{:S(2)}, u32[]{:S(2)}) collective-permute-start(bf16[96,768]{1,0:T(8,128)(2,1)S(1)} %shard_map.85), channel_id=1, source_target_pairs={{1,0},{0,1},{3,2},{2,3},{5,4},{4,5},{7,6},{6,7},{9,8},{8,9},{11,10... | collective-permute-start | bytes 442376 | tf_op jit(solution)/shard_map/ppermute | solution.py:332
  34.7 2.5 %shard_map.82.here = bf16[96,2048]{1,0:T(8,128)(2,1)S(1)} custom-call(bf16[128,2048]{1,0:T(8,128)(2,1)S(1)} %collective-permute-done.rows, bf16[384,128]{1,0:T(8,128)(2,1)S(1)} %get-tuple-element.18.place, f32[1,2048]{1,0:T(1,128)S(1)} %get-tuple-element.19.gain, bf16[2048,1024]{1,0:T(8,128)(2,1)S(1)} %bitcast.14, bf16[2048,1024]{1,0:T(8,128)(2,1)S(1)} %bitcast.18, ...), custom_call_target="tpu_custom_call" | custom-call | flops 1207959552 | tf_op jit(solution)/shard_map/pallas_call | solution.py:70
  37.2 0.4 %collective-permute-done.8.left = bf16[96,1280]{1,0:T(8,128)(2,1)S(1)} collective-permute-done((bf16[96,1280]{1,0:T(8,128)(2,1)S(1)}, bf16[96,1280]{1,0:T(8,128)(2,1)S(1)}, u32[]{:S(2)}, u32[]{:S(2)}) %collective-permute-start.8) | collective-permute-done | bytes 245792 | tf_op jit(solution)/shard_map/ppermute | solution.py:332
  37.6 0.4 shard_map.83.base
  38.0 0.1 collective-permute-done.9.left
  38.1 0.8 %shard_map.84._ = bf16[128,2048]{1,0:T(8,128)(2,1)} custom-call(f32[128,2048]{1,0:T(8,128)S(1)} %shard_map.83.base, bf16[128,1280]{1,0:T(8,128)(2,1)S(1)} %collective-permute-done.9.left), custom_call_target="tpu_custom_call" | custom-call | tf_op jit(solution)/shard_map/pallas_call | solution.py:308
  38.9 0.8 %collective-permute-done.10.slots_right = bf16[96,768]{1,0:T(8,128)(2,1)S(1)} collective-permute-done((bf16[96,768]{1,0:T(8,128)(2,1)S(1)}, bf16[96,768]{1,0:T(8,128)(2,1)S(1)}, u32[]{:S(2)}, u32[]{:S(2)}) %collective-permute-start.10) | collective-permute-done | bytes 147488 | tf_op jit(solution)/shard_map/ppermute | solution.py:332
  39.7 0.1 collective-permute-done.11.right
  39.7 0.9 %shard_map.86 = bf16[128,2048]{1,0:T(8,128)(2,1)} custom-call(bf16[128,2048]{1,0:T(8,128)(2,1)} %shard_map.84._, f32[128,2048]{1,0:T(8,128)S(1)} %shard_map.83.base, bf16[896,96]{1,0:T(8,128)(2,1)S(1)} %get-tuple-element.16.place_t, f32[128,8]{1,0:T(8,128)S(1)} %get-tuple-element.17.weight_t, ...), custom_call_target="tpu_custom_call", output_to_operand_aliasing={{}: (0, {})} | custom-call | tf_op jit(solution)/shard_map/pallas_call | solution.py:315
  (1 shorter events, 0.0 us)
Async XLA Ops:
  0.0 12.6 %collective-permute-start.3 = (bf16[128,2048]{1,0:T(8,128)(2,1)}, bf16[128,2048]{1,0:T(8,128)(2,1)S(1)}, u32[]{:S(2)}, u32[]{:S(2)}) collective-permute-start(bf16[128,2048]{1,0:T(8,128)(2,1)} %bitcast.23), channel_id=1, source_target_pairs={{29,0},{28,1},{31,2},{30,3},{2,4},{3,5},{0,6},{1,7},{5,8},{4,9},{7... | collective-permute-start | bytes 1572872 | tf_op jit(solution)/shard_map/ppermute | solution.py:332
  2.4 16.2 %collective-permute-start = (bf16[128,2048]{1,0:T(8,128)(2,1)}, bf16[128,2048]{1,0:T(8,128)(2,1)S(1)}, u32[]{:S(2)}, u32[]{:S(2)}) collective-permute-start(bf16[128,2048]{1,0:T(8,128)(2,1)} %bitcast.24), channel_id=1, source_target_pairs={{28,0},{29,1},{30,2},{31,3},{0,4},{1,5},{2,6},{3,7},{4,8},{5,9},{6... | collective-permute-start | bytes 1572872 | tf_op jit(solution)/shard_map/ppermute | solution.py:332
  4.1 10.8 %copy-start = (bf16[1,2048,1024]{2,1,0:T(8,128)(2,1)S(1)}, bf16[1,2048,1024]{2,1,0:T(8,128)(2,1)}, u32[]{:S(2)}) copy-start(bf16[1,2048,1024]{2,1,0:T(8,128)(2,1)} %param.11) | copy-start | bytes 12582916
  4.1 10.8 %copy-start.1 = (bf16[1,2048,1024]{2,1,0:T(8,128)(2,1)S(1)}, bf16[1,2048,1024]{2,1,0:T(8,128)(2,1)}, u32[]{:S(2)}) copy-start(bf16[1,2048,1024]{2,1,0:T(8,128)(2,1)} %param.12) | copy-start | bytes 12582916
  4.1 10.8 %copy-start.2 = (bf16[1,1024,2048]{2,1,0:T(8,128)(2,1)S(1)}, bf16[1,1024,2048]{2,1,0:T(8,128)(2,1)}, u32[]{:S(2)}) copy-start(bf16[1,1024,2048]{2,1,0:T(8,128)(2,1)} %param.13) | copy-start | bytes 12582916
  5.0 5.4 %collective-permute-start.2 = (f32[8,128]{1,0:T(8,128)S(1)}, f32[8,128]{1,0:T(8,128)S(1)}, u32[]{:S(2)}, u32[]{:S(2)}) collective-permute-start(f32[8,128]{1,0:T(8,128)S(1)} %get-tuple-element.15.own), channel_id=1, source_target_pairs={{2,0},{3,1},{0,2},{1,3},{5,4},{4,5},{7,6},{6,7},{10,8},{11,9},{8,1... | collective-permute-start | bytes 12296 | tf_op jit(solution)/shard_map/ppermute | solution.py:332
  6.6 3.9 %collective-permute-start.1 = (f32[8,128]{1,0:T(8,128)S(1)}, f32[8,128]{1,0:T(8,128)S(1)}, u32[]{:S(2)}, u32[]{:S(2)}) collective-permute-start(f32[8,128]{1,0:T(8,128)S(1)} %get-tuple-element.15.own), channel_id=1, source_target_pairs={{1,0},{0,1},{3,2},{2,3},{6,4},{7,5},{4,6},{5,7},{9,8},{8,9},{11,10... | collective-permute-start | bytes 12296 | tf_op jit(solution)/shard_map/ppermute | solution.py:332
  12.8 7.8 %collective-permute-start.5 = (bf16[96,2048]{1,0:T(8,128)(2,1)S(1)}, bf16[96,2048]{1,0:T(8,128)(2,1)S(1)}, u32[]{:S(2)}, u32[]{:S(2)}) collective-permute-start(bf16[96,2048]{1,0:T(8,128)(2,1)S(1)} %shard_map.75.after), channel_id=1, source_target_pairs={{2,0},{3,1},{0,2},{1,3},{5,4},{4,5},{7,6},{6,7},{10,8},{11,9},{8,1... | collective-permute-start | bytes 1179656 | tf_op jit(solution)/shard_map/ppermute | solution.py:332
  18.9 7.8 %collective-permute-start.4 = (bf16[96,2048]{1,0:T(8,128)(2,1)S(1)}, bf16[96,2048]{1,0:T(8,128)(2,1)S(1)}, u32[]{:S(2)}, u32[]{:S(2)}) collective-permute-start(bf16[96,2048]{1,0:T(8,128)(2,1)S(1)} %shard_map.77.after), channel_id=1, source_target_pairs={{2,0},{3,1},{0,2},{1,3},{5,4},{4,5},{7,6},{6,7},{10,8},{11,9},{8,1... | collective-permute-start | bytes 1179656 | tf_op jit(solution)/shard_map/ppermute | solution.py:332
  23.0 7.6 %collective-permute-start.7 = (bf16[96,1280]{1,0:T(8,128)(2,1)S(1)}, bf16[96,1280]{1,0:T(8,128)(2,1)S(1)}, u32[]{:S(2)}, u32[]{:S(2)}) collective-permute-start(bf16[96,1280]{1,0:T(8,128)(2,1)S(1)} %get-tuple-element.20.after), channel_id=1, source_target_pairs={{2,0},{3,1},{0,2},{1,3},{5,4},{4,5},{7,6},{6,7},{10,8},{11,9},{8,1... | collective-permute-start | bytes 737288 | tf_op jit(solution)/shard_map/ppermute | solution.py:332
  25.0 7.2 %collective-permute-start.6 = (bf16[96,768]{1,0:T(8,128)(2,1)S(1)}, bf16[96,768]{1,0:T(8,128)(2,1)S(1)}, u32[]{:S(2)}, u32[]{:S(2)}) collective-permute-start(bf16[96,768]{1,0:T(8,128)(2,1)S(1)} %get-tuple-element.22), channel_id=1, source_target_pairs={{1,0},{0,1},{3,2},{2,3},{5,4},{4,5},{7,6},{6,7},{9,8},{8,9},{11,10... | collective-permute-start | bytes 442376 | tf_op jit(solution)/shard_map/ppermute | solution.py:332
  29.0 8.6 %collective-permute-start.8 = (bf16[96,1280]{1,0:T(8,128)(2,1)S(1)}, bf16[96,1280]{1,0:T(8,128)(2,1)S(1)}, u32[]{:S(2)}, u32[]{:S(2)}) collective-permute-start(bf16[96,1280]{1,0:T(8,128)(2,1)S(1)} %get-tuple-element.23), channel_id=1, source_target_pairs={{2,0},{3,1},{0,2},{1,3},{5,4},{4,5},{7,6},{6,7},{10,8},{11,9},{8,1... | collective-permute-start | bytes 737288 | tf_op jit(solution)/shard_map/ppermute | solution.py:332
  30.9 7.1 %collective-permute-start.9 = (bf16[128,1280]{1,0:T(8,128)(2,1)S(1)}, bf16[128,1280]{1,0:T(8,128)(2,1)S(1)}, u32[]{:S(2)}, u32[]{:S(2)}) collective-permute-start(bf16[128,1280]{1,0:T(8,128)(2,1)S(1)} %shard_map.80.refs_2_), channel_id=1, source_target_pairs={{1,0},{0,1},{3,2},{2,3},{6,4},{7,5},{4,6},{5,7},{9,8},{8,9},{11,10... | collective-permute-start | bytes 983048 | tf_op jit(solution)/shard_map/ppermute | solution.py:332
  32.5 7.2 %collective-permute-start.11 = (bf16[128,768]{1,0:T(8,128)(2,1)S(1)}, bf16[128,768]{1,0:T(8,128)(2,1)S(1)}, u32[]{:S(2)}, u32[]{:S(2)}) collective-permute-start(bf16[128,768]{1,0:T(8,128)(2,1)S(1)} %shard_map.81.after), channel_id=1, source_target_pairs={{2,0},{3,1},{0,2},{1,3},{6,4},{7,5},{4,6},{5,7},{10,8},{11,9},{8,1... | collective-permute-start | bytes 589832 | tf_op jit(solution)/shard_map/ppermute | solution.py:332
  34.0 5.6 %collective-permute-start.10 = (bf16[96,768]{1,0:T(8,128)(2,1)S(1)}, bf16[96,768]{1,0:T(8,128)(2,1)S(1)}, u32[]{:S(2)}, u32[]{:S(2)}) collective-permute-start(bf16[96,768]{1,0:T(8,128)(2,1)S(1)} %shard_map.85), channel_id=1, source_target_pairs={{1,0},{0,1},{3,2},{2,3},{5,4},{4,5},{7,6},{6,7},{9,8},{8,9},{11,10... | collective-permute-start | bytes 442376 | tf_op jit(solution)/shard_map/ppermute | solution.py:332
